TPU v7x, 32 devices: a whole 2x2x4 slice. The times are simulated.
32 devices in a mesh: dp: 4 (over x, core), expert: 4 (over z), fsdp: 2 (over y).
Axes of the slice: x: 2, y: 2, z: 4, core: 2. Of those that a mesh axis runs over, the one named last changes fastest.
Arguments:
- grads: float32 [4, 16, 256, 512], P('dp', 'expert', 'fsdp'), may hold values from -65 to 65
- owner_slot: int32 [16], P('expert'), may hold values from 0 to 7, as said below
- momentum: bfloat16 [32, 256, 512], P(('dp', 'expert', 'fsdp')), may hold values from -6 to 6
Outputs:
- updates: bfloat16 [16, 256, 512], P('expert', 'fsdp')
- new_momentum: bfloat16 [32, 256, 512], P(('dp', 'expert', 'fsdp'))
Inputs may be any that keep to these rules, and one draw needn't show every extreme that they name: Within each group e, the 4 entries owner_slot[e * 4 + j] are distinct; in every group some owner o holds all 1 of its slots.
All inputs are finite; a program needn't handle non-finite values.
Results may differ from a plain program's by a relative error of at most 0.001.
Values may be sent and summed in bfloat16 or wider, within the bound.
No kernel may reach another device: no remote copies, remote signals or barrier semaphores. Data moves between devices by JAX's collectives and lax.ppermute only.
A program may use at most 64 MiB of HBM per device.

v0:
```python
import math

import jax
import jax.numpy as jnp
from jax import lax
from jax.sharding import PartitionSpec as P

R = 256
C = 512
ITERS = 5


COEF_A = 3.4445
COEF_B = -4.775
COEF_C = 2.0315
MOMENT = 0.95


def orthogonalize(stack):
    norms = jnp.sqrt(jnp.sum(stack * stack, axis=(1, 2), keepdims=True))
    current = stack / (norms + 1e-07)
    for step in range(ITERS):
        gram = jnp.einsum("krc,ksc->krs", current, current, precision=lax.Precision.HIGHEST)
        square = jnp.einsum("krs,kst->krt", gram, gram, precision=lax.Precision.HIGHEST)
        poly = COEF_B * gram + COEF_C * square
        current = COEF_A * current + jnp.einsum(
            "krs,ksc->krc", poly, current, precision=lax.Precision.HIGHEST
        )
    return current


def per_device(grads, owner_slot, momentum):
    partial_rows = grads[0]
    mats, rows_shard, width = partial_rows.shape
    n_replica = lax.axis_size("dp")
    n_shard = lax.axis_size("fsdp")
    owners = n_replica * n_shard
    cap = momentum.shape[0]
    rows_owner = rows_shard // n_replica
    reduced = lax.psum_scatter(partial_rows, "dp", scatter_dimension=1, tiled=True)
    slot_ids = jnp.arange(owners * cap, dtype=jnp.int32)
    matched = owner_slot[None, :] == slot_ids[:, None]
    holder = jnp.sum(jnp.where(matched, jnp.arange(mats, dtype=jnp.int32)[None, :], 0), axis=1)
    filled = jnp.any(matched, axis=1)
    outgoing = jnp.where(filled[:, None, None], jnp.take(reduced, holder, axis=0), 0.0)
    outgoing = outgoing.reshape(n_replica, n_shard, cap, rows_owner, width)
    arrived = lax.all_to_all(
        outgoing.reshape(owners, cap, rows_owner, width),
        ("dp", "fsdp"),
        split_axis=0,
        concat_axis=0,
        tiled=True,
    )
    arrived = arrived.reshape(n_replica, n_shard, cap, rows_owner, width)
    whole = jnp.transpose(arrived, (2, 1, 0, 3, 4)).reshape(
        cap, n_shard * n_replica * rows_owner, width
    )
    buffer = MOMENT * momentum.astype(jnp.float32) + whole
    new_momentum = buffer.astype(jnp.bfloat16)
    nesterov = whole + MOMENT * buffer
    factor = 0.2 * math.sqrt(max(R, C))
    ortho = (factor * orthogonalize(nesterov)).astype(jnp.bfloat16)
    leaving = jnp.transpose(
        ortho.reshape(cap, n_shard, n_replica, rows_owner, width), (2, 1, 0, 3, 4)
    )
    returned = lax.all_to_all(
        leaving.reshape(owners, cap, rows_owner, width),
        ("dp", "fsdp"),
        split_axis=0,
        concat_axis=0,
        tiled=True,
    )
    returned = returned.reshape(owners * cap, rows_owner, width)
    mine = jnp.take(returned, owner_slot, axis=0)
    updates = lax.all_gather(mine, "dp", axis=1, tiled=True)
    return (updates, new_momentum)


def solution(mesh):
    placed = (P("dp", "expert", "fsdp", None), P("expert"), P(("dp", "expert", "fsdp"), None, None))
    return jax.shard_map(
        per_device,
        mesh=mesh,
        in_specs=placed,
        out_specs=(P("expert", "fsdp", None), P(("dp", "expert", "fsdp"), None, None)),
        check_vma=False,
    )
```

profile of v0, /device:TPU:0, one launch (start us, length us, event | category | flops | bytes accessed | tf_op | source)
XLA Modules:
  0.0 90.1 jit_solution(15047892615667583834)
XLA Ops:
  7.2 0.7 reduce-scatter.2.cloned.1.call-update
  8.1 30.0 %reduce-scatter.2.cloned.1.call-done = f32[4,32,512]{2,1,0:T(8,128)} async-done(((f32[4,128,512]{2,1,0:T(8,128)}), f32[4,32,512]{2,1,0:T(8,128)}) %reduce-scatter.2.cloned.1.call-update) | async-done | bytes 262160 | tf_op jit(solution)/shard_map/reduce_scatter | solution.py:40
  38.1 1.5 %gather_fusion = f32[8,32,512]{2,1,0:T(8,128)S(1)} fusion(f32[4,32,512]{2,1,0:T(8,128)} %reduce-scatter.2.cloned.1.call-done, s32[1024]{0:T(1024)S(1)} %pad_clamp_fusion.1), kind=kCustom, calls=%fused_computation | custom fusion | bytes 1048608 | tf_op jit(solution)/shard_map/jit(_take)/gather | solution.py:45
  39.7 0.9 %fusion.27 = f32[8,1,32,512]{3,2,1,0:T(8,128)} fusion(f32[8,32,512]{2,1,0:T(8,128)S(1)} %gather_fusion, pred[8]{0:T(512)(128)(4,1)S(1)} %compare_and_fusion, pred[8]{0:T(512)(128)(4,1)S(1)} %fusion.30), kind=kLoop, calls=%fused_computation.42 | loop fusion | flops 262144 | bytes 1048592 | tf_op jit(solution)/shard_map/jit(_where)/select_n | solution.py:45
  40.6 3.5 %all-to-all-start = ((f32[8,1,32,512]{3,2,1,0:T(8,128)}), f32[8,1,32,512]{3,2,1,0:T(8,128)S(1)}, u32[]{:S(2)}, u32[]{:S(2)}) async-start(f32[8,1,32,512]{3,2,1,0:T(8,128)} %fusion.27), calls=%async_computation.1 | async-start | bytes 1048576 | tf_op jit(solution)/shard_map/all_to_all | solution.py:47
  44.1 8.8 %all-to-all-done = f32[8,1,32,512]{3,2,1,0:T(8,128)S(1)} async-done(((f32[8,1,32,512]{3,2,1,0:T(8,128)}), f32[8,1,32,512]{3,2,1,0:T(8,128)S(1)}, u32[]{:S(2)}, u32[]{:S(2)}) %all-to-all-start) | async-done | bytes 524320 | tf_op jit(solution)/shard_map/all_to_all | solution.py:47
  52.9 0.9 %copy-done = bf16[1,256,512]{2,1,0:T(8,128)(2,1)S(1)} copy-done((bf16[1,256,512]{2,1,0:T(8,128)(2,1)S(1)}, bf16[1,256,512]{2,1,0:T(8,128)(2,1)}, u32[]{:S(2)}) %copy-start) | copy-done | bytes 262168
  53.8 0.7 multiply_reduce_fusion
  55.3 0.8 fusion.28
  56.1 0.6 fusion.25
  57.1 0.6 fusion
  57.8 0.6 fusion.22
  58.8 0.6 fusion.1
  59.4 0.6 fusion.19
  60.4 0.6 fusion.2
  61.1 0.6 fusion.16
  62.1 0.6 fusion.3
  62.8 0.6 fusion.13
  63.8 0.6 fusion.6
  64.4 0.7 copy.12
  65.1 3.4 %all-to-all-start.1 = ((bf16[8,1,32,512]{3,2,1,0:T(8,128)(2,1)}), bf16[8,1,32,512]{3,2,1,0:T(8,128)(2,1)S(1)}, u32[]{:S(2)}, u32[]{:S(2)}) async-start(bf16[8,1,32,512]{3,2,1,0:T(8,128)(2,1)} %bitcast.21), calls=%async_computation.2 | async-start | bytes 524288 | tf_op jit(solution)/shard_map/all_to_all | solution.py:66
  68.6 5.9 %all-to-all-done.1 = bf16[8,1,32,512]{3,2,1,0:T(8,128)(2,1)S(1)} async-done(((bf16[8,1,32,512]{3,2,1,0:T(8,128)(2,1)}), bf16[8,1,32,512]{3,2,1,0:T(8,128)(2,1)S(1)}, u32[]{:S(2)}, u32[]{:S(2)}) %all-to-all-start.1) | async-done | bytes 262176 | tf_op jit(solution)/shard_map/all_to_all | solution.py:66
  75.2 7.3 %all_gather.3 = bf16[4,128,512]{2,1,0:T(8,128)(2,1)S(1)} all-gather(bf16[4,32,512]{2,1,0:T(8,128)(2,1)S(1)} %broadcast_select_fusion), channel_id=1, replica_groups=mesh['dp'=4,'expert'=4,'fsdp'=2] {'dp'}, dimensions={1}, use_global_device_ids=true | all-gather | bytes 655360 | tf_op jit(solution)/shard_map/all_gather | solution.py:75
  82.5 0.8 copy.15
  (20 shorter events, 2.8 us)
Async XLA Ops:
  7.2 31.0 %reduce-scatter.2.cloned.1.call-start = ((), (), s32[]{:S(2)}) async-start(), calls=%async_computation.3 | async-start | bytes 1310720 | tf_op jit(solution)/shard_map/reduce_scatter | solution.py:40
  7.2 0.7 copy-start.1
  40.6 12.3 %all-to-all-start = ((f32[8,1,32,512]{3,2,1,0:T(8,128)}), f32[8,1,32,512]{3,2,1,0:T(8,128)S(1)}, u32[]{:S(2)}, u32[]{:S(2)}) async-start(f32[8,1,32,512]{3,2,1,0:T(8,128)} %fusion.27), calls=%async_computation.1 | async-start | bytes 1048576 | tf_op jit(solution)/shard_map/all_to_all | solution.py:47
  52.9 1.0 %copy-start = (bf16[1,256,512]{2,1,0:T(8,128)(2,1)S(1)}, bf16[1,256,512]{2,1,0:T(8,128)(2,1)}, u32[]{:S(2)}) copy-start(bf16[1,256,512]{2,1,0:T(8,128)(2,1)} %param.5) | copy-start | bytes 786436
  65.1 9.4 %all-to-all-start.1 = ((bf16[8,1,32,512]{3,2,1,0:T(8,128)(2,1)}), bf16[8,1,32,512]{3,2,1,0:T(8,128)(2,1)S(1)}, u32[]{:S(2)}, u32[]{:S(2)}) async-start(bf16[8,1,32,512]{3,2,1,0:T(8,128)(2,1)} %bitcast.21), calls=%async_computation.2 | async-start | bytes 524288 | tf_op jit(solution)/shard_map/all_to_all | solution.py:66
Sparse Core Ops, SparseCore 0:
  10.5 27.5 reduce-scatter.1
where the time goes:
time: 90.5 us; the launch traced here: 90.1 us
  waiting for transfers between devices  45.4 us (50%)
  between operations  14.9 us (16%)
  matrix products  8.22 us (9%)
  blocking collectives  7.32 us (8%)
  starting transfers between devices  6.95 us (8%)
  local copies, waits for them, and re-layouts  4.55 us (5%)
  other arithmetic  2.79 us (3%)
    reduce_scatter x1, waiting for transfers between devices, per_device(): lax.psum_scatter(partial_rows, 'dp', scatter_dimension=1, tiled=True)  30 us
    all_to_all x1, waiting for transfers between devices, per_device(): lax.all_to_all(outgoing.reshape(owners, cap, rows_owner, width), ('dp', '...  8.76 us
    all_gather x1, blocking collectives, per_device(): updates = lax.all_gather(mine, 'dp', axis=1, tiled=True)  7.32 us
    all_to_all x1, waiting for transfers between devices, per_device(): lax.all_to_all(leaving.reshape(owners, cap, rows_owner, width), ('dp', 'f...  5.93 us
    all_to_all x1, starting transfers between devices, per_device(): lax.all_to_all(outgoing.reshape(owners, cap, rows_owner, width), ('dp', '...  3.49 us
    all_to_all x1, starting transfers between devices, per_device(): lax.all_to_all(leaving.reshape(owners, cap, rows_owner, width), ('dp', 'f...  3.41 us
    dot_general x5, matrix products, orthogonalize(): jnp.einsum('krs,ksc->krc', poly, current, precision=lax.Precision.HIGHEST)  3.23 us
    dot_general x5, matrix products, orthogonalize(): jnp.einsum('krc,ksc->krs', current, current, precision=lax.Precision.HIGH...  3.09 us
  transfers between devices with their start and end apart: 3, of which 3 were waited for; matrix products, arithmetic and copies ran while one was open for 0% of the time, Pallas kernels for 0%

commit v1 on v0

--- a/solution.py
+++ b/solution.py
@@ -1,8 +1,11 @@
+import functools
 import math
 
 import jax
 import jax.numpy as jnp
 from jax import lax
+from jax.experimental import pallas as pl
+from jax.experimental.pallas import tpu as pltpu
 from jax.sharding import PartitionSpec as P
 
 R = 256
@@ -14,6 +17,12 @@
 COEF_B = -4.775
 COEF_C = 2.0315
 MOMENT = 0.95
+FACTOR = 0.2 * math.sqrt(max(R, C))
+
+AXES = ("dp", "fsdp")
+SMEM = pl.BlockSpec(memory_space=pltpu.SMEM)
+VMEM = pl.BlockSpec(memory_space=pltpu.VMEM)
+ANY = pl.BlockSpec(memory_space=pl.ANY)
 
 
 def orthogonalize(stack):
@@ -29,7 +38,7 @@
     return current
 
 
-def per_device(grads, owner_slot, momentum):
+def per_device_general(grads, owner_slot, momentum):
     partial_rows = grads[0]
     mats, rows_shard, width = partial_rows.shape
     n_replica = lax.axis_size("dp")
@@ -43,7 +52,6 @@
     holder = jnp.sum(jnp.where(matched, jnp.arange(mats, dtype=jnp.int32)[None, :], 0), axis=1)
     filled = jnp.any(matched, axis=1)
     outgoing = jnp.where(filled[:, None, None], jnp.take(reduced, holder, axis=0), 0.0)
-    outgoing = outgoing.reshape(n_replica, n_shard, cap, rows_owner, width)
     arrived = lax.all_to_all(
         outgoing.reshape(owners, cap, rows_owner, width),
         ("dp", "fsdp"),
@@ -58,8 +66,7 @@
     buffer = MOMENT * momentum.astype(jnp.float32) + whole
     new_momentum = buffer.astype(jnp.bfloat16)
     nesterov = whole + MOMENT * buffer
-    factor = 0.2 * math.sqrt(max(R, C))
-    ortho = (factor * orthogonalize(nesterov)).astype(jnp.bfloat16)
+    ortho = (FACTOR * orthogonalize(nesterov)).astype(jnp.bfloat16)
     leaving = jnp.transpose(
         ortho.reshape(cap, n_shard, n_replica, rows_owner, width), (2, 1, 0, 3, 4)
     )
@@ -76,8 +83,319 @@
     return (updates, new_momentum)
 
 
+def here():
+    d = lax.axis_index("dp")
+    return d // 2, d % 2, lax.axis_index("fsdp")
+
+
+def matrix_at(slots, chip, core):
+    slot = (chip // 2) * 4 + core * 2 + chip % 2
+    found = jnp.int32(-1)
+    for j in range(4):
+        found = jnp.where(slots[j] == slot, jnp.int32(j), found)
+    return found
+
+
+def deal(slots):
+    at = [[matrix_at(slots, chip, core) for core in (0, 1)] for chip in range(4)]
+    one, zero = jnp.int32(1), jnp.int32(0)
+    extra = [
+        jnp.where(at[q][0] >= 0, one, zero) + jnp.where(at[q][1] >= 0, one, zero) - 1
+        for q in range(4)
+    ]
+    row = [extra[y] + extra[2 + y] for y in (0, 1)]
+    out_y = [
+        jnp.where((row[q % 2] > 0) & (extra[q ^ 1] < 0), one, zero) for q in range(4)
+    ]
+    out_x = [
+        jnp.where(extra[q] - out_y[q] + out_y[q ^ 1] > 0, one, zero) for q in range(4)
+    ]
+    keep = [jnp.where(at[q][0] >= 0, at[q][0], at[q][1]) for q in range(4)]
+    give = [jnp.where(at[q][1] >= 0, at[q][1], at[q][0]) for q in range(4)]
+    matrix = [
+        jnp.clip(
+            jnp.where(
+                out_y[q ^ 1] > 0, give[q ^ 1], jnp.where(out_x[q ^ 2] > 0, give[q ^ 2], keep[q])
+            ),
+            0,
+            3,
+        )
+        for q in range(4)
+    ]
+    return at, out_x, out_y, matrix
+
+
+def pick(values, index):
+    result = values[0]
+    for k in range(1, len(values)):
+        result = jnp.where(index == k, values[k], result)
+    return result
+
+
+def sum_kernel(slots, own, other, mom, mom_other, to_x, to_y, to_d, mom_out):
+    x, c, y = here()
+
+    @pl.when(c == 1)
+    def _():
+        at, _, _, matrix = deal([slots[j] for j in range(4)])
+        q = 2 * x + y
+        for out, flip in ((to_d, 3), (to_x, 2), (to_y, 1)):
+            m = pick([matrix[k ^ flip] for k in range(4)], q)
+            out[...] = own[0, m] + other[0, m]
+        mine = pick([at[k][1] for k in range(4)], q) >= 0
+
+        @pl.when(mine)
+        def _():
+            mom_out[...] = mom[0]
+
+        @pl.when(jnp.logical_not(mine))
+        def _():
+            mom_out[...] = mom_other[0]
+
+
+def polynomial_step(current):
+    contract = functools.partial(
+        lax.dot_general, precision=lax.Precision.HIGH, preferred_element_type=jnp.float32
+    )
+    gram = contract(current, current, (((1,), (1,)), ((), ())))
+    square = contract(gram, gram, (((1,), (0,)), ((), ())))
+    poly = COEF_B * gram + COEF_C * square
+    return COEF_A * current + contract(poly, current, (((1,), (0,)), ((), ())))
+
+
+def first_kernel(
+    steps, slots, own, other, in_x, in_y, in_d, mom, mom_other, mom_x, mom_y, new, current
+):
+    x, c, y = here()
+    half = own.shape[2]
+
+    @pl.when(c == 0)
+    def _():
+        at, out_x, out_y, matrix = deal([slots[j] for j in range(4)])
+        q = 2 * x + y
+        m = pick(matrix, q)
+        from_y = pick([out_y[k ^ 1] for k in range(4)], q) > 0
+        from_x = pick([out_x[k ^ 2] for k in range(4)], q) > 0
+        from_0 = pick([at[k][0] for k in range(4)], q) >= 0
+        pieces = []
+        for part, start in enumerate((y * half, (1 - y) * half)):
+            rows = pl.ds(pl.multiple_of(start, half), half)
+            if part == 0:
+                total = (own[0, m] + other[0, m]) + in_x[...]
+            else:
+                total = in_y[...] + in_d[...]
+            held = jnp.where(from_0, mom[0, rows], mom_other[0, rows])
+            held = jnp.where(from_x, mom_x[rows], held)
+            held = jnp.where(from_y, mom_y[rows], held)
+            buffer = MOMENT * held.astype(jnp.float32) + total
+            new[rows] = buffer.astype(jnp.bfloat16)
+            pieces.append(total + MOMENT * buffer)
+        nesterov = jnp.concatenate(pieces, axis=0)
+        norm = jnp.sqrt(jnp.sum(nesterov * nesterov))
+        value = nesterov / (norm + 1e-07)
+        for _ in range(steps):
+            value = polynomial_step(value)
+        current[...] = value
+
+
+def middle_kernel(steps, before, after):
+    _, c, _ = here()
+
+    @pl.when(c == 0)
+    def _():
+        value = before[...]
+        for _ in range(steps):
+            value = polynomial_step(value)
+        after[...] = value
+
+
+def last_kernel(steps, before, mine, others):
+    _, c, _ = here()
+    half = mine.shape[0]
+
+    @pl.when(c == 0)
+    def _():
+        value = before[...]
+        for _ in range(steps):
+            value = polynomial_step(value)
+        value = (FACTOR * value).astype(jnp.bfloat16)
+        mine[...] = value[:half]
+        others[...] = value[half:]
+
+
+def back_kernel(slots, new_x, new_y, back):
+    x, c, y = here()
+
+    @pl.when(c == 1)
+    def _():
+        _, out_x, _, _ = deal([slots[j] for j in range(4)])
+        along_x = pick(out_x, 2 * x + y) > 0
+        back[...] = jnp.where(along_x, new_x[...], new_y[...])
+
+
+def momentum_kernel(slots, mom, new, back, new_in, out):
+    x, c, y = here()
+    at, out_x, out_y, _ = deal([slots[j] for j in range(4)])
+    q = 2 * x + y
+    at_0 = pick([at[k][0] for k in range(4)], q) >= 0
+    at_1 = pick([at[k][1] for k in range(4)], q) >= 0
+    gone = pick([out_x[k] + out_y[k] for k in range(4)], q) > 0
+    mine = jnp.where(c == 0, at_0, at_1)
+    away = jnp.where(c == 0, gone & jnp.logical_not(at_1), gone)
+
+    @pl.when(jnp.logical_not(mine))
+    def _():
+        out[0] = (MOMENT * mom[0].astype(jnp.float32)).astype(jnp.bfloat16)
+
+    @pl.when(mine & (c == 0) & away)
+    def _():
+        out[0] = new_in[...]
+
+    @pl.when(mine & (c == 0) & jnp.logical_not(away))
+    def _():
+        out[0] = new[...]
+
+    @pl.when(mine & (c == 1) & away)
+    def _():
+        out[0] = back[...]
+
+    @pl.when(mine & (c == 1) & jnp.logical_not(away))
+    def _():
+        out[0] = new_in[...]
+
+
+def gather_kernel(slots, mine, up_l, up_x, up_y, up_d, in_x, in_y, in_d, out, sems):
+    x, c, y = here()
+    _, _, _, matrix = deal([slots[j] for j in range(4)])
+    q = 2 * x + y
+    for core, sources in ((0, (mine, in_y, in_x, in_d)), (1, (up_l, up_y, up_x, up_d))):
+
+        @pl.when(c == core)
+        def _():
+            copies = []
+            for flip, source in enumerate(sources):
+                m = pick([matrix[k ^ flip] for k in range(4)], q)
+                copy = pltpu.make_async_copy(source, out.at[m], sems.at[flip])
+                copy.start()
+                copies.append(copy)
+            for copy in copies:
+                copy.wait()
+
+
+def chip_device(x, c, y):
+    return (2 * x + c) * 2 + y
+
+
+CHIPS = [(x, y) for x in (0, 1) for y in (0, 1)]
+
+
+def swap_cores(value):
+    pairs = [
+        (chip_device(x, c, y), chip_device(x, 1 - c, y)) for x, y in CHIPS for c in (0, 1)
+    ]
+    return lax.ppermute(value, AXES, pairs)
+
+
+def across(value, sender, flip_x, flip_y):
+    pairs = [
+        (chip_device(x, sender, y), chip_device(x ^ flip_x, 1 - sender, y ^ flip_y))
+        for x, y in CHIPS
+    ]
+    pairs += [(chip_device(x, 1 - sender, y), chip_device(x, sender, y)) for x, y in CHIPS]
+    return lax.ppermute(value, AXES, pairs)
+
+
+def between_ones(value, flip_x, flip_y):
+    pairs = [
+        (chip_device(x, 1, y), chip_device(x ^ flip_x, 1, y ^ flip_y)) for x, y in CHIPS
+    ]
+    pairs += [(chip_device(x, 0, y), chip_device(x, 0, y)) for x, y in CHIPS]
+    return lax.ppermute(value, AXES, pairs)
+
+
+def run(kernel, in_specs, out_shapes, out_specs=None, scratch=(), flops=0, moved=0):
+    return pl.pallas_call(
+        kernel,
+        in_specs=in_specs,
+        out_shape=out_shapes,
+        out_specs=out_specs if out_specs is not None else [VMEM] * len(out_shapes),
+        scratch_shapes=list(scratch),
+        compiler_params=pltpu.CompilerParams(vmem_limit_bytes=24 * 2**20),
+        cost_estimate=pl.CostEstimate(flops=flops, bytes_accessed=moved, transcendentals=0),
+    )
+
+
+def per_device_chips(grads, owner_slot, momentum):
+    _, mats, half, width = grads.shape
+    rows = momentum.shape[1]
+    f32, bf16 = jnp.float32, jnp.bfloat16
+    piece = jax.ShapeDtypeStruct((half, width), f32)
+    whole = jax.ShapeDtypeStruct((rows, width), f32)
+    moment = jax.ShapeDtypeStruct((rows, width), bf16)
+    update = jax.ShapeDtypeStruct((half, width), bf16)
+    step_flops = 6 * (2 * rows * rows * width * 2 + 2 * rows * rows * rows)
+
+    grads_other = swap_cores(grads)
+    mom_other = swap_cores(momentum)
+    to_x, to_y, to_d, mom_out = run(
+        sum_kernel, [SMEM] + [VMEM] * 4, [piece, piece, piece, moment], moved=3 * 2**20
+    )(owner_slot, grads, grads_other, momentum, mom_other)
+    in_d = across(to_d, 1, 1, 1)
+    in_x = across(to_x, 1, 1, 0)
+    in_y = across(to_y, 1, 0, 1)
+    mom_x = across(mom_out, 1, 1, 0)
+    mom_y = across(mom_out, 1, 0, 1)
+    new, current = run(
+        functools.partial(first_kernel, 1),
+        [SMEM] + [VMEM] * 9,
+        [moment, whole],
+        flops=step_flops,
+        moved=3 * 2**20,
+    )(owner_slot, grads, grads_other, in_x, in_y, in_d, momentum, mom_other, mom_x, mom_y)
+    new_l = swap_cores(new)
+    (current,) = run(
+        functools.partial(middle_kernel, 2), [VMEM], [whole], flops=2 * step_flops, moved=2**20
+    )(current)
+    new_x = between_ones(new_l, 1, 0)
+    new_y = between_ones(new_l, 0, 1)
+    mine, others = run(
+        functools.partial(last_kernel, 2), [VMEM], [update, update], flops=2 * step_flops, moved=2**20
+    )(current)
+    up_d = across(others, 0, 1, 1)
+    up_x = across(mine, 0, 1, 0)
+    up_y = across(others, 0, 0, 1)
+    up_l = swap_cores(mine)
+    (back,) = run(back_kernel, [SMEM, VMEM, VMEM], [moment], moved=2**19)(owner_slot, new_x, new_y)
+    back_in = swap_cores(back)
+    new_in = jnp.where(lax.axis_index("dp") % 2 == 0, back_in, new_l)
+    (new_momentum,) = run(
+        momentum_kernel,
+        [SMEM] + [VMEM] * 4,
+        [jax.ShapeDtypeStruct(momentum.shape, bf16)],
+        moved=2**19,
+    )(owner_slot, momentum, new, back, new_in)
+    over_d, over_x, over_y = swap_cores(up_d), swap_cores(up_x), swap_cores(up_y)
+    (updates,) = run(
+        gather_kernel,
+        [SMEM] + [VMEM] * 8,
+        [jax.ShapeDtypeStruct((mats, half, width), bf16)],
+        out_specs=[ANY],
+        scratch=[pltpu.SemaphoreType.DMA((4,))],
+        moved=2**20,
+    )(owner_slot, mine, up_l, up_x, up_y, up_d, over_x, over_y, over_d)
+    return (updates, new_momentum)
+
+
 def solution(mesh):
     placed = (P("dp", "expert", "fsdp", None), P("expert"), P(("dp", "expert", "fsdp"), None, None))
+    n_replica, n_shard = mesh.shape["dp"], mesh.shape["fsdp"]
+
+    def per_device(grads, owner_slot, momentum):
+        mats, cap = grads.shape[1], momentum.shape[0]
+        if (n_replica, n_shard, mats, cap) == (4, 2, 4, 1):
+            return per_device_chips(grads, owner_slot, momentum)
+        return per_device_general(grads, owner_slot, momentum)
+
     return jax.shard_map(
         per_device,
         mesh=mesh,

time: 90.5 us -> 42.4 us (0.47)
  waiting for transfers between devices: 45.4 us -> 15.1 us
  between operations: 14.9 us -> 0.76 us
  Pallas kernels: 0 us -> 11.1 us
  matrix products: 8.22 us -> 0 us
  blocking collectives: 7.32 us -> 0 us
  starting transfers between devices: 6.95 us -> 12.3 us
  other arithmetic: 2.79 us -> 0.03 us
  local copies, waits for them, and re-layouts: 4.55 us -> 2.84 us
    reduce_scatter x1 -> x0, waiting for transfers between devices: 30 us -> none  [per_device(): lax.psum_scatter(partial_rows, 'dp', scatter_dimension=1, tiled=True)]
    ppermute x0 -> x18, waiting for transfers between devices: none -> 15.1 us  [the longest x8 9.45 us: across(): return lax.ppermute(value, AXES, pairs)]
    all_to_all x2 -> x0, waiting for transfers between devices: 14.7 us -> none  [the longest x1 8.76 us: per_device(): lax.all_to_all(outgoing.reshape(owners, cap, rows_owner, width), ('dp', '...]
    ppermute x0 -> x18, starting transfers between devices: none -> 12.3 us  [the longest x8 6.93 us: across(): return lax.ppermute(value, AXES, pairs)]
    pallas_call x0 -> x7, Pallas kernels: none -> 11.1 us  [the longest x1 2.48 us: per_device_chips(): run(functools.partial(first_kernel, 1), [SMEM] + [VMEM] * 9, [moment, who...]
    dot_general x15 -> x0, matrix products: 8.22 us -> none  [the longest x5 3.23 us: orthogonalize(): jnp.einsum('krs,ksc->krc', poly, current, precision=lax.Precision.HIGHEST)]
    all_gather x1 -> x0, blocking collectives: 7.32 us -> none  [per_device(): updates = lax.all_gather(mine, 'dp', axis=1, tiled=True)]
    all_to_all x2 -> x0, starting transfers between devices: 6.91 us -> none  [the longest x1 3.49 us: per_device(): lax.all_to_all(outgoing.reshape(owners, cap, rows_owner, width), ('dp', '...]
  transfers between devices with their start and end apart: 3 -> 18, of which waited for: 3 -> 10; matrix products, arithmetic and copies ran while one was open for 0% -> 0% of each run, Pallas kernels for 0% -> 16%
where the time goes in v1:
time: 42.4 us; the launch traced here: 42.1 us
  waiting for transfers between devices  15.1 us (36%)
  starting transfers between devices  12.3 us (29%)
  Pallas kernels  11.1 us (26%)
  local copies, waits for them, and re-layouts  2.84 us (7%)
  between operations  0.76 us (2%)
    ppermute x8, waiting for transfers between devices, across(): return lax.ppermute(value, AXES, pairs)  9.45 us
    ppermute x8, starting transfers between devices, across(): return lax.ppermute(value, AXES, pairs)  6.93 us
    ppermute x8, waiting for transfers between devices, swap_cores(): return lax.ppermute(value, AXES, pairs)  5.66 us
    ppermute x8, starting transfers between devices, swap_cores(): return lax.ppermute(value, AXES, pairs)  4.08 us
    unnamed x10, local copies, waits for them, and re-layouts  2.84 us
    pallas_call x1, Pallas kernels, per_device_chips(): run(functools.partial(first_kernel, 1), [SMEM] + [VMEM] * 9, [moment, who...  2.48 us
    pallas_call x1, Pallas kernels, per_device_chips(): run(functools.partial(middle_kernel, 2), [VMEM], [whole], flops=2 * step_...  2.33 us
    pallas_call x1, Pallas kernels, per_device_chips(): run(functools.partial(last_kernel, 2), [VMEM], [update, update], flops=2...  2.32 us
  transfers between devices with their start and end apart: 18, of which 10 were waited for; matrix products, arithmetic and copies ran while one was open for 0% of the time, Pallas kernels for 16%

profile of v1, /device:TPU:0, one launch (start us, length us, event | category | flops | bytes accessed | tf_op | source)
XLA Modules:
  0.0 42.1 jit_solution(8604505533279204644)
XLA Ops:
  1.2 2.8 %collective-permute-done.1.mom_other = bf16[1,256,512]{2,1,0:T(8,128)(2,1)S(1)} collective-permute-done((bf16[1,256,512]{2,1,0:T(8,128)(2,1)}, bf16[1,256,512]{2,1,0:T(8,128)(2,1)S(1)}, u32[]{:S(2)}, u32[]{:S(2)}) %collective-permute-start.1) | collective-permute-done | bytes 262176 | tf_op jit(solution)/shard_map/ppermute | solution.py:296
  4.0 1.2 %copy-done = f32[1,4,128,512]{3,2,1,0:T(8,128)S(1)} copy-done((f32[1,4,128,512]{3,2,1,0:T(8,128)S(1)}, f32[1,4,128,512]{3,2,1,0:T(8,128)}, u32[]{:S(2)}) %copy-start) | copy-done | bytes 1048600
  5.3 0.9 %copy-done.1 = bf16[1,256,512]{2,1,0:T(8,128)(2,1)S(1)} copy-done((bf16[1,256,512]{2,1,0:T(8,128)(2,1)S(1)}, bf16[1,256,512]{2,1,0:T(8,128)(2,1)}, u32[]{:S(2)}) %copy-start.1) | copy-done | bytes 262168
  6.2 0.7 %copy-done.3 = s32[4]{0:T(128)S(1)} copy-done((s32[4]{0:T(128)S(1)}, s32[4]{0:T(128)}, u32[]{:S(2)}) %copy-start.3) | copy-done | bytes 40
  8.0 2.4 %collective-permute-start.3 = (f32[128,512]{1,0:T(8,128)S(1)}, f32[128,512]{1,0:T(8,128)S(1)}, u32[]{:S(2)}, u32[]{:S(2)}) collective-permute-start(f32[128,512]{1,0:T(8,128)S(1)} %get-tuple-element.11), channel_id=1, source_target_pairs={{8,1},{9,0},{24,17},{25,16},{0,8},{1,9},{16,24},{17,25},{10,3},{11... | collective-permute-start | bytes 786440 | tf_op jit(solution)/shard_map/ppermute | solution.py:305
  10.8 1.3 %collective-permute-start.5 = (bf16[256,512]{1,0:T(8,128)(2,1)S(1)}, bf16[256,512]{1,0:T(8,128)(2,1)S(1)}, u32[]{:S(2)}, u32[]{:S(2)}) collective-permute-start(bf16[256,512]{1,0:T(8,128)(2,1)S(1)} %get-tuple-element.13), channel_id=1, source_target_pairs={{8,16},{9,17},{24,0},{25,1},{0,8},{1,9},{16,24},{17,25},{10,18},{1... | collective-permute-start | bytes 786440 | tf_op jit(solution)/shard_map/ppermute | solution.py:305
  12.4 1.9 %collective-permute-done.2.in_x = f32[128,512]{1,0:T(8,128)S(1)} collective-permute-done((f32[128,512]{1,0:T(8,128)S(1)}, f32[128,512]{1,0:T(8,128)S(1)}, u32[]{:S(2)}, u32[]{:S(2)}) %collective-permute-start.2) | collective-permute-done | bytes 262176 | tf_op jit(solution)/shard_map/ppermute | solution.py:305
  14.3 1.4 %collective-permute-done.3.in_y = f32[128,512]{1,0:T(8,128)S(1)} collective-permute-done((f32[128,512]{1,0:T(8,128)S(1)}, f32[128,512]{1,0:T(8,128)S(1)}, u32[]{:S(2)}, u32[]{:S(2)}) %collective-permute-start.3) | collective-permute-done | bytes 262176 | tf_op jit(solution)/shard_map/ppermute | solution.py:305
  15.6 2.9 %collective-permute-done.4.in_d = f32[128,512]{1,0:T(8,128)S(1)} collective-permute-done((f32[128,512]{1,0:T(8,128)S(1)}, f32[128,512]{1,0:T(8,128)S(1)}, u32[]{:S(2)}, u32[]{:S(2)}) %collective-permute-start.4) | collective-permute-done | bytes 262176 | tf_op jit(solution)/shard_map/ppermute | solution.py:305
  18.5 1.5 %collective-permute-done.5.mom_x = bf16[256,512]{1,0:T(8,128)(2,1)S(1)} collective-permute-done((bf16[256,512]{1,0:T(8,128)(2,1)S(1)}, bf16[256,512]{1,0:T(8,128)(2,1)S(1)}, u32[]{:S(2)}, u32[]{:S(2)}) %collective-permute-start.5) | collective-permute-done | bytes 262176 | tf_op jit(solution)/shard_map/ppermute | solution.py:305
  20.1 1.2 %collective-permute-done.6.mom_y = bf16[256,512]{1,0:T(8,128)(2,1)S(1)} collective-permute-done((bf16[256,512]{1,0:T(8,128)(2,1)S(1)}, bf16[256,512]{1,0:T(8,128)(2,1)S(1)}, u32[]{:S(2)}, u32[]{:S(2)}) %collective-permute-start.6) | collective-permute-done | bytes 262176 | tf_op jit(solution)/shard_map/ppermute | solution.py:305
  21.3 2.5 %shard_map.51 = (bf16[256,512]{1,0:T(8,128)(2,1)S(1)}, f32[256,512]{1,0:T(8,128)S(1)}) custom-call(s32[4]{0:T(128)S(1)} %copy-done.3, f32[1,4,128,512]{3,2,1,0:T(8,128)S(1)} %copy-done, f32[1,4,128,512]{3,2,1,0:T(8,128)S(1)} %collective-permute-done.other, f32[128,512]{1,0:T(8,128)S(1)} %collective-permute-done.2.in_x, ...), custom_call_target="tpu_custom_call" | custom-call | flops 1006632960 | bytes 3145728 | tf_op jit(solution)/shard_map/pallas_call | solution.py:348
  23.8 1.5 %collective-permute-done.14 = bf16[256,512]{1,0:T(8,128)(2,1)S(1)} collective-permute-done((bf16[256,512]{1,0:T(8,128)(2,1)S(1)}, bf16[256,512]{1,0:T(8,128)(2,1)S(1)}, u32[]{:S(2)}, u32[]{:S(2)}) %collective-permute-start.14) | collective-permute-done | bytes 262176 | tf_op jit(solution)/shard_map/ppermute | solution.py:296
  25.3 0.7 %collective-permute-start.15 = (bf16[256,512]{1,0:T(8,128)(2,1)S(1)}, bf16[256,512]{1,0:T(8,128)(2,1)S(1)}, u32[]{:S(2)}, u32[]{:S(2)}) collective-permute-start(bf16[256,512]{1,0:T(8,128)(2,1)S(1)} %collective-permute-done.14), channel_id=1, source_target_pairs={{8,24},{9,25},{24,8},{25,9},{0,0},{1,1},{16,16},{17,17},{10,26},{1... | collective-permute-start | bytes 786440 | tf_op jit(solution)/shard_map/ppermute | solution.py:313
  26.0 0.7 %collective-permute-start.16 = (bf16[256,512]{1,0:T(8,128)(2,1)S(1)}, bf16[256,512]{1,0:T(8,128)(2,1)S(1)}, u32[]{:S(2)}, u32[]{:S(2)}) collective-permute-start(bf16[256,512]{1,0:T(8,128)(2,1)S(1)} %collective-permute-done.14), channel_id=1, source_target_pairs={{8,9},{9,8},{24,25},{25,24},{0,0},{1,1},{16,16},{17,17},{10,11},{1... | collective-permute-start | bytes 786440 | tf_op jit(solution)/shard_map/ppermute | solution.py:313
  26.7 2.3 %shard_map.52.before = f32[256,512]{1,0:T(8,128)S(1)} custom-call(f32[256,512]{1,0:T(8,128)S(1)} %get-tuple-element.14.before), custom_call_target="tpu_custom_call" | custom-call | flops 2013265920 | bytes 1048576 | tf_op jit(solution)/shard_map/pallas_call | solution.py:356
  29.0 2.3 %shard_map.53 = (bf16[128,512]{1,0:T(8,128)(2,1)S(1)}, bf16[128,512]{1,0:T(8,128)(2,1)S(1)}) custom-call(f32[256,512]{1,0:T(8,128)S(1)} %shard_map.52.before), custom_call_target="tpu_custom_call" | custom-call | flops 2013265920 | bytes 1048576 | tf_op jit(solution)/shard_map/pallas_call | solution.py:361
  31.4 0.9 %collective-permute-start.9 = (bf16[128,512]{1,0:T(8,128)(2,1)S(1)}, bf16[128,512]{1,0:T(8,128)(2,1)S(1)}, u32[]{:S(2)}, u32[]{:S(2)}) collective-permute-start(bf16[128,512]{1,0:T(8,128)(2,1)S(1)} %get-tuple-element.16), channel_id=1, source_target_pairs={{0,9},{1,8},{16,25},{17,24},{8,0},{9,1},{24,16},{25,17},{2,11},{3,... | collective-permute-start | bytes 393224 | tf_op jit(solution)/shard_map/ppermute | solution.py:305
  32.4 1.0 %collective-permute-start.10 = (bf16[128,512]{1,0:T(8,128)(2,1)S(1)}, bf16[128,512]{1,0:T(8,128)(2,1)S(1)}, u32[]{:S(2)}, u32[]{:S(2)}) collective-permute-start(bf16[128,512]{1,0:T(8,128)(2,1)S(1)} %get-tuple-element.16), channel_id=1, source_target_pairs={{0,25},{1,24},{16,9},{17,8},{8,0},{9,1},{24,16},{25,17},{2,27},{3,... | collective-permute-start | bytes 393224 | tf_op jit(solution)/shard_map/ppermute | solution.py:305
  33.9 2.0 %collective-permute-start.17 = (bf16[256,512]{1,0:T(8,128)(2,1)S(1)}, bf16[256,512]{1,0:T(8,128)(2,1)S(1)}, u32[]{:S(2)}, u32[]{:S(2)}) collective-permute-start(bf16[256,512]{1,0:T(8,128)(2,1)S(1)} %shard_map.55.back), channel_id=1, source_target_pairs={{0,8},{8,0},{1,9},{9,1},{16,24},{24,16},{17,25},{25,17},{2,10},{10... | collective-permute-start | bytes 786440 | tf_op jit(solution)/shard_map/ppermute | solution.py:296
  37.0 0.9 %collective-permute-start.12 = (bf16[128,512]{1,0:T(8,128)(2,1)S(1)}, bf16[128,512]{1,0:T(8,128)(2,1)S(1)}, u32[]{:S(2)}, u32[]{:S(2)}) collective-permute-start(bf16[128,512]{1,0:T(8,128)(2,1)S(1)} %collective-permute-done.9.up_y), channel_id=1, source_target_pairs={{0,8},{8,0},{1,9},{9,1},{16,24},{24,16},{17,25},{25,17},{2,10},{10... | collective-permute-start | bytes 393224 | tf_op jit(solution)/shard_map/ppermute | solution.py:296
  38.0 1.0 %collective-permute-done.12.in_y = bf16[128,512]{1,0:T(8,128)(2,1)S(1)} collective-permute-done((bf16[128,512]{1,0:T(8,128)(2,1)S(1)}, bf16[128,512]{1,0:T(8,128)(2,1)S(1)}, u32[]{:S(2)}, u32[]{:S(2)}) %collective-permute-start.12) | collective-permute-done | bytes 131104 | tf_op jit(solution)/shard_map/ppermute | solution.py:296
  39.3 1.4 %shard_map.54 = bf16[4,128,512]{2,1,0:T(8,128)(2,1)} custom-call(s32[4]{0:T(128)S(1)} %copy-done.4, bf16[128,512]{1,0:T(8,128)(2,1)S(1)} %get-tuple-element.15.mine, bf16[128,512]{1,0:T(8,128)(2,1)S(1)} %collective-permute-done.7.up_l, bf16[128,512]{1,0:T(8,128)(2,1)S(1)} %collective-permute-done.8.up_x, bf16[128,512]{1,0:T(8,128)(2,1)S(1)} %collective-permute-done.9.up_y, ...), custom_call_target="tpu_custom_call" | custom-call | bytes 1048576 | tf_op jit(solution)/shard_map/pallas_call | solution.py:378
  40.8 1.4 %shard_map.56 = bf16[1,256,512]{2,1,0:T(8,128)(2,1)} custom-call(s32[4]{0:T(128)S(1)} %copy-done.4, bf16[1,256,512]{2,1,0:T(8,128)(2,1)S(1)} %copy-done.2, bf16[256,512]{1,0:T(8,128)(2,1)S(1)} %get-tuple-element.17.new, bf16[256,512]{1,0:T(8,128)(2,1)S(1)} %shard_map.55.back, bf16[256,512]{1,0:T(8,128)(2,1)S(1)} %broadcast_select_fusion.new_in), custom_call_target="tpu_custom_call" | custom-call | bytes 524288 | tf_op jit(solution)/shard_map/pallas_call | solution.py:371
  (30 shorter events, 4.6 us)
Async XLA Ops:
  0.6 3.4 %collective-permute-start = (f32[1,4,128,512]{3,2,1,0:T(8,128)}, f32[1,4,128,512]{3,2,1,0:T(8,128)S(1)}, u32[]{:S(2)}, u32[]{:S(2)}) collective-permute-start(f32[1,4,128,512]{3,2,1,0:T(8,128)} %own.3), channel_id=1, source_target_pairs={{0,8},{8,0},{1,9},{9,1},{16,24},{24,16},{17,25},{25,17},{2,10},{10... | collective-permute-start | bytes 3145736 | tf_op jit(solution)/shard_map/ppermute | solution.py:296
  1.1 2.9 %collective-permute-start.1 = (bf16[1,256,512]{2,1,0:T(8,128)(2,1)}, bf16[1,256,512]{2,1,0:T(8,128)(2,1)S(1)}, u32[]{:S(2)}, u32[]{:S(2)}) collective-permute-start(bf16[1,256,512]{2,1,0:T(8,128)(2,1)} %mom.5), channel_id=1, source_target_pairs={{0,8},{8,0},{1,9},{9,1},{16,24},{24,16},{17,25},{25,17},{2,10},{10... | collective-permute-start | bytes 786440 | tf_op jit(solution)/shard_map/ppermute | solution.py:296
  4.0 1.2 %copy-start = (f32[1,4,128,512]{3,2,1,0:T(8,128)S(1)}, f32[1,4,128,512]{3,2,1,0:T(8,128)}, u32[]{:S(2)}) copy-start(f32[1,4,128,512]{3,2,1,0:T(8,128)} %own.3) | copy-start | bytes 3145732
  5.2 0.9 %copy-start.1 = (bf16[1,256,512]{2,1,0:T(8,128)(2,1)S(1)}, bf16[1,256,512]{2,1,0:T(8,128)(2,1)}, u32[]{:S(2)}) copy-start(bf16[1,256,512]{2,1,0:T(8,128)(2,1)} %mom.5) | copy-start | bytes 786436
  6.2 0.7 %copy-start.3 = (s32[4]{0:T(128)S(1)}, s32[4]{0:T(128)}, u32[]{:S(2)}) copy-start(s32[4]{0:T(128)} %slots.9) | copy-start | bytes 52
  6.9 14.4 %copy-start.2 = (bf16[1,256,512]{2,1,0:T(8,128)(2,1)S(1)}, bf16[1,256,512]{2,1,0:T(8,128)(2,1)}, u32[]{:S(2)}) copy-start(bf16[1,256,512]{2,1,0:T(8,128)(2,1)} %mom.5) | copy-start | bytes 786436
  7.4 6.9 %collective-permute-start.2 = (f32[128,512]{1,0:T(8,128)S(1)}, f32[128,512]{1,0:T(8,128)S(1)}, u32[]{:S(2)}, u32[]{:S(2)}) collective-permute-start(f32[128,512]{1,0:T(8,128)S(1)} %get-tuple-element.10), channel_id=1, source_target_pairs={{8,16},{9,17},{24,0},{25,1},{0,8},{1,9},{16,24},{17,25},{10,18},{1... | collective-permute-start | bytes 786440 | tf_op jit(solution)/shard_map/ppermute | solution.py:305
  8.0 7.6 %collective-permute-start.3 = (f32[128,512]{1,0:T(8,128)S(1)}, f32[128,512]{1,0:T(8,128)S(1)}, u32[]{:S(2)}, u32[]{:S(2)}) collective-permute-start(f32[128,512]{1,0:T(8,128)S(1)} %get-tuple-element.11), channel_id=1, source_target_pairs={{8,1},{9,0},{24,17},{25,16},{0,8},{1,9},{16,24},{17,25},{10,3},{11... | collective-permute-start | bytes 786440 | tf_op jit(solution)/shard_map/ppermute | solution.py:305
  10.5 8.1 %collective-permute-start.4 = (f32[128,512]{1,0:T(8,128)S(1)}, f32[128,512]{1,0:T(8,128)S(1)}, u32[]{:S(2)}, u32[]{:S(2)}) collective-permute-start(f32[128,512]{1,0:T(8,128)S(1)} %get-tuple-element.12), channel_id=1, source_target_pairs={{8,17},{9,16},{24,1},{25,0},{0,8},{1,9},{16,24},{17,25},{10,19},{1... | collective-permute-start | bytes 786440 | tf_op jit(solution)/shard_map/ppermute | solution.py:305
  10.8 9.3 %collective-permute-start.5 = (bf16[256,512]{1,0:T(8,128)(2,1)S(1)}, bf16[256,512]{1,0:T(8,128)(2,1)S(1)}, u32[]{:S(2)}, u32[]{:S(2)}) collective-permute-start(bf16[256,512]{1,0:T(8,128)(2,1)S(1)} %get-tuple-element.13), channel_id=1, source_target_pairs={{8,16},{9,17},{24,0},{25,1},{0,8},{1,9},{16,24},{17,25},{10,18},{1... | collective-permute-start | bytes 786440 | tf_op jit(solution)/shard_map/ppermute | solution.py:305
  12.1 9.2 %collective-permute-start.6 = (bf16[256,512]{1,0:T(8,128)(2,1)S(1)}, bf16[256,512]{1,0:T(8,128)(2,1)S(1)}, u32[]{:S(2)}, u32[]{:S(2)}) collective-permute-start(bf16[256,512]{1,0:T(8,128)(2,1)S(1)} %get-tuple-element.13), channel_id=1, source_target_pairs={{8,1},{9,0},{24,17},{25,16},{0,8},{1,9},{16,24},{17,25},{10,3},{11... | collective-permute-start | bytes 786440 | tf_op jit(solution)/shard_map/ppermute | solution.py:305
  23.7 1.6 %collective-permute-start.14 = (bf16[256,512]{1,0:T(8,128)(2,1)S(1)}, bf16[256,512]{1,0:T(8,128)(2,1)S(1)}, u32[]{:S(2)}, u32[]{:S(2)}) collective-permute-start(bf16[256,512]{1,0:T(8,128)(2,1)S(1)} %get-tuple-element.17.new), channel_id=1, source_target_pairs={{0,8},{8,0},{1,9},{9,1},{16,24},{24,16},{17,25},{25,17},{2,10},{10... | collective-permute-start | bytes 786440 | tf_op jit(solution)/shard_map/ppermute | solution.py:296
  25.3 8.0 %collective-permute-start.15 = (bf16[256,512]{1,0:T(8,128)(2,1)S(1)}, bf16[256,512]{1,0:T(8,128)(2,1)S(1)}, u32[]{:S(2)}, u32[]{:S(2)}) collective-permute-start(bf16[256,512]{1,0:T(8,128)(2,1)S(1)} %collective-permute-done.14), channel_id=1, source_target_pairs={{8,24},{9,25},{24,8},{25,9},{0,0},{1,1},{16,16},{17,17},{10,26},{1... | collective-permute-start | bytes 786440 | tf_op jit(solution)/shard_map/ppermute | solution.py:313
  26.0 7.4 %collective-permute-start.16 = (bf16[256,512]{1,0:T(8,128)(2,1)S(1)}, bf16[256,512]{1,0:T(8,128)(2,1)S(1)}, u32[]{:S(2)}, u32[]{:S(2)}) collective-permute-start(bf16[256,512]{1,0:T(8,128)(2,1)S(1)} %collective-permute-done.14), channel_id=1, source_target_pairs={{8,9},{9,8},{24,25},{25,24},{0,0},{1,1},{16,16},{17,17},{10,11},{1... | collective-permute-start | bytes 786440 | tf_op jit(solution)/shard_map/ppermute | solution.py:313
  31.4 2.0 %copy-start.4 = (s32[4]{0:T(128)S(1)}, s32[4]{0:T(128)}, u32[]{:S(2)}) copy-start(s32[4]{0:T(128)} %slots.9) | copy-start | bytes 52
  31.4 4.7 %collective-permute-start.8 = (bf16[128,512]{1,0:T(8,128)(2,1)S(1)}, bf16[128,512]{1,0:T(8,128)(2,1)S(1)}, u32[]{:S(2)}, u32[]{:S(2)}) collective-permute-start(bf16[128,512]{1,0:T(8,128)(2,1)S(1)} %get-tuple-element.15.mine), channel_id=1, source_target_pairs={{0,24},{1,25},{16,8},{17,9},{8,0},{9,1},{24,16},{25,17},{2,26},{3,... | collective-permute-start | bytes 393224 | tf_op jit(solution)/shard_map/ppermute | solution.py:305
  31.4 5.6 %collective-permute-start.9 = (bf16[128,512]{1,0:T(8,128)(2,1)S(1)}, bf16[128,512]{1,0:T(8,128)(2,1)S(1)}, u32[]{:S(2)}, u32[]{:S(2)}) collective-permute-start(bf16[128,512]{1,0:T(8,128)(2,1)S(1)} %get-tuple-element.16), channel_id=1, source_target_pairs={{0,9},{1,8},{16,25},{17,24},{8,0},{9,1},{24,16},{25,17},{2,11},{3,... | collective-permute-start | bytes 393224 | tf_op jit(solution)/shard_map/ppermute | solution.py:305
  32.4 5.6 %collective-permute-start.10 = (bf16[128,512]{1,0:T(8,128)(2,1)S(1)}, bf16[128,512]{1,0:T(8,128)(2,1)S(1)}, u32[]{:S(2)}, u32[]{:S(2)}) collective-permute-start(bf16[128,512]{1,0:T(8,128)(2,1)S(1)} %get-tuple-element.16), channel_id=1, source_target_pairs={{0,25},{1,24},{16,9},{17,8},{8,0},{9,1},{24,16},{25,17},{2,27},{3,... | collective-permute-start | bytes 393224 | tf_op jit(solution)/shard_map/ppermute | solution.py:305
  33.9 6.8 %collective-permute-start.17 = (bf16[256,512]{1,0:T(8,128)(2,1)S(1)}, bf16[256,512]{1,0:T(8,128)(2,1)S(1)}, u32[]{:S(2)}, u32[]{:S(2)}) collective-permute-start(bf16[256,512]{1,0:T(8,128)(2,1)S(1)} %shard_map.55.back), channel_id=1, source_target_pairs={{0,8},{8,0},{1,9},{9,1},{16,24},{24,16},{17,25},{25,17},{2,10},{10... | collective-permute-start | bytes 786440 | tf_op jit(solution)/shard_map/ppermute | solution.py:296
  35.9 2.0 %collective-permute-start.7 = (bf16[128,512]{1,0:T(8,128)(2,1)S(1)}, bf16[128,512]{1,0:T(8,128)(2,1)S(1)}, u32[]{:S(2)}, u32[]{:S(2)}) collective-permute-start(bf16[128,512]{1,0:T(8,128)(2,1)S(1)} %get-tuple-element.15.mine), channel_id=1, source_target_pairs={{0,8},{8,0},{1,9},{9,1},{16,24},{24,16},{17,25},{25,17},{2,10},{10... | collective-permute-start | bytes 393224 | tf_op jit(solution)/shard_map/ppermute | solution.py:296
  36.0 1.9 %collective-permute-start.11 = (bf16[128,512]{1,0:T(8,128)(2,1)S(1)}, bf16[128,512]{1,0:T(8,128)(2,1)S(1)}, u32[]{:S(2)}, u32[]{:S(2)}) collective-permute-start(bf16[128,512]{1,0:T(8,128)(2,1)S(1)} %collective-permute-done.8.up_x), channel_id=1, source_target_pairs={{0,8},{8,0},{1,9},{9,1},{16,24},{24,16},{17,25},{25,17},{2,10},{10... | collective-permute-start | bytes 393224 | tf_op jit(solution)/shard_map/ppermute | solution.py:296
  37.0 1.9 %collective-permute-start.12 = (bf16[128,512]{1,0:T(8,128)(2,1)S(1)}, bf16[128,512]{1,0:T(8,128)(2,1)S(1)}, u32[]{:S(2)}, u32[]{:S(2)}) collective-permute-start(bf16[128,512]{1,0:T(8,128)(2,1)S(1)} %collective-permute-done.9.up_y), channel_id=1, source_target_pairs={{0,8},{8,0},{1,9},{9,1},{16,24},{24,16},{17,25},{25,17},{2,10},{10... | collective-permute-start | bytes 393224 | tf_op jit(solution)/shard_map/ppermute | solution.py:296
  37.9 1.3 %collective-permute-start.13 = (bf16[128,512]{1,0:T(8,128)(2,1)S(1)}, bf16[128,512]{1,0:T(8,128)(2,1)S(1)}, u32[]{:S(2)}, u32[]{:S(2)}) collective-permute-start(bf16[128,512]{1,0:T(8,128)(2,1)S(1)} %collective-permute-done.10.up_d), channel_id=1, source_target_pairs={{0,8},{8,0},{1,9},{9,1},{16,24},{24,16},{17,25},{25,17},{2,10},{10... | collective-permute-start | bytes 393224 | tf_op jit(solution)/shard_map/ppermute | solution.py:296

commit v2 on v1

--- a/solution.py
+++ b/solution.py
@@ -20,7 +20,6 @@
 FACTOR = 0.2 * math.sqrt(max(R, C))
 
 AXES = ("dp", "fsdp")
-SMEM = pl.BlockSpec(memory_space=pltpu.SMEM)
 VMEM = pl.BlockSpec(memory_space=pltpu.VMEM)
 ANY = pl.BlockSpec(memory_space=pl.ANY)
 
@@ -132,25 +131,62 @@
     return result
 
 
-def sum_kernel(slots, own, other, mom, mom_other, to_x, to_y, to_d, mom_out):
+def load_kernel(grads, momentum, slots, grads_near, momentum_near, plan, slots_near, sems):
+    copies = [
+        pltpu.make_async_copy(source, target, sems.at[k])
+        for k, (source, target) in enumerate(
+            ((slots, slots_near), (momentum.at[0], momentum_near), (grads.at[0], grads_near))
+        )
+    ]
+    for copy in copies:
+        copy.start()
+    copies[0].wait()
     x, c, y = here()
+    at, out_x, out_y, matrix = deal([slots_near[j] for j in range(4)])
+    q = 2 * x + y
+    one, zero = jnp.int32(1), jnp.int32(0)
+    at_0 = pick([at[k][0] for k in range(4)], q) >= 0
+    at_1 = pick([at[k][1] for k in range(4)], q) >= 0
+    leaves_x = pick(out_x, q)
+    leaves_y = pick(out_y, q)
+    comes_x = pick([out_x[k ^ 2] for k in range(4)], q) > 0
+    comes_y = pick([out_y[k ^ 1] for k in range(4)], q) > 0
+    mine = jnp.where(c == 0, at_0, at_1)
+    away = jnp.where((c == 1) | jnp.logical_not(at_1), leaves_x + 2 * leaves_y, zero)
+    entries = [pick([matrix[k ^ flip] for k in range(4)], q) for flip in range(4)]
+    entries.append(jnp.where(comes_y, 3, jnp.where(comes_x, 2, jnp.where(at_0, zero, one))))
+    entries.append(jnp.where(at_1, one, zero))
+    entries.append(jnp.where(mine, one + away, zero))
+    entries.append(leaves_x)
+    row = lax.broadcasted_iota(jnp.int32, plan.shape, 0)
+    table = jnp.zeros(plan.shape, jnp.int32)
+    for k, entry in enumerate(entries):
+        table = jnp.where(row == k, entry, table)
+    plan[...] = table
+    copies[1].wait()
+    copies[2].wait()
+
+
+SOURCE, GIVER, SLOT, LEAVES_X = 4, 5, 6, 7
+
+
+def give_kernel(plan, mom, mom_other, mom_out):
+    _, c, _ = here()
 
     @pl.when(c == 1)
     def _():
-        at, _, _, matrix = deal([slots[j] for j in range(4)])
-        q = 2 * x + y
+        mine = plan[GIVER, 0] == 1
+        mom_out[...] = jnp.where(mine, mom[...], mom_other[0])
+
+
+def sum_kernel(plan, own, other, to_d, to_x, to_y):
+    _, c, _ = here()
+
+    @pl.when(c == 1)
+    def _():
         for out, flip in ((to_d, 3), (to_x, 2), (to_y, 1)):
-            m = pick([matrix[k ^ flip] for k in range(4)], q)
-            out[...] = own[0, m] + other[0, m]
-        mine = pick([at[k][1] for k in range(4)], q) >= 0
-
-        @pl.when(mine)
-        def _():
-            mom_out[...] = mom[0]
-
-        @pl.when(jnp.logical_not(mine))
-        def _():
-            mom_out[...] = mom_other[0]
+            m = plan[flip, 0]
+            out[...] = own[m] + other[0, m]
 
 
 def polynomial_step(current):
@@ -163,39 +199,33 @@
     return COEF_A * current + contract(poly, current, (((1,), (0,)), ((), ())))
 
 
-def first_kernel(
-    steps, slots, own, other, in_x, in_y, in_d, mom, mom_other, mom_x, mom_y, new, current
+def nesterov_kernel(
+    plan, own, other, in_x, in_y, in_d, mom, mom_other, mom_x, mom_y, new, current
 ):
-    x, c, y = here()
-    half = own.shape[2]
+    _, c, y = here()
+    half = own.shape[1]
 
     @pl.when(c == 0)
     def _():
-        at, out_x, out_y, matrix = deal([slots[j] for j in range(4)])
-        q = 2 * x + y
-        m = pick(matrix, q)
-        from_y = pick([out_y[k ^ 1] for k in range(4)], q) > 0
-        from_x = pick([out_x[k ^ 2] for k in range(4)], q) > 0
-        from_0 = pick([at[k][0] for k in range(4)], q) >= 0
+        m = plan[0, 0]
+        source = plan[SOURCE, 0]
+        squares = jnp.float32(0)
         pieces = []
         for part, start in enumerate((y * half, (1 - y) * half)):
             rows = pl.ds(pl.multiple_of(start, half), half)
             if part == 0:
-                total = (own[0, m] + other[0, m]) + in_x[...]
+                total = (own[m] + other[0, m]) + in_x[...]
             else:
                 total = in_y[...] + in_d[...]
-            held = jnp.where(from_0, mom[0, rows], mom_other[0, rows])
-            held = jnp.where(from_x, mom_x[rows], held)
-            held = jnp.where(from_y, mom_y[rows], held)
+            held = pick([mom[rows], mom_other[0, rows], mom_x[rows], mom_y[rows]], source)
             buffer = MOMENT * held.astype(jnp.float32) + total
             new[rows] = buffer.astype(jnp.bfloat16)
-            pieces.append(total + MOMENT * buffer)
-        nesterov = jnp.concatenate(pieces, axis=0)
-        norm = jnp.sqrt(jnp.sum(nesterov * nesterov))
-        value = nesterov / (norm + 1e-07)
-        for _ in range(steps):
-            value = polynomial_step(value)
-        current[...] = value
+            piece = total + MOMENT * buffer
+            squares = squares + jnp.sum(piece * piece)
+            pieces.append(piece)
+        norm = jnp.sqrt(squares) + 1e-07
+        for part in (0, 1):
+            current[part * half : (part + 1) * half] = pieces[part] / norm
 
 
 def middle_kernel(steps, before, after):
@@ -209,7 +239,7 @@
         after[...] = value
 
 
-def last_kernel(steps, before, mine, others):
+def last_kernel(steps, before, others, mine):
     _, c, _ = here()
     half = mine.shape[0]
 
@@ -223,63 +253,45 @@
         others[...] = value[half:]
 
 
-def back_kernel(slots, new_x, new_y, back):
-    x, c, y = here()
+def back_kernel(plan, mom, new_l, new_x, new_y, back, hold):
+    _, c, _ = here()
 
     @pl.when(c == 1)
     def _():
-        _, out_x, _, _ = deal([slots[j] for j in range(4)])
-        along_x = pick(out_x, 2 * x + y) > 0
-        back[...] = jnp.where(along_x, new_x[...], new_y[...])
-
-
-def momentum_kernel(slots, mom, new, back, new_in, out):
-    x, c, y = here()
-    at, out_x, out_y, _ = deal([slots[j] for j in range(4)])
-    q = 2 * x + y
-    at_0 = pick([at[k][0] for k in range(4)], q) >= 0
-    at_1 = pick([at[k][1] for k in range(4)], q) >= 0
-    gone = pick([out_x[k] + out_y[k] for k in range(4)], q) > 0
-    mine = jnp.where(c == 0, at_0, at_1)
-    away = jnp.where(c == 0, gone & jnp.logical_not(at_1), gone)
-
-    @pl.when(jnp.logical_not(mine))
-    def _():
-        out[0] = (MOMENT * mom[0].astype(jnp.float32)).astype(jnp.bfloat16)
-
-    @pl.when(mine & (c == 0) & away)
-    def _():
-        out[0] = new_in[...]
-
-    @pl.when(mine & (c == 0) & jnp.logical_not(away))
-    def _():
-        out[0] = new[...]
-
-    @pl.when(mine & (c == 1) & away)
-    def _():
-        out[0] = back[...]
-
-    @pl.when(mine & (c == 1) & jnp.logical_not(away))
-    def _():
-        out[0] = new_in[...]
-
-
-def gather_kernel(slots, mine, up_l, up_x, up_y, up_d, in_x, in_y, in_d, out, sems):
-    x, c, y = here()
-    _, _, _, matrix = deal([slots[j] for j in range(4)])
-    q = 2 * x + y
+        back[...] = jnp.where(plan[LEAVES_X, 0] == 1, new_x[...], new_y[...])
+
+    faded = (MOMENT * mom[...].astype(jnp.float32)).astype(jnp.bfloat16)
+    slot = jnp.where(c == 1, plan[SLOT, 0], 0)
+    hold[...] = pick([faded, new_l[...], new_x[...], new_y[...]], slot)
+
+
+def finish_kernel(
+    plan, mine, up_l, up_x, up_y, up_d, in_x, in_y, in_d, new, back, hold, updates, moment, sems
+):
+    _, c, _ = here()
     for core, sources in ((0, (mine, in_y, in_x, in_d)), (1, (up_l, up_y, up_x, up_d))):
 
         @pl.when(c == core)
         def _():
-            copies = []
             for flip, source in enumerate(sources):
-                m = pick([matrix[k ^ flip] for k in range(4)], q)
-                copy = pltpu.make_async_copy(source, out.at[m], sems.at[flip])
-                copy.start()
-                copies.append(copy)
-            for copy in copies:
-                copy.wait()
+                m = plan[flip, 0]
+                pltpu.make_async_copy(source, updates.at[m], sems.at[flip]).start()
+
+    slot = plan[SLOT, 0]
+    held = (c == 1) | (slot == 0)
+    for chosen, source in (
+        (held, hold),
+        (jnp.logical_not(held) & (slot == 1), new),
+        (jnp.logical_not(held) & (slot > 1), back),
+    ):
+
+        @pl.when(chosen)
+        def _():
+            pltpu.make_async_copy(source, moment.at[0], sems.at[4]).start()
+
+    for flip in range(4):
+        pltpu.make_async_copy(mine, updates.at[flip], sems.at[flip]).wait()
+    pltpu.make_async_copy(hold, moment.at[0], sems.at[4]).wait()
 
 
 def chip_device(x, c, y):
@@ -302,14 +314,6 @@
         for x, y in CHIPS
     ]
     pairs += [(chip_device(x, 1 - sender, y), chip_device(x, sender, y)) for x, y in CHIPS]
-    return lax.ppermute(value, AXES, pairs)
-
-
-def between_ones(value, flip_x, flip_y):
-    pairs = [
-        (chip_device(x, 1, y), chip_device(x ^ flip_x, 1, y ^ flip_y)) for x, y in CHIPS
-    ]
-    pairs += [(chip_device(x, 0, y), chip_device(x, 0, y)) for x, y in CHIPS]
     return lax.ppermute(value, AXES, pairs)
 
 
@@ -335,54 +339,57 @@
     update = jax.ShapeDtypeStruct((half, width), bf16)
     step_flops = 6 * (2 * rows * rows * width * 2 + 2 * rows * rows * rows)
 
+    near = jax.ShapeDtypeStruct((mats, half, width), f32)
+    table = jax.ShapeDtypeStruct((8, 128), jnp.int32)
+
+    mom_other = swap_cores(momentum)
     grads_other = swap_cores(grads)
-    mom_other = swap_cores(momentum)
-    to_x, to_y, to_d, mom_out = run(
-        sum_kernel, [SMEM] + [VMEM] * 4, [piece, piece, piece, moment], moved=3 * 2**20
-    )(owner_slot, grads, grads_other, momentum, mom_other)
+    own, mom, plan = run(
+        load_kernel,
+        [ANY] * 3,
+        [near, moment, table],
+        scratch=[pltpu.SMEM((mats,), jnp.int32), pltpu.SemaphoreType.DMA((3,))],
+        moved=2**21,
+    )(*(pltpu.with_memory_space_constraint(a, pltpu.HBM) for a in (grads, momentum, owner_slot)))
+    (mom_out,) = run(give_kernel, [VMEM] * 3, [moment], moved=2**18)(plan, mom, mom_other)
+    mom_x = across(mom_out, 1, 1, 0)
+    mom_y = across(mom_out, 1, 0, 1)
+    to_d, to_x, to_y = run(sum_kernel, [VMEM] * 3, [piece, piece, piece], moved=2**20)(
+        plan, own, grads_other
+    )
     in_d = across(to_d, 1, 1, 1)
     in_x = across(to_x, 1, 1, 0)
     in_y = across(to_y, 1, 0, 1)
-    mom_x = across(mom_out, 1, 1, 0)
-    mom_y = across(mom_out, 1, 0, 1)
-    new, current = run(
-        functools.partial(first_kernel, 1),
-        [SMEM] + [VMEM] * 9,
-        [moment, whole],
-        flops=step_flops,
-        moved=3 * 2**20,
-    )(owner_slot, grads, grads_other, in_x, in_y, in_d, momentum, mom_other, mom_x, mom_y)
-    new_l = swap_cores(new)
+    new, current = run(nesterov_kernel, [VMEM] * 10, [moment, whole], moved=2**20)(
+        plan, own, grads_other, in_x, in_y, in_d, mom, mom_other, mom_x, mom_y
+    )
+    new_x = across(new, 0, 1, 0)
     (current,) = run(
         functools.partial(middle_kernel, 2), [VMEM], [whole], flops=2 * step_flops, moved=2**20
     )(current)
-    new_x = between_ones(new_l, 1, 0)
-    new_y = between_ones(new_l, 0, 1)
-    mine, others = run(
-        functools.partial(last_kernel, 2), [VMEM], [update, update], flops=2 * step_flops, moved=2**20
+    new, current = lax.optimization_barrier((new, current))
+    new_y = across(new, 0, 0, 1)
+    new_l = swap_cores(new)
+    others, mine = run(
+        functools.partial(last_kernel, 3), [VMEM], [update, update], flops=3 * step_flops, moved=2**20
     )(current)
     up_d = across(others, 0, 1, 1)
     up_x = across(mine, 0, 1, 0)
     up_y = across(others, 0, 0, 1)
     up_l = swap_cores(mine)
-    (back,) = run(back_kernel, [SMEM, VMEM, VMEM], [moment], moved=2**19)(owner_slot, new_x, new_y)
+    back, hold = run(back_kernel, [VMEM] * 5, [moment, moment], moved=2**19)(
+        plan, mom, new_l, new_x, new_y
+    )
     back_in = swap_cores(back)
-    new_in = jnp.where(lax.axis_index("dp") % 2 == 0, back_in, new_l)
-    (new_momentum,) = run(
-        momentum_kernel,
-        [SMEM] + [VMEM] * 4,
-        [jax.ShapeDtypeStruct(momentum.shape, bf16)],
-        moved=2**19,
-    )(owner_slot, momentum, new, back, new_in)
     over_d, over_x, over_y = swap_cores(up_d), swap_cores(up_x), swap_cores(up_y)
-    (updates,) = run(
-        gather_kernel,
-        [SMEM] + [VMEM] * 8,
-        [jax.ShapeDtypeStruct((mats, half, width), bf16)],
-        out_specs=[ANY],
-        scratch=[pltpu.SemaphoreType.DMA((4,))],
+    updates, new_momentum = run(
+        finish_kernel,
+        [VMEM] * 12,
+        [jax.ShapeDtypeStruct((mats, half, width), bf16), jax.ShapeDtypeStruct(momentum.shape, bf16)],
+        out_specs=[ANY, ANY],
+        scratch=[pltpu.SemaphoreType.DMA((5,))],
         moved=2**20,
-    )(owner_slot, mine, up_l, up_x, up_y, up_d, over_x, over_y, over_d)
+    )(plan, mine, up_l, up_x, up_y, up_d, over_x, over_y, over_d, new, back_in, hold)
     return (updates, new_momentum)
 
 

time: 42.4 us -> 34 us (0.80)
  local copies, waits for them, and re-layouts: 2.84 us -> 0 us
  waiting for transfers between devices: 15.1 us -> 12.7 us
  Pallas kernels: 11.1 us -> 8.73 us
  starting transfers between devices: 12.3 us -> 11.7 us
    ppermute x8, waiting for transfers between devices: 5.66 us -> 2.79 us  [swap_cores(): return lax.ppermute(value, AXES, pairs)]
    unnamed x10 -> x0, local copies, waits for them, and re-layouts: 2.84 us -> none
    pallas_call x6 -> x7, Pallas kernels: 8.72 us -> 6.4 us  [the longest x1 3.39 us: per_device_chips(): run(functools.partial(last_kernel, 3), [VMEM], [update, update], flops=3...]
    ppermute x2 -> x0, starting transfers between devices: 1.34 us -> none  [between_ones(): return lax.ppermute(value, AXES, pairs)]
    ppermute x8, starting transfers between devices: 4.08 us -> 4.67 us  [swap_cores(): return lax.ppermute(value, AXES, pairs)]
    ppermute x8 -> x10, waiting for transfers between devices: 9.45 us -> 9.87 us  [across(): return lax.ppermute(value, AXES, pairs)]
    ppermute x8 -> x10, starting transfers between devices: 6.93 us -> 7.03 us  [across(): return lax.ppermute(value, AXES, pairs)]
  transfers between devices with their start and end apart: 18 -> 18, of which waited for: 10 -> 8; matrix products, arithmetic and copies ran while one was open for 0% -> 0% of each run, Pallas kernels for 16% -> 14%
where the time goes in v2:
time: 34 us; the launch traced here: 33.8 us
  waiting for transfers between devices  12.7 us (37%)
  starting transfers between devices  11.7 us (34%)
  Pallas kernels  8.73 us (26%)
  between operations  0.71 us (2%)
    ppermute x10, waiting for transfers between devices, across(): return lax.ppermute(value, AXES, pairs)  9.87 us
    ppermute x10, starting transfers between devices, across(): return lax.ppermute(value, AXES, pairs)  7.03 us
    ppermute x8, starting transfers between devices, swap_cores(): return lax.ppermute(value, AXES, pairs)  4.67 us
    pallas_call x1, Pallas kernels, per_device_chips(): run(functools.partial(last_kernel, 3), [VMEM], [update, update], flops=3...  3.39 us
    ppermute x8, waiting for transfers between devices, swap_cores(): return lax.ppermute(value, AXES, pairs)  2.79 us
    pallas_call x1, Pallas kernels, per_device_chips(): run(functools.partial(middle_kernel, 2), [VMEM], [whole], flops=2 * step_...  2.33 us
    pallas_call x1, Pallas kernels, per_device_chips(): run(load_kernel, [ANY] * 3, [near, moment, table], scratch=[pltpu.SMEM((m...  1.34 us
    pallas_call x1, Pallas kernels, per_device_chips(): run(finish_kernel, [VMEM] * 12, [jax.ShapeDtypeStruct((mats, half, width)...  0.95 us
  transfers between devices with their start and end apart: 18, of which 8 were waited for; matrix products, arithmetic and copies ran while one was open for 0% of the time, Pallas kernels for 14%

profile of v2, /device:TPU:0, one launch (start us, length us, event | category | flops | bytes accessed | tf_op | source)
XLA Modules:
  0.0 33.8 jit_solution(10628705808154808567)
XLA Ops:
  0.6 0.5 %collective-permute-start = (f32[1,4,128,512]{3,2,1,0:T(8,128)}, f32[1,4,128,512]{3,2,1,0:T(8,128)S(1)}, u32[]{:S(2)}, u32[]{:S(2)}) collective-permute-start(f32[1,4,128,512]{3,2,1,0:T(8,128)} %grads.1), channel_id=1, source_target_pairs={{0,8},{8,0},{1,9},{9,1},{16,24},{24,16},{17,25},{25,17},{2,10},{10... | collective-permute-start | bytes 3145736 | tf_op jit(solution)/shard_map/ppermute | solution.py:308
  1.2 1.3 %shard_map.50 = (f32[4,128,512]{2,1,0:T(8,128)S(1)}, bf16[256,512]{1,0:T(8,128)(2,1)S(1)}, s32[8,128]{1,0:T(8,128)S(1)}) custom-call(f32[1,4,128,512]{3,2,1,0:T(8,128)} %grads.1, bf16[1,256,512]{2,1,0:T(8,128)(2,1)} %momentum.1, s32[4]{0:T(128)} %slots.1), custom_call_target="tpu_custom_call" | custom-call | bytes 2097152 | tf_op jit(solution)/shard_map/pallas_call | solution.py:347
  2.6 1.4 %collective-permute-done.4.mom_other = bf16[1,256,512]{2,1,0:T(8,128)(2,1)S(1)} collective-permute-done((bf16[1,256,512]{2,1,0:T(8,128)(2,1)}, bf16[1,256,512]{2,1,0:T(8,128)(2,1)S(1)}, u32[]{:S(2)}, u32[]{:S(2)}) %collective-permute-start.4) | collective-permute-done | bytes 262176 | tf_op jit(solution)/shard_map/ppermute | solution.py:308
  4.0 0.5 %collective-permute-start.6 = (bf16[256,512]{1,0:T(8,128)(2,1)S(1)}, bf16[256,512]{1,0:T(8,128)(2,1)S(1)}, u32[]{:S(2)}, u32[]{:S(2)}) collective-permute-start(bf16[256,512]{1,0:T(8,128)(2,1)S(1)} %shard_map.52), channel_id=1, source_target_pairs={{8,1},{9,0},{24,17},{25,16},{0,8},{1,9},{16,24},{17,25},{10,3},{11... | collective-permute-start | bytes 786440 | tf_op jit(solution)/shard_map/ppermute | solution.py:317
  4.5 2.5 %collective-permute-start.5 = (bf16[256,512]{1,0:T(8,128)(2,1)S(1)}, bf16[256,512]{1,0:T(8,128)(2,1)S(1)}, u32[]{:S(2)}, u32[]{:S(2)}) collective-permute-start(bf16[256,512]{1,0:T(8,128)(2,1)S(1)} %shard_map.52), channel_id=1, source_target_pairs={{8,16},{9,17},{24,0},{25,1},{0,8},{1,9},{16,24},{17,25},{10,18},{1... | collective-permute-start | bytes 786440 | tf_op jit(solution)/shard_map/ppermute | solution.py:317
  7.0 0.4 %collective-permute-start.1 = (f32[128,512]{1,0:T(8,128)S(1)}, f32[128,512]{1,0:T(8,128)S(1)}, u32[]{:S(2)}, u32[]{:S(2)}) collective-permute-start(f32[128,512]{1,0:T(8,128)S(1)} %get-tuple-element.18), channel_id=1, source_target_pairs={{8,16},{9,17},{24,0},{25,1},{0,8},{1,9},{16,24},{17,25},{10,18},{1... | collective-permute-start | bytes 786440 | tf_op jit(solution)/shard_map/ppermute | solution.py:317
  7.4 1.2 %collective-permute-start.2 = (f32[128,512]{1,0:T(8,128)S(1)}, f32[128,512]{1,0:T(8,128)S(1)}, u32[]{:S(2)}, u32[]{:S(2)}) collective-permute-start(f32[128,512]{1,0:T(8,128)S(1)} %get-tuple-element.19), channel_id=1, source_target_pairs={{8,1},{9,0},{24,17},{25,16},{0,8},{1,9},{16,24},{17,25},{10,3},{11... | collective-permute-start | bytes 786440 | tf_op jit(solution)/shard_map/ppermute | solution.py:317
  8.6 0.4 %collective-permute-start.3 = (f32[128,512]{1,0:T(8,128)S(1)}, f32[128,512]{1,0:T(8,128)S(1)}, u32[]{:S(2)}, u32[]{:S(2)}) collective-permute-start(f32[128,512]{1,0:T(8,128)S(1)} %get-tuple-element.20), channel_id=1, source_target_pairs={{8,17},{9,16},{24,1},{25,0},{0,8},{1,9},{16,24},{17,25},{10,19},{1... | collective-permute-start | bytes 786440 | tf_op jit(solution)/shard_map/ppermute | solution.py:317
  9.1 1.8 %collective-permute-done.6.mom_y = bf16[256,512]{1,0:T(8,128)(2,1)S(1)} collective-permute-done((bf16[256,512]{1,0:T(8,128)(2,1)S(1)}, bf16[256,512]{1,0:T(8,128)(2,1)S(1)}, u32[]{:S(2)}, u32[]{:S(2)}) %collective-permute-start.6) | collective-permute-done | bytes 262176 | tf_op jit(solution)/shard_map/ppermute | solution.py:317
  10.8 1.3 %collective-permute-done.5.mom_x = bf16[256,512]{1,0:T(8,128)(2,1)S(1)} collective-permute-done((bf16[256,512]{1,0:T(8,128)(2,1)S(1)}, bf16[256,512]{1,0:T(8,128)(2,1)S(1)}, u32[]{:S(2)}, u32[]{:S(2)}) %collective-permute-start.5) | collective-permute-done | bytes 262176 | tf_op jit(solution)/shard_map/ppermute | solution.py:317
  12.2 2.8 %collective-permute-done.1.in_x = f32[128,512]{1,0:T(8,128)S(1)} collective-permute-done((f32[128,512]{1,0:T(8,128)S(1)}, f32[128,512]{1,0:T(8,128)S(1)}, u32[]{:S(2)}, u32[]{:S(2)}) %collective-permute-start.1) | collective-permute-done | bytes 262176 | tf_op jit(solution)/shard_map/ppermute | solution.py:317
  15.0 3.0 %collective-permute-done.3.in_d = f32[128,512]{1,0:T(8,128)S(1)} collective-permute-done((f32[128,512]{1,0:T(8,128)S(1)}, f32[128,512]{1,0:T(8,128)S(1)}, u32[]{:S(2)}, u32[]{:S(2)}) %collective-permute-start.3) | collective-permute-done | bytes 262176 | tf_op jit(solution)/shard_map/ppermute | solution.py:317
  18.0 0.6 %shard_map.53 = (bf16[256,512]{1,0:T(8,128)(2,1)S(1)}, f32[256,512]{1,0:T(8,128)S(1)}) custom-call(s32[8,128]{1,0:T(8,128)S(1)} %get-tuple-element.16.plan, f32[4,128,512]{2,1,0:T(8,128)S(1)} %get-tuple-element.17.own, f32[1,4,128,512]{3,2,1,0:T(8,128)S(1)} %collective-permute-done.other, f32[128,512]{1,0:T(8,128)S(1)} %collective-permute-done.1.in_x, ...), custom_call_target="tpu_custom_call" | custom-call | bytes 1048576 | tf_op jit(solution)/shard_map/pallas_call | solution.py:363
  18.6 2.3 %shard_map.54.before = f32[256,512]{1,0:T(8,128)S(1)} custom-call(f32[256,512]{1,0:T(8,128)S(1)} %get-tuple-element.23.before), custom_call_target="tpu_custom_call" | custom-call | flops 2013265920 | bytes 1048576 | tf_op jit(solution)/shard_map/pallas_call | solution.py:367
  21.0 0.5 %collective-permute-start.14 = (bf16[256,512]{1,0:T(8,128)(2,1)S(1)}, bf16[256,512]{1,0:T(8,128)(2,1)S(1)}, u32[]{:S(2)}, u32[]{:S(2)}) collective-permute-start(bf16[256,512]{1,0:T(8,128)(2,1)S(1)} %get-tuple-element.27.new), channel_id=1, source_target_pairs={{0,8},{8,0},{1,9},{9,1},{16,24},{24,16},{17,25},{25,17},{2,10},{10... | collective-permute-start | bytes 786440 | tf_op jit(solution)/shard_map/ppermute | solution.py:308
  21.5 1.2 %collective-permute-start.15 = (bf16[256,512]{1,0:T(8,128)(2,1)S(1)}, bf16[256,512]{1,0:T(8,128)(2,1)S(1)}, u32[]{:S(2)}, u32[]{:S(2)}) collective-permute-start(bf16[256,512]{1,0:T(8,128)(2,1)S(1)} %get-tuple-element.27.new), channel_id=1, source_target_pairs={{0,24},{1,25},{16,8},{17,9},{8,0},{9,1},{24,16},{25,17},{2,26},{3,... | collective-permute-start | bytes 786440 | tf_op jit(solution)/shard_map/ppermute | solution.py:317
  22.7 3.4 %shard_map.55 = (bf16[128,512]{1,0:T(8,128)(2,1)S(1)}, bf16[128,512]{1,0:T(8,128)(2,1)S(1)}) custom-call(f32[256,512]{1,0:T(8,128)S(1)} %shard_map.54.before), custom_call_target="tpu_custom_call" | custom-call | flops 3019898880 | bytes 1048576 | tf_op jit(solution)/shard_map/pallas_call | solution.py:373
  26.1 0.6 %collective-permute-start.9 = (bf16[128,512]{1,0:T(8,128)(2,1)S(1)}, bf16[128,512]{1,0:T(8,128)(2,1)S(1)}, u32[]{:S(2)}, u32[]{:S(2)}) collective-permute-start(bf16[128,512]{1,0:T(8,128)(2,1)S(1)} %get-tuple-element.26), channel_id=1, source_target_pairs={{0,9},{1,8},{16,25},{17,24},{8,0},{9,1},{24,16},{25,17},{2,11},{3,... | collective-permute-start | bytes 393224 | tf_op jit(solution)/shard_map/ppermute | solution.py:317
  27.0 0.6 %collective-permute-start.17 = (bf16[256,512]{1,0:T(8,128)(2,1)S(1)}, bf16[256,512]{1,0:T(8,128)(2,1)S(1)}, u32[]{:S(2)}, u32[]{:S(2)}) collective-permute-start(bf16[256,512]{1,0:T(8,128)(2,1)S(1)} %get-tuple-element.28), channel_id=1, source_target_pairs={{0,8},{8,0},{1,9},{9,1},{16,24},{24,16},{17,25},{25,17},{2,10},{10... | collective-permute-start | bytes 786440 | tf_op jit(solution)/shard_map/ppermute | solution.py:308
  27.7 0.9 %collective-permute-done.10.up_d = bf16[128,512]{1,0:T(8,128)(2,1)S(1)} collective-permute-done((bf16[128,512]{1,0:T(8,128)(2,1)S(1)}, bf16[128,512]{1,0:T(8,128)(2,1)S(1)}, u32[]{:S(2)}, u32[]{:S(2)}) %collective-permute-start.10) | collective-permute-done | bytes 131104 | tf_op jit(solution)/shard_map/ppermute | solution.py:317
  28.6 1.5 %collective-permute-start.13 = (bf16[128,512]{1,0:T(8,128)(2,1)S(1)}, bf16[128,512]{1,0:T(8,128)(2,1)S(1)}, u32[]{:S(2)}, u32[]{:S(2)}) collective-permute-start(bf16[128,512]{1,0:T(8,128)(2,1)S(1)} %collective-permute-done.10.up_d), channel_id=1, source_target_pairs={{0,8},{8,0},{1,9},{9,1},{16,24},{24,16},{17,25},{25,17},{2,10},{10... | collective-permute-start | bytes 393224 | tf_op jit(solution)/shard_map/ppermute | solution.py:308
  30.1 1.4 %collective-permute-start.12 = (bf16[128,512]{1,0:T(8,128)(2,1)S(1)}, bf16[128,512]{1,0:T(8,128)(2,1)S(1)}, u32[]{:S(2)}, u32[]{:S(2)}) collective-permute-start(bf16[128,512]{1,0:T(8,128)(2,1)S(1)} %collective-permute-done.9.up_y), channel_id=1, source_target_pairs={{0,8},{8,0},{1,9},{9,1},{16,24},{24,16},{17,25},{25,17},{2,10},{10... | collective-permute-start | bytes 393224 | tf_op jit(solution)/shard_map/ppermute | solution.py:308
  31.5 1.0 %collective-permute-done.12.in_y = bf16[128,512]{1,0:T(8,128)(2,1)S(1)} collective-permute-done((bf16[128,512]{1,0:T(8,128)(2,1)S(1)}, bf16[128,512]{1,0:T(8,128)(2,1)S(1)}, u32[]{:S(2)}, u32[]{:S(2)}) %collective-permute-start.12) | collective-permute-done | bytes 131104 | tf_op jit(solution)/shard_map/ppermute | solution.py:308
  32.8 1.0 %shard_map.57 = (bf16[4,128,512]{2,1,0:T(8,128)(2,1)}, bf16[1,256,512]{2,1,0:T(8,128)(2,1)}) custom-call(s32[8,128]{1,0:T(8,128)S(1)} %get-tuple-element.16.plan, bf16[128,512]{1,0:T(8,128)(2,1)S(1)} %get-tuple-element.25.mine, bf16[128,512]{1,0:T(8,128)(2,1)S(1)} %collective-permute-done.7.up_l, bf16[128,512]{1,0:T(8,128)(2,1)S(1)} %collective-permute-done.8.up_x, ...), custom_call_target="tpu_custom_call" | custom-call | bytes 1048576 | tf_op jit(solution)/shard_map/pallas_call | solution.py:385
  (20 shorter events, 0.9 us)
Async XLA Ops:
  0.6 6.4 %collective-permute-start = (f32[1,4,128,512]{3,2,1,0:T(8,128)}, f32[1,4,128,512]{3,2,1,0:T(8,128)S(1)}, u32[]{:S(2)}, u32[]{:S(2)}) collective-permute-start(f32[1,4,128,512]{3,2,1,0:T(8,128)} %grads.1), channel_id=1, source_target_pairs={{0,8},{8,0},{1,9},{9,1},{16,24},{24,16},{17,25},{25,17},{2,10},{10... | collective-permute-start | bytes 3145736 | tf_op jit(solution)/shard_map/ppermute | solution.py:308
  1.1 2.9 %collective-permute-start.4 = (bf16[1,256,512]{2,1,0:T(8,128)(2,1)}, bf16[1,256,512]{2,1,0:T(8,128)(2,1)S(1)}, u32[]{:S(2)}, u32[]{:S(2)}) collective-permute-start(bf16[1,256,512]{2,1,0:T(8,128)(2,1)} %momentum.1), channel_id=1, source_target_pairs={{0,8},{8,0},{1,9},{9,1},{16,24},{24,16},{17,25},{25,17},{2,10},{10... | collective-permute-start | bytes 786440 | tf_op jit(solution)/shard_map/ppermute | solution.py:308
  4.0 6.8 %collective-permute-start.6 = (bf16[256,512]{1,0:T(8,128)(2,1)S(1)}, bf16[256,512]{1,0:T(8,128)(2,1)S(1)}, u32[]{:S(2)}, u32[]{:S(2)}) collective-permute-start(bf16[256,512]{1,0:T(8,128)(2,1)S(1)} %shard_map.52), channel_id=1, source_target_pairs={{8,1},{9,0},{24,17},{25,16},{0,8},{1,9},{16,24},{17,25},{10,3},{11... | collective-permute-start | bytes 786440 | tf_op jit(solution)/shard_map/ppermute | solution.py:317
  4.5 7.7 %collective-permute-start.5 = (bf16[256,512]{1,0:T(8,128)(2,1)S(1)}, bf16[256,512]{1,0:T(8,128)(2,1)S(1)}, u32[]{:S(2)}, u32[]{:S(2)}) collective-permute-start(bf16[256,512]{1,0:T(8,128)(2,1)S(1)} %shard_map.52), channel_id=1, source_target_pairs={{8,16},{9,17},{24,0},{25,1},{0,8},{1,9},{16,24},{17,25},{10,18},{1... | collective-permute-start | bytes 786440 | tf_op jit(solution)/shard_map/ppermute | solution.py:317
  7.0 8.0 %collective-permute-start.1 = (f32[128,512]{1,0:T(8,128)S(1)}, f32[128,512]{1,0:T(8,128)S(1)}, u32[]{:S(2)}, u32[]{:S(2)}) collective-permute-start(f32[128,512]{1,0:T(8,128)S(1)} %get-tuple-element.18), channel_id=1, source_target_pairs={{8,16},{9,17},{24,0},{25,1},{0,8},{1,9},{16,24},{17,25},{10,18},{1... | collective-permute-start | bytes 786440 | tf_op jit(solution)/shard_map/ppermute | solution.py:317
  7.4 7.6 %collective-permute-start.2 = (f32[128,512]{1,0:T(8,128)S(1)}, f32[128,512]{1,0:T(8,128)S(1)}, u32[]{:S(2)}, u32[]{:S(2)}) collective-permute-start(f32[128,512]{1,0:T(8,128)S(1)} %get-tuple-element.19), channel_id=1, source_target_pairs={{8,1},{9,0},{24,17},{25,16},{0,8},{1,9},{16,24},{17,25},{10,3},{11... | collective-permute-start | bytes 786440 | tf_op jit(solution)/shard_map/ppermute | solution.py:317
  8.6 9.4 %collective-permute-start.3 = (f32[128,512]{1,0:T(8,128)S(1)}, f32[128,512]{1,0:T(8,128)S(1)}, u32[]{:S(2)}, u32[]{:S(2)}) collective-permute-start(f32[128,512]{1,0:T(8,128)S(1)} %get-tuple-element.20), channel_id=1, source_target_pairs={{8,17},{9,16},{24,1},{25,0},{0,8},{1,9},{16,24},{17,25},{10,19},{1... | collective-permute-start | bytes 786440 | tf_op jit(solution)/shard_map/ppermute | solution.py:317
  20.9 5.8 %collective-permute-start.16 = (bf16[256,512]{1,0:T(8,128)(2,1)S(1)}, bf16[256,512]{1,0:T(8,128)(2,1)S(1)}, u32[]{:S(2)}, u32[]{:S(2)}) collective-permute-start(bf16[256,512]{1,0:T(8,128)(2,1)S(1)} %get-tuple-element.27.new), channel_id=1, source_target_pairs={{0,9},{1,8},{16,25},{17,24},{8,0},{9,1},{24,16},{25,17},{2,11},{3,... | collective-permute-start | bytes 786440 | tf_op jit(solution)/shard_map/ppermute | solution.py:317
  21.0 5.8 %collective-permute-start.14 = (bf16[256,512]{1,0:T(8,128)(2,1)S(1)}, bf16[256,512]{1,0:T(8,128)(2,1)S(1)}, u32[]{:S(2)}, u32[]{:S(2)}) collective-permute-start(bf16[256,512]{1,0:T(8,128)(2,1)S(1)} %get-tuple-element.27.new), channel_id=1, source_target_pairs={{0,8},{8,0},{1,9},{9,1},{16,24},{24,16},{17,25},{25,17},{2,10},{10... | collective-permute-start | bytes 786440 | tf_op jit(solution)/shard_map/ppermute | solution.py:308
  21.5 5.4 %collective-permute-start.15 = (bf16[256,512]{1,0:T(8,128)(2,1)S(1)}, bf16[256,512]{1,0:T(8,128)(2,1)S(1)}, u32[]{:S(2)}, u32[]{:S(2)}) collective-permute-start(bf16[256,512]{1,0:T(8,128)(2,1)S(1)} %get-tuple-element.27.new), channel_id=1, source_target_pairs={{0,24},{1,25},{16,8},{17,9},{8,0},{9,1},{24,16},{25,17},{2,26},{3,... | collective-permute-start | bytes 786440 | tf_op jit(solution)/shard_map/ppermute | solution.py:317
  26.1 2.6 %collective-permute-start.10 = (bf16[128,512]{1,0:T(8,128)(2,1)S(1)}, bf16[128,512]{1,0:T(8,128)(2,1)S(1)}, u32[]{:S(2)}, u32[]{:S(2)}) collective-permute-start(bf16[128,512]{1,0:T(8,128)(2,1)S(1)} %get-tuple-element.26), channel_id=1, source_target_pairs={{0,25},{1,24},{16,9},{17,8},{8,0},{9,1},{24,16},{25,17},{2,27},{3,... | collective-permute-start | bytes 393224 | tf_op jit(solution)/shard_map/ppermute | solution.py:317
  26.1 4.0 %collective-permute-start.9 = (bf16[128,512]{1,0:T(8,128)(2,1)S(1)}, bf16[128,512]{1,0:T(8,128)(2,1)S(1)}, u32[]{:S(2)}, u32[]{:S(2)}) collective-permute-start(bf16[128,512]{1,0:T(8,128)(2,1)S(1)} %get-tuple-element.26), channel_id=1, source_target_pairs={{0,9},{1,8},{16,25},{17,24},{8,0},{9,1},{24,16},{25,17},{2,11},{3,... | collective-permute-start | bytes 393224 | tf_op jit(solution)/shard_map/ppermute | solution.py:317
  26.7 4.8 %collective-permute-start.8 = (bf16[128,512]{1,0:T(8,128)(2,1)S(1)}, bf16[128,512]{1,0:T(8,128)(2,1)S(1)}, u32[]{:S(2)}, u32[]{:S(2)}) collective-permute-start(bf16[128,512]{1,0:T(8,128)(2,1)S(1)} %get-tuple-element.25.mine), channel_id=1, source_target_pairs={{0,24},{1,25},{16,8},{17,9},{8,0},{9,1},{24,16},{25,17},{2,26},{3,... | collective-permute-start | bytes 393224 | tf_op jit(solution)/shard_map/ppermute | solution.py:317
  27.0 5.8 %collective-permute-start.17 = (bf16[256,512]{1,0:T(8,128)(2,1)S(1)}, bf16[256,512]{1,0:T(8,128)(2,1)S(1)}, u32[]{:S(2)}, u32[]{:S(2)}) collective-permute-start(bf16[256,512]{1,0:T(8,128)(2,1)S(1)} %get-tuple-element.28), channel_id=1, source_target_pairs={{0,8},{8,0},{1,9},{9,1},{16,24},{24,16},{17,25},{25,17},{2,10},{10... | collective-permute-start | bytes 786440 | tf_op jit(solution)/shard_map/ppermute | solution.py:308
  27.6 3.9 %collective-permute-start.7 = (bf16[128,512]{1,0:T(8,128)(2,1)S(1)}, bf16[128,512]{1,0:T(8,128)(2,1)S(1)}, u32[]{:S(2)}, u32[]{:S(2)}) collective-permute-start(bf16[128,512]{1,0:T(8,128)(2,1)S(1)} %get-tuple-element.25.mine), channel_id=1, source_target_pairs={{0,8},{8,0},{1,9},{9,1},{16,24},{24,16},{17,25},{25,17},{2,10},{10... | collective-permute-start | bytes 393224 | tf_op jit(solution)/shard_map/ppermute | solution.py:308
  28.6 2.9 %collective-permute-start.13 = (bf16[128,512]{1,0:T(8,128)(2,1)S(1)}, bf16[128,512]{1,0:T(8,128)(2,1)S(1)}, u32[]{:S(2)}, u32[]{:S(2)}) collective-permute-start(bf16[128,512]{1,0:T(8,128)(2,1)S(1)} %collective-permute-done.10.up_d), channel_id=1, source_target_pairs={{0,8},{8,0},{1,9},{9,1},{16,24},{24,16},{17,25},{25,17},{2,10},{10... | collective-permute-start | bytes 393224 | tf_op jit(solution)/shard_map/ppermute | solution.py:308
  30.1 2.3 %collective-permute-start.12 = (bf16[128,512]{1,0:T(8,128)(2,1)S(1)}, bf16[128,512]{1,0:T(8,128)(2,1)S(1)}, u32[]{:S(2)}, u32[]{:S(2)}) collective-permute-start(bf16[128,512]{1,0:T(8,128)(2,1)S(1)} %collective-permute-done.9.up_y), channel_id=1, source_target_pairs={{0,8},{8,0},{1,9},{9,1},{16,24},{24,16},{17,25},{25,17},{2,10},{10... | collective-permute-start | bytes 393224 | tf_op jit(solution)/shard_map/ppermute | solution.py:308
  31.5 1.3 %collective-permute-start.11 = (bf16[128,512]{1,0:T(8,128)(2,1)S(1)}, bf16[128,512]{1,0:T(8,128)(2,1)S(1)}, u32[]{:S(2)}, u32[]{:S(2)}) collective-permute-start(bf16[128,512]{1,0:T(8,128)(2,1)S(1)} %collective-permute-done.8.up_x), channel_id=1, source_target_pairs={{0,8},{8,0},{1,9},{9,1},{16,24},{24,16},{17,25},{25,17},{2,10},{10... | collective-permute-start | bytes 393224 | tf_op jit(solution)/shard_map/ppermute | solution.py:308

commit v3 on v2

--- a/solution.py
+++ b/solution.py
@@ -189,18 +189,35 @@
             out[...] = own[m] + other[0, m]
 
 
+def parts_of(value):
+    high = value.astype(jnp.bfloat16)
+    return high, (value - high.astype(jnp.float32)).astype(jnp.bfloat16)
+
+
 def polynomial_step(current):
-    contract = functools.partial(
-        lax.dot_general, precision=lax.Precision.HIGH, preferred_element_type=jnp.float32
-    )
-    gram = contract(current, current, (((1,), (1,)), ((), ())))
-    square = contract(gram, gram, (((1,), (0,)), ((), ())))
-    poly = COEF_B * gram + COEF_C * square
-    return COEF_A * current + contract(poly, current, (((1,), (0,)), ((), ())))
+    dot = functools.partial(lax.dot_general, preferred_element_type=jnp.float32)
+    plain, turned = (((1,), (0,)), ((), ())), (((1,), (1,)), ((), ()))
+    high, low = parts_of(current)
+    mixed = dot(high, low, turned)
+    gram = dot(high, high, turned) + (mixed + mixed.T)
+    gram_high, gram_low = parts_of(gram)
+    rows = current.shape[0] // 2
+    blocks = []
+    for k in (0, 1):
+        block = slice(k * rows, (k + 1) * rows)
+        square = dot(gram_high[block], gram_high, plain) + (
+            dot(gram_high[block], gram_low, plain) + dot(gram_low[block], gram_high, plain)
+        )
+        poly_high, poly_low = parts_of(COEF_B * gram[block] + COEF_C * square)
+        change = dot(poly_high, high, plain) + (
+            dot(poly_high, low, plain) + dot(poly_low, high, plain)
+        )
+        blocks.append(COEF_A * current[block] + change)
+    return jnp.concatenate(blocks, axis=0)
 
 
 def nesterov_kernel(
-    plan, own, other, in_x, in_y, in_d, mom, mom_other, mom_x, mom_y, new, current
+    plan, mom_other, mom_x, mom_y, other, in_d, in_x, in_y, own, mom, new, current
 ):
     _, c, y = here()
     half = own.shape[1]
@@ -228,32 +245,21 @@
             current[part * half : (part + 1) * half] = pieces[part] / norm
 
 
-def middle_kernel(steps, before, after):
+def orthogonalize_kernel(start, others, mine):
     _, c, _ = here()
+    half = mine.shape[0]
 
     @pl.when(c == 0)
     def _():
-        value = before[...]
-        for _ in range(steps):
-            value = polynomial_step(value)
-        after[...] = value
-
-
-def last_kernel(steps, before, others, mine):
-    _, c, _ = here()
-    half = mine.shape[0]
-
-    @pl.when(c == 0)
-    def _():
-        value = before[...]
-        for _ in range(steps):
+        value = start[...]
+        for _ in range(ITERS):
             value = polynomial_step(value)
         value = (FACTOR * value).astype(jnp.bfloat16)
         mine[...] = value[:half]
         others[...] = value[half:]
 
 
-def back_kernel(plan, mom, new_l, new_x, new_y, back, hold):
+def back_kernel(plan, mom, new_x, new_y, new_l, back, hold):
     _, c, _ = here()
 
     @pl.when(c == 1)
@@ -266,7 +272,7 @@
 
 
 def finish_kernel(
-    plan, mine, up_l, up_x, up_y, up_d, in_x, in_y, in_d, new, back, hold, updates, moment, sems
+    plan, new, back, hold, up_x, up_y, up_d, up_l, in_x, in_y, in_d, mine, updates, moment, sems
 ):
     _, c, _ = here()
     for core, sources in ((0, (mine, in_y, in_x, in_d)), (1, (up_l, up_y, up_x, up_d))):
@@ -337,20 +343,21 @@
     whole = jax.ShapeDtypeStruct((rows, width), f32)
     moment = jax.ShapeDtypeStruct((rows, width), bf16)
     update = jax.ShapeDtypeStruct((half, width), bf16)
-    step_flops = 6 * (2 * rows * rows * width * 2 + 2 * rows * rows * rows)
 
     near = jax.ShapeDtypeStruct((mats, half, width), f32)
     table = jax.ShapeDtypeStruct((8, 128), jnp.int32)
 
     mom_other = swap_cores(momentum)
-    grads_other = swap_cores(grads)
+    far = functools.partial(pltpu.with_memory_space_constraint, memory_space=pltpu.HBM)
     own, mom, plan = run(
         load_kernel,
         [ANY] * 3,
         [near, moment, table],
         scratch=[pltpu.SMEM((mats,), jnp.int32), pltpu.SemaphoreType.DMA((3,))],
         moved=2**21,
-    )(*(pltpu.with_memory_space_constraint(a, pltpu.HBM) for a in (grads, momentum, owner_slot)))
+    )(far(grads), far(momentum), far(owner_slot))
+    mom_other, plan, grads = lax.optimization_barrier((mom_other, plan, grads))
+    grads_other = swap_cores(grads)
     (mom_out,) = run(give_kernel, [VMEM] * 3, [moment], moved=2**18)(plan, mom, mom_other)
     mom_x = across(mom_out, 1, 1, 0)
     mom_y = across(mom_out, 1, 0, 1)
@@ -361,27 +368,21 @@
     in_x = across(to_x, 1, 1, 0)
     in_y = across(to_y, 1, 0, 1)
     new, current = run(nesterov_kernel, [VMEM] * 10, [moment, whole], moved=2**20)(
-        plan, own, grads_other, in_x, in_y, in_d, mom, mom_other, mom_x, mom_y
+        plan, mom_other, mom_x, mom_y, grads_other, in_d, in_x, in_y, own, mom
     )
     new_x = across(new, 0, 1, 0)
-    (current,) = run(
-        functools.partial(middle_kernel, 2), [VMEM], [whole], flops=2 * step_flops, moved=2**20
-    )(current)
-    new, current = lax.optimization_barrier((new, current))
     new_y = across(new, 0, 0, 1)
     new_l = swap_cores(new)
-    others, mine = run(
-        functools.partial(last_kernel, 3), [VMEM], [update, update], flops=3 * step_flops, moved=2**20
-    )(current)
-    up_d = across(others, 0, 1, 1)
+    others, mine = run(orthogonalize_kernel, [VMEM], [update, update], moved=2**20)(current)
     up_x = across(mine, 0, 1, 0)
     up_y = across(others, 0, 0, 1)
+    up_d = across(others, 0, 1, 1)
     up_l = swap_cores(mine)
     back, hold = run(back_kernel, [VMEM] * 5, [moment, moment], moved=2**19)(
-        plan, mom, new_l, new_x, new_y
+        plan, mom, new_x, new_y, new_l
     )
     back_in = swap_cores(back)
-    over_d, over_x, over_y = swap_cores(up_d), swap_cores(up_x), swap_cores(up_y)
+    over_x, over_y, over_d = swap_cores(up_x), swap_cores(up_y), swap_cores(up_d)
     updates, new_momentum = run(
         finish_kernel,
         [VMEM] * 12,
@@ -389,7 +390,7 @@
         out_specs=[ANY, ANY],
         scratch=[pltpu.SemaphoreType.DMA((5,))],
         moved=2**20,
-    )(plan, mine, up_l, up_x, up_y, up_d, over_x, over_y, over_d, new, back_in, hold)
+    )(plan, new, back_in, hold, up_x, up_y, up_d, up_l, over_x, over_y, over_d, mine)
     return (updates, new_momentum)
 
 

time: 34 us -> 32 us (0.941)
  waiting for transfers between devices: 12.7 us -> 9.95 us
  starting transfers between devices: 11.7 us -> 13.3 us
  Pallas kernels: 8.73 us -> 7.82 us
    ppermute x10, starting transfers between devices: 7.03 us -> 8.65 us  [across(): return lax.ppermute(value, AXES, pairs)]
    ppermute x8, waiting for transfers between devices: 2.79 us -> 1.37 us  [swap_cores(): return lax.ppermute(value, AXES, pairs)]
    ppermute x10, waiting for transfers between devices: 9.87 us -> 8.58 us  [across(): return lax.ppermute(value, AXES, pairs)]
    pallas_call x2 -> x1, Pallas kernels: 5.72 us -> 4.8 us  [per_device_chips(): run(orthogonalize_kernel, [VMEM], [update, update], moved=2 ** 20)(current)]
  transfers between devices with their start and end apart: 18 -> 18, of which waited for: 8 -> 8; matrix products, arithmetic and copies ran while one was open for 0% -> 0% of each run, Pallas kernels for 14% -> 20%
where the time goes in v3:
time: 32 us; the launch traced here: 31.8 us
  starting transfers between devices  13.3 us (42%)
  waiting for transfers between devices  9.95 us (31%)
  Pallas kernels  7.82 us (24%)
  between operations  0.72 us (2%)
    ppermute x10, starting transfers between devices, across(): return lax.ppermute(value, AXES, pairs)  8.65 us
    ppermute x10, waiting for transfers between devices, across(): return lax.ppermute(value, AXES, pairs)  8.58 us
    pallas_call x1, Pallas kernels, per_device_chips(): run(orthogonalize_kernel, [VMEM], [update, update], moved=2 ** 20)(current)  4.8 us
    ppermute x8, starting transfers between devices, swap_cores(): return lax.ppermute(value, AXES, pairs)  4.69 us
    ppermute x8, waiting for transfers between devices, swap_cores(): return lax.ppermute(value, AXES, pairs)  1.37 us
    pallas_call x1, Pallas kernels, per_device_chips(): run(load_kernel, [ANY] * 3, [near, moment, table], scratch=[pltpu.SMEM((m...  1.34 us
    pallas_call x1, Pallas kernels, per_device_chips(): run(finish_kernel, [VMEM] * 12, [jax.ShapeDtypeStruct((mats, half, width)...  0.95 us
  transfers between devices with their start and end apart: 18, of which 8 were waited for; matrix products, arithmetic and copies ran while one was open for 0% of the time, Pallas kernels for 20%

profile of v3, /device:TPU:0, one launch (start us, length us, event | category | flops | bytes accessed | tf_op | source)
XLA Modules:
  0.0 31.8 jit_solution(73274768906938400)
XLA Ops:
  0.6 0.5 %collective-permute-start = (bf16[1,256,512]{2,1,0:T(8,128)(2,1)}, bf16[1,256,512]{2,1,0:T(8,128)(2,1)S(1)}, u32[]{:S(2)}, u32[]{:S(2)}) collective-permute-start(bf16[1,256,512]{2,1,0:T(8,128)(2,1)} %momentum.1), channel_id=1, source_target_pairs={{0,8},{8,0},{1,9},{9,1},{16,24},{24,16},{17,25},{25,17},{2,10},{10... | collective-permute-start | bytes 786440 | tf_op jit(solution)/shard_map/ppermute | solution.py:314
  1.2 1.3 %shard_map.50 = (f32[4,128,512]{2,1,0:T(8,128)S(1)}, bf16[256,512]{1,0:T(8,128)(2,1)S(1)}, s32[8,128]{1,0:T(8,128)S(1)}) custom-call(f32[1,4,128,512]{3,2,1,0:T(8,128)} %grads.1, bf16[1,256,512]{2,1,0:T(8,128)(2,1)} %momentum.1, s32[4]{0:T(128)} %slots.1), custom_call_target="tpu_custom_call" | custom-call | bytes 2097152 | tf_op jit(solution)/shard_map/pallas_call | solution.py:352
  2.5 0.4 %collective-permute-start.3 = (f32[1,4,128,512]{3,2,1,0:T(8,128)S(1)}, f32[1,4,128,512]{3,2,1,0:T(8,128)S(1)}, u32[]{:S(2)}, u32[]{:S(2)}) collective-permute-start(f32[1,4,128,512]{3,2,1,0:T(8,128)S(1)} %copy-done), channel_id=1, source_target_pairs={{0,8},{8,0},{1,9},{9,1},{16,24},{24,16},{17,25},{25,17},{2,10},{10... | collective-permute-start | bytes 3145736 | tf_op jit(solution)/shard_map/ppermute | solution.py:314
  2.9 0.3 collective-permute-start.2
  3.2 2.5 %collective-permute-start.1 = (bf16[256,512]{1,0:T(8,128)(2,1)S(1)}, bf16[256,512]{1,0:T(8,128)(2,1)S(1)}, u32[]{:S(2)}, u32[]{:S(2)}) collective-permute-start(bf16[256,512]{1,0:T(8,128)(2,1)S(1)} %shard_map.51), channel_id=1, source_target_pairs={{8,16},{9,17},{24,0},{25,1},{0,8},{1,9},{16,24},{17,25},{10,18},{1... | collective-permute-start | bytes 786440 | tf_op jit(solution)/shard_map/ppermute | solution.py:323
  5.7 0.6 %collective-permute-start.4 = (f32[128,512]{1,0:T(8,128)S(1)}, f32[128,512]{1,0:T(8,128)S(1)}, u32[]{:S(2)}, u32[]{:S(2)}) collective-permute-start(f32[128,512]{1,0:T(8,128)S(1)} %get-tuple-element.23), channel_id=1, source_target_pairs={{8,17},{9,16},{24,1},{25,0},{0,8},{1,9},{16,24},{17,25},{10,19},{1... | collective-permute-start | bytes 786440 | tf_op jit(solution)/shard_map/ppermute | solution.py:323
  6.3 2.8 %collective-permute-start.5 = (f32[128,512]{1,0:T(8,128)S(1)}, f32[128,512]{1,0:T(8,128)S(1)}, u32[]{:S(2)}, u32[]{:S(2)}) collective-permute-start(f32[128,512]{1,0:T(8,128)S(1)} %get-tuple-element.24), channel_id=1, source_target_pairs={{8,16},{9,17},{24,0},{25,1},{0,8},{1,9},{16,24},{17,25},{10,18},{1... | collective-permute-start | bytes 786440 | tf_op jit(solution)/shard_map/ppermute | solution.py:323
  9.1 0.6 %collective-permute-done.2.mom_y = bf16[256,512]{1,0:T(8,128)(2,1)S(1)} collective-permute-done((bf16[256,512]{1,0:T(8,128)(2,1)S(1)}, bf16[256,512]{1,0:T(8,128)(2,1)S(1)}, u32[]{:S(2)}, u32[]{:S(2)}) %collective-permute-start.2) | collective-permute-done | bytes 262176 | tf_op jit(solution)/shard_map/ppermute | solution.py:323
  9.7 1.2 %collective-permute-done.1.mom_x = bf16[256,512]{1,0:T(8,128)(2,1)S(1)} collective-permute-done((bf16[256,512]{1,0:T(8,128)(2,1)S(1)}, bf16[256,512]{1,0:T(8,128)(2,1)S(1)}, u32[]{:S(2)}, u32[]{:S(2)}) %collective-permute-start.1) | collective-permute-done | bytes 262176 | tf_op jit(solution)/shard_map/ppermute | solution.py:323
  10.9 3.3 %collective-permute-done.4.in_d = f32[128,512]{1,0:T(8,128)S(1)} collective-permute-done((f32[128,512]{1,0:T(8,128)S(1)}, f32[128,512]{1,0:T(8,128)S(1)}, u32[]{:S(2)}, u32[]{:S(2)}) %collective-permute-start.4) | collective-permute-done | bytes 262176 | tf_op jit(solution)/shard_map/ppermute | solution.py:323
  14.2 2.3 %collective-permute-done.5.in_x = f32[128,512]{1,0:T(8,128)S(1)} collective-permute-done((f32[128,512]{1,0:T(8,128)S(1)}, f32[128,512]{1,0:T(8,128)S(1)}, u32[]{:S(2)}, u32[]{:S(2)}) %collective-permute-start.5) | collective-permute-done | bytes 262176 | tf_op jit(solution)/shard_map/ppermute | solution.py:323
  16.5 0.4 %collective-permute-done.6.in_y = f32[128,512]{1,0:T(8,128)S(1)} collective-permute-done((f32[128,512]{1,0:T(8,128)S(1)}, f32[128,512]{1,0:T(8,128)S(1)}, u32[]{:S(2)}, u32[]{:S(2)}) %collective-permute-start.6) | collective-permute-done | bytes 262176 | tf_op jit(solution)/shard_map/ppermute | solution.py:323
  16.9 0.6 %shard_map.53 = (bf16[256,512]{1,0:T(8,128)(2,1)S(1)}, f32[256,512]{1,0:T(8,128)S(1)}) custom-call(s32[8,128]{1,0:T(8,128)S(1)} %get-tuple-element.18.plan, bf16[1,256,512]{2,1,0:T(8,128)(2,1)S(1)} %collective-permute-done.mom_other, bf16[256,512]{1,0:T(8,128)(2,1)S(1)} %collective-permute-done.1.mom_x, bf16[256,512]{1,0:T(8,128)(2,1)S(1)} %collective-permute-done.2.mom_y, ...), custom_call_target="tpu_custom_call" | custom-call | bytes 1048576 | tf_op jit(solution)/shard_map/pallas_call | solution.py:370
  17.6 1.2 %collective-permute-start.8 = (bf16[256,512]{1,0:T(8,128)(2,1)S(1)}, bf16[256,512]{1,0:T(8,128)(2,1)S(1)}, u32[]{:S(2)}, u32[]{:S(2)}) collective-permute-start(bf16[256,512]{1,0:T(8,128)(2,1)S(1)} %get-tuple-element.26.new), channel_id=1, source_target_pairs={{0,9},{1,8},{16,25},{17,24},{8,0},{9,1},{24,16},{25,17},{2,11},{3,... | collective-permute-start | bytes 786440 | tf_op jit(solution)/shard_map/ppermute | solution.py:323
  18.7 0.4 %collective-permute-start.7 = (bf16[256,512]{1,0:T(8,128)(2,1)S(1)}, bf16[256,512]{1,0:T(8,128)(2,1)S(1)}, u32[]{:S(2)}, u32[]{:S(2)}) collective-permute-start(bf16[256,512]{1,0:T(8,128)(2,1)S(1)} %get-tuple-element.26.new), channel_id=1, source_target_pairs={{0,24},{1,25},{16,8},{17,9},{8,0},{9,1},{24,16},{25,17},{2,26},{3,... | collective-permute-start | bytes 786440 | tf_op jit(solution)/shard_map/ppermute | solution.py:323
  19.1 4.8 %shard_map.55 = (bf16[128,512]{1,0:T(8,128)(2,1)S(1)}, bf16[128,512]{1,0:T(8,128)(2,1)S(1)}) custom-call(f32[256,512]{1,0:T(8,128)S(1)} %get-tuple-element.29.start), custom_call_target="tpu_custom_call" | custom-call | bytes 1048576 | tf_op jit(solution)/shard_map/pallas_call | solution.py:376
  24.0 0.8 %collective-permute-start.12 = (bf16[128,512]{1,0:T(8,128)(2,1)S(1)}, bf16[128,512]{1,0:T(8,128)(2,1)S(1)}, u32[]{:S(2)}, u32[]{:S(2)}) collective-permute-start(bf16[128,512]{1,0:T(8,128)(2,1)S(1)} %get-tuple-element.31), channel_id=1, source_target_pairs={{0,9},{1,8},{16,25},{17,24},{8,0},{9,1},{24,16},{25,17},{2,11},{3,... | collective-permute-start | bytes 393224 | tf_op jit(solution)/shard_map/ppermute | solution.py:323
  25.0 0.6 %collective-permute-start.10 = (bf16[256,512]{1,0:T(8,128)(2,1)S(1)}, bf16[256,512]{1,0:T(8,128)(2,1)S(1)}, u32[]{:S(2)}, u32[]{:S(2)}) collective-permute-start(bf16[256,512]{1,0:T(8,128)(2,1)S(1)} %get-tuple-element.27), channel_id=1, source_target_pairs={{0,8},{8,0},{1,9},{9,1},{16,24},{24,16},{17,25},{25,17},{2,10},{10... | collective-permute-start | bytes 786440 | tf_op jit(solution)/shard_map/ppermute | solution.py:314
  25.7 0.8 %collective-permute-done.13.up_d = bf16[128,512]{1,0:T(8,128)(2,1)S(1)} collective-permute-done((bf16[128,512]{1,0:T(8,128)(2,1)S(1)}, bf16[128,512]{1,0:T(8,128)(2,1)S(1)}, u32[]{:S(2)}, u32[]{:S(2)}) %collective-permute-start.13) | collective-permute-done | bytes 131104 | tf_op jit(solution)/shard_map/ppermute | solution.py:323
  26.5 1.7 %collective-permute-start.17 = (bf16[128,512]{1,0:T(8,128)(2,1)S(1)}, bf16[128,512]{1,0:T(8,128)(2,1)S(1)}, u32[]{:S(2)}, u32[]{:S(2)}) collective-permute-start(bf16[128,512]{1,0:T(8,128)(2,1)S(1)} %collective-permute-done.13.up_d), channel_id=1, source_target_pairs={{0,8},{8,0},{1,9},{9,1},{16,24},{24,16},{17,25},{25,17},{2,10},{10... | collective-permute-start | bytes 393224 | tf_op jit(solution)/shard_map/ppermute | solution.py:314
  28.2 1.3 %collective-permute-start.16 = (bf16[128,512]{1,0:T(8,128)(2,1)S(1)}, bf16[128,512]{1,0:T(8,128)(2,1)S(1)}, u32[]{:S(2)}, u32[]{:S(2)}) collective-permute-start(bf16[128,512]{1,0:T(8,128)(2,1)S(1)} %collective-permute-done.12.up_y), channel_id=1, source_target_pairs={{0,8},{8,0},{1,9},{9,1},{16,24},{24,16},{17,25},{25,17},{2,10},{10... | collective-permute-start | bytes 393224 | tf_op jit(solution)/shard_map/ppermute | solution.py:314
  29.5 1.0 %collective-permute-done.16.in_y = bf16[128,512]{1,0:T(8,128)(2,1)S(1)} collective-permute-done((bf16[128,512]{1,0:T(8,128)(2,1)S(1)}, bf16[128,512]{1,0:T(8,128)(2,1)S(1)}, u32[]{:S(2)}, u32[]{:S(2)}) %collective-permute-start.16) | collective-permute-done | bytes 131104 | tf_op jit(solution)/shard_map/ppermute | solution.py:314
  30.5 0.4 %collective-permute-done.15.in_x = bf16[128,512]{1,0:T(8,128)(2,1)S(1)} collective-permute-done((bf16[128,512]{1,0:T(8,128)(2,1)S(1)}, bf16[128,512]{1,0:T(8,128)(2,1)S(1)}, u32[]{:S(2)}, u32[]{:S(2)}) %collective-permute-start.15) | collective-permute-done | bytes 131104 | tf_op jit(solution)/shard_map/ppermute | solution.py:314
  30.9 1.0 %shard_map.56 = (bf16[4,128,512]{2,1,0:T(8,128)(2,1)}, bf16[1,256,512]{2,1,0:T(8,128)(2,1)}) custom-call(s32[8,128]{1,0:T(8,128)S(1)} %get-tuple-element.18.plan, bf16[256,512]{1,0:T(8,128)(2,1)S(1)} %get-tuple-element.26.new, bf16[256,512]{1,0:T(8,128)(2,1)S(1)} %collective-permute-done.10.back, bf16[256,512]{1,0:T(8,128)(2,1)S(1)} %get-tuple-element.28.hold, ...), custom_call_target="tpu_custom_call" | custom-call | bytes 1048576 | tf_op jit(solution)/shard_map/pallas_call | solution.py:386
  (21 shorter events, 0.4 us)
Async XLA Ops:
  0.6 1.9 %copy-start = (f32[1,4,128,512]{3,2,1,0:T(8,128)S(1)}, f32[1,4,128,512]{3,2,1,0:T(8,128)}, u32[]{:S(2)}) copy-start(f32[1,4,128,512]{3,2,1,0:T(8,128)} %grads.1) | copy-start | bytes 3145732
  0.6 1.9 %collective-permute-start = (bf16[1,256,512]{2,1,0:T(8,128)(2,1)}, bf16[1,256,512]{2,1,0:T(8,128)(2,1)S(1)}, u32[]{:S(2)}, u32[]{:S(2)}) collective-permute-start(bf16[1,256,512]{2,1,0:T(8,128)(2,1)} %momentum.1), channel_id=1, source_target_pairs={{0,8},{8,0},{1,9},{9,1},{16,24},{24,16},{17,25},{25,17},{2,10},{10... | collective-permute-start | bytes 786440 | tf_op jit(solution)/shard_map/ppermute | solution.py:314
  2.5 3.2 %collective-permute-start.3 = (f32[1,4,128,512]{3,2,1,0:T(8,128)S(1)}, f32[1,4,128,512]{3,2,1,0:T(8,128)S(1)}, u32[]{:S(2)}, u32[]{:S(2)}) collective-permute-start(f32[1,4,128,512]{3,2,1,0:T(8,128)S(1)} %copy-done), channel_id=1, source_target_pairs={{0,8},{8,0},{1,9},{9,1},{16,24},{24,16},{17,25},{25,17},{2,10},{10... | collective-permute-start | bytes 3145736 | tf_op jit(solution)/shard_map/ppermute | solution.py:314
  2.9 6.8 %collective-permute-start.2 = (bf16[256,512]{1,0:T(8,128)(2,1)S(1)}, bf16[256,512]{1,0:T(8,128)(2,1)S(1)}, u32[]{:S(2)}, u32[]{:S(2)}) collective-permute-start(bf16[256,512]{1,0:T(8,128)(2,1)S(1)} %shard_map.51), channel_id=1, source_target_pairs={{8,1},{9,0},{24,17},{25,16},{0,8},{1,9},{16,24},{17,25},{10,3},{11... | collective-permute-start | bytes 786440 | tf_op jit(solution)/shard_map/ppermute | solution.py:323
  3.2 7.7 %collective-permute-start.1 = (bf16[256,512]{1,0:T(8,128)(2,1)S(1)}, bf16[256,512]{1,0:T(8,128)(2,1)S(1)}, u32[]{:S(2)}, u32[]{:S(2)}) collective-permute-start(bf16[256,512]{1,0:T(8,128)(2,1)S(1)} %shard_map.51), channel_id=1, source_target_pairs={{8,16},{9,17},{24,0},{25,1},{0,8},{1,9},{16,24},{17,25},{10,18},{1... | collective-permute-start | bytes 786440 | tf_op jit(solution)/shard_map/ppermute | solution.py:323
  5.7 8.5 %collective-permute-start.4 = (f32[128,512]{1,0:T(8,128)S(1)}, f32[128,512]{1,0:T(8,128)S(1)}, u32[]{:S(2)}, u32[]{:S(2)}) collective-permute-start(f32[128,512]{1,0:T(8,128)S(1)} %get-tuple-element.23), channel_id=1, source_target_pairs={{8,17},{9,16},{24,1},{25,0},{0,8},{1,9},{16,24},{17,25},{10,19},{1... | collective-permute-start | bytes 786440 | tf_op jit(solution)/shard_map/ppermute | solution.py:323
  6.3 10.2 %collective-permute-start.5 = (f32[128,512]{1,0:T(8,128)S(1)}, f32[128,512]{1,0:T(8,128)S(1)}, u32[]{:S(2)}, u32[]{:S(2)}) collective-permute-start(f32[128,512]{1,0:T(8,128)S(1)} %get-tuple-element.24), channel_id=1, source_target_pairs={{8,16},{9,17},{24,0},{25,1},{0,8},{1,9},{16,24},{17,25},{10,18},{1... | collective-permute-start | bytes 786440 | tf_op jit(solution)/shard_map/ppermute | solution.py:323
  9.1 7.8 %collective-permute-start.6 = (f32[128,512]{1,0:T(8,128)S(1)}, f32[128,512]{1,0:T(8,128)S(1)}, u32[]{:S(2)}, u32[]{:S(2)}) collective-permute-start(f32[128,512]{1,0:T(8,128)S(1)} %get-tuple-element.25), channel_id=1, source_target_pairs={{8,1},{9,0},{24,17},{25,16},{0,8},{1,9},{16,24},{17,25},{10,3},{11... | collective-permute-start | bytes 786440 | tf_op jit(solution)/shard_map/ppermute | solution.py:323
  17.5 7.3 %collective-permute-start.9 = (bf16[256,512]{1,0:T(8,128)(2,1)S(1)}, bf16[256,512]{1,0:T(8,128)(2,1)S(1)}, u32[]{:S(2)}, u32[]{:S(2)}) collective-permute-start(bf16[256,512]{1,0:T(8,128)(2,1)S(1)} %get-tuple-element.26.new), channel_id=1, source_target_pairs={{0,8},{8,0},{1,9},{9,1},{16,24},{24,16},{17,25},{25,17},{2,10},{10... | collective-permute-start | bytes 786440 | tf_op jit(solution)/shard_map/ppermute | solution.py:314
  17.6 7.3 %collective-permute-start.8 = (bf16[256,512]{1,0:T(8,128)(2,1)S(1)}, bf16[256,512]{1,0:T(8,128)(2,1)S(1)}, u32[]{:S(2)}, u32[]{:S(2)}) collective-permute-start(bf16[256,512]{1,0:T(8,128)(2,1)S(1)} %get-tuple-element.26.new), channel_id=1, source_target_pairs={{0,9},{1,8},{16,25},{17,24},{8,0},{9,1},{24,16},{25,17},{2,11},{3,... | collective-permute-start | bytes 786440 | tf_op jit(solution)/shard_map/ppermute | solution.py:323
  18.7 6.1 %collective-permute-start.7 = (bf16[256,512]{1,0:T(8,128)(2,1)S(1)}, bf16[256,512]{1,0:T(8,128)(2,1)S(1)}, u32[]{:S(2)}, u32[]{:S(2)}) collective-permute-start(bf16[256,512]{1,0:T(8,128)(2,1)S(1)} %get-tuple-element.26.new), channel_id=1, source_target_pairs={{0,24},{1,25},{16,8},{17,9},{8,0},{9,1},{24,16},{25,17},{2,26},{3,... | collective-permute-start | bytes 786440 | tf_op jit(solution)/shard_map/ppermute | solution.py:323
  23.9 2.6 %collective-permute-start.13 = (bf16[128,512]{1,0:T(8,128)(2,1)S(1)}, bf16[128,512]{1,0:T(8,128)(2,1)S(1)}, u32[]{:S(2)}, u32[]{:S(2)}) collective-permute-start(bf16[128,512]{1,0:T(8,128)(2,1)S(1)} %get-tuple-element.31), channel_id=1, source_target_pairs={{0,25},{1,24},{16,9},{17,8},{8,0},{9,1},{24,16},{25,17},{2,27},{3,... | collective-permute-start | bytes 393224 | tf_op jit(solution)/shard_map/ppermute | solution.py:323
  24.0 4.2 %collective-permute-start.12 = (bf16[128,512]{1,0:T(8,128)(2,1)S(1)}, bf16[128,512]{1,0:T(8,128)(2,1)S(1)}, u32[]{:S(2)}, u32[]{:S(2)}) collective-permute-start(bf16[128,512]{1,0:T(8,128)(2,1)S(1)} %get-tuple-element.31), channel_id=1, source_target_pairs={{0,9},{1,8},{16,25},{17,24},{8,0},{9,1},{24,16},{25,17},{2,11},{3,... | collective-permute-start | bytes 393224 | tf_op jit(solution)/shard_map/ppermute | solution.py:323
  24.8 4.7 %collective-permute-start.11 = (bf16[128,512]{1,0:T(8,128)(2,1)S(1)}, bf16[128,512]{1,0:T(8,128)(2,1)S(1)}, u32[]{:S(2)}, u32[]{:S(2)}) collective-permute-start(bf16[128,512]{1,0:T(8,128)(2,1)S(1)} %get-tuple-element.30.mine), channel_id=1, source_target_pairs={{0,24},{1,25},{16,8},{17,9},{8,0},{9,1},{24,16},{25,17},{2,26},{3,... | collective-permute-start | bytes 393224 | tf_op jit(solution)/shard_map/ppermute | solution.py:323
  25.0 5.9 %collective-permute-start.10 = (bf16[256,512]{1,0:T(8,128)(2,1)S(1)}, bf16[256,512]{1,0:T(8,128)(2,1)S(1)}, u32[]{:S(2)}, u32[]{:S(2)}) collective-permute-start(bf16[256,512]{1,0:T(8,128)(2,1)S(1)} %get-tuple-element.27), channel_id=1, source_target_pairs={{0,8},{8,0},{1,9},{9,1},{16,24},{24,16},{17,25},{25,17},{2,10},{10... | collective-permute-start | bytes 786440 | tf_op jit(solution)/shard_map/ppermute | solution.py:314
  25.6 3.9 %collective-permute-start.14 = (bf16[128,512]{1,0:T(8,128)(2,1)S(1)}, bf16[128,512]{1,0:T(8,128)(2,1)S(1)}, u32[]{:S(2)}, u32[]{:S(2)}) collective-permute-start(bf16[128,512]{1,0:T(8,128)(2,1)S(1)} %get-tuple-element.30.mine), channel_id=1, source_target_pairs={{0,8},{8,0},{1,9},{9,1},{16,24},{24,16},{17,25},{25,17},{2,10},{10... | collective-permute-start | bytes 393224 | tf_op jit(solution)/shard_map/ppermute | solution.py:314
  26.5 3.1 %collective-permute-start.17 = (bf16[128,512]{1,0:T(8,128)(2,1)S(1)}, bf16[128,512]{1,0:T(8,128)(2,1)S(1)}, u32[]{:S(2)}, u32[]{:S(2)}) collective-permute-start(bf16[128,512]{1,0:T(8,128)(2,1)S(1)} %collective-permute-done.13.up_d), channel_id=1, source_target_pairs={{0,8},{8,0},{1,9},{9,1},{16,24},{24,16},{17,25},{25,17},{2,10},{10... | collective-permute-start | bytes 393224 | tf_op jit(solution)/shard_map/ppermute | solution.py:314
  28.2 2.3 %collective-permute-start.16 = (bf16[128,512]{1,0:T(8,128)(2,1)S(1)}, bf16[128,512]{1,0:T(8,128)(2,1)S(1)}, u32[]{:S(2)}, u32[]{:S(2)}) collective-permute-start(bf16[128,512]{1,0:T(8,128)(2,1)S(1)} %collective-permute-done.12.up_y), channel_id=1, source_target_pairs={{0,8},{8,0},{1,9},{9,1},{16,24},{24,16},{17,25},{25,17},{2,10},{10... | collective-permute-start | bytes 393224 | tf_op jit(solution)/shard_map/ppermute | solution.py:314
  29.5 1.3 %collective-permute-start.15 = (bf16[128,512]{1,0:T(8,128)(2,1)S(1)}, bf16[128,512]{1,0:T(8,128)(2,1)S(1)}, u32[]{:S(2)}, u32[]{:S(2)}) collective-permute-start(bf16[128,512]{1,0:T(8,128)(2,1)S(1)} %collective-permute-done.11.up_x), channel_id=1, source_target_pairs={{0,8},{8,0},{1,9},{9,1},{16,24},{24,16},{17,25},{25,17},{2,10},{10... | collective-permute-start | bytes 393224 | tf_op jit(solution)/shard_map/ppermute | solution.py:314

commit v4 on v3

--- a/solution.py
+++ b/solution.py
@@ -131,7 +131,9 @@
     return result
 
 
-def load_kernel(grads, momentum, slots, grads_near, momentum_near, plan, slots_near, sems):
+def load_kernel(
+    grads, momentum, slots, grads_near, momentum_near, faded, plan, slots_near, sems
+):
     copies = [
         pltpu.make_async_copy(source, target, sems.at[k])
         for k, (source, target) in enumerate(
@@ -157,17 +159,17 @@
     entries.append(jnp.where(comes_y, 3, jnp.where(comes_x, 2, jnp.where(at_0, zero, one))))
     entries.append(jnp.where(at_1, one, zero))
     entries.append(jnp.where(mine, one + away, zero))
-    entries.append(leaves_x)
     row = lax.broadcasted_iota(jnp.int32, plan.shape, 0)
     table = jnp.zeros(plan.shape, jnp.int32)
     for k, entry in enumerate(entries):
         table = jnp.where(row == k, entry, table)
     plan[...] = table
     copies[1].wait()
+    faded[...] = (MOMENT * momentum_near[...].astype(jnp.float32)).astype(jnp.bfloat16)
     copies[2].wait()
 
 
-SOURCE, GIVER, SLOT, LEAVES_X = 4, 5, 6, 7
+SOURCE, GIVER, SLOT = 4, 5, 6
 
 
 def give_kernel(plan, mom, mom_other, mom_out):
@@ -245,34 +247,34 @@
             current[part * half : (part + 1) * half] = pieces[part] / norm
 
 
-def orthogonalize_kernel(start, others, mine):
+def middle_kernel(steps, before, after):
+    _, c, _ = here()
+
+    @pl.when(c == 0)
+    def _():
+        value = before[...]
+        for _ in range(steps):
+            value = polynomial_step(value)
+        after[...] = value
+
+
+def last_kernel(steps, start, others, mine):
     _, c, _ = here()
     half = mine.shape[0]
 
     @pl.when(c == 0)
     def _():
         value = start[...]
-        for _ in range(ITERS):
+        for _ in range(steps):
             value = polynomial_step(value)
         value = (FACTOR * value).astype(jnp.bfloat16)
         mine[...] = value[:half]
         others[...] = value[half:]
 
 
-def back_kernel(plan, mom, new_x, new_y, new_l, back, hold):
-    _, c, _ = here()
-
-    @pl.when(c == 1)
-    def _():
-        back[...] = jnp.where(plan[LEAVES_X, 0] == 1, new_x[...], new_y[...])
-
-    faded = (MOMENT * mom[...].astype(jnp.float32)).astype(jnp.bfloat16)
-    slot = jnp.where(c == 1, plan[SLOT, 0], 0)
-    hold[...] = pick([faded, new_l[...], new_x[...], new_y[...]], slot)
-
-
 def finish_kernel(
-    plan, new, back, hold, up_x, up_y, up_d, up_l, in_x, in_y, in_d, mine, updates, moment, sems
+    plan, faded, new, back, back_in, up_d, up_x, up_y, up_l, in_d, in_x, in_y, mine,
+    updates, moment, sems,
 ):
     _, c, _ = here()
     for core, sources in ((0, (mine, in_y, in_x, in_d)), (1, (up_l, up_y, up_x, up_d))):
@@ -284,11 +286,12 @@
                 pltpu.make_async_copy(source, updates.at[m], sems.at[flip]).start()
 
     slot = plan[SLOT, 0]
-    held = (c == 1) | (slot == 0)
+    handed = (slot == 3) & (c == 1)
     for chosen, source in (
-        (held, hold),
-        (jnp.logical_not(held) & (slot == 1), new),
-        (jnp.logical_not(held) & (slot > 1), back),
+        (slot == 0, faded),
+        (slot == 1, new),
+        ((slot > 1) & jnp.logical_not(handed), back),
+        (handed, back_in),
     ):
 
         @pl.when(chosen)
@@ -297,7 +300,7 @@
 
     for flip in range(4):
         pltpu.make_async_copy(mine, updates.at[flip], sems.at[flip]).wait()
-    pltpu.make_async_copy(hold, moment.at[0], sems.at[4]).wait()
+    pltpu.make_async_copy(faded, moment.at[0], sems.at[4]).wait()
 
 
 def chip_device(x, c, y):
@@ -320,6 +323,12 @@
         for x, y in CHIPS
     ]
     pairs += [(chip_device(x, 1 - sender, y), chip_device(x, sender, y)) for x, y in CHIPS]
+    return lax.ppermute(value, AXES, pairs)
+
+
+def both_ways(value):
+    pairs = [(chip_device(x, 0, y), chip_device(1 - x, 1, y)) for x, y in CHIPS]
+    pairs += [(chip_device(x, 1, y), chip_device(x, 0, 1 - y)) for x, y in CHIPS]
     return lax.ppermute(value, AXES, pairs)
 
 
@@ -349,10 +358,10 @@
 
     mom_other = swap_cores(momentum)
     far = functools.partial(pltpu.with_memory_space_constraint, memory_space=pltpu.HBM)
-    own, mom, plan = run(
+    own, mom, faded, plan = run(
         load_kernel,
         [ANY] * 3,
-        [near, moment, table],
+        [near, moment, moment, table],
         scratch=[pltpu.SMEM((mats,), jnp.int32), pltpu.SemaphoreType.DMA((3,))],
         moved=2**21,
     )(far(grads), far(momentum), far(owner_slot))
@@ -370,27 +379,28 @@
     new, current = run(nesterov_kernel, [VMEM] * 10, [moment, whole], moved=2**20)(
         plan, mom_other, mom_x, mom_y, grads_other, in_d, in_x, in_y, own, mom
     )
-    new_x = across(new, 0, 1, 0)
-    new_y = across(new, 0, 0, 1)
     new_l = swap_cores(new)
-    others, mine = run(orthogonalize_kernel, [VMEM], [update, update], moved=2**20)(current)
+    (current,) = run(functools.partial(middle_kernel, 2), [VMEM], [whole], moved=2**20)(current)
+    new_l, current = lax.optimization_barrier((new_l, current))
+    new = jnp.where(lax.axis_index("dp") % 2 == 0, new, new_l)
+    back = both_ways(new)
+    others, mine = run(
+        functools.partial(last_kernel, ITERS - 2), [VMEM], [update, update], moved=2**20
+    )(current)
+    up_d = across(others, 0, 1, 1)
     up_x = across(mine, 0, 1, 0)
     up_y = across(others, 0, 0, 1)
-    up_d = across(others, 0, 1, 1)
     up_l = swap_cores(mine)
-    back, hold = run(back_kernel, [VMEM] * 5, [moment, moment], moved=2**19)(
-        plan, mom, new_x, new_y, new_l
-    )
     back_in = swap_cores(back)
-    over_x, over_y, over_d = swap_cores(up_x), swap_cores(up_y), swap_cores(up_d)
+    over_d, over_x, over_y = swap_cores(up_d), swap_cores(up_x), swap_cores(up_y)
     updates, new_momentum = run(
         finish_kernel,
-        [VMEM] * 12,
+        [VMEM] * 13,
         [jax.ShapeDtypeStruct((mats, half, width), bf16), jax.ShapeDtypeStruct(momentum.shape, bf16)],
         out_specs=[ANY, ANY],
         scratch=[pltpu.SemaphoreType.DMA((5,))],
         moved=2**20,
-    )(plan, new, back_in, hold, up_x, up_y, up_d, up_l, over_x, over_y, over_d, mine)
+    )(plan, faded, new, back, back_in, up_d, up_x, up_y, up_l, over_d, over_x, over_y, mine)
     return (updates, new_momentum)
 
 

time: 32 us -> 30.5 us (0.953)
  starting transfers between devices: 13.3 us -> 12.4 us
  waiting for transfers between devices: 9.95 us -> 9.34 us
    ppermute x10 -> x8, starting transfers between devices: 8.65 us -> 7.43 us  [across(): return lax.ppermute(value, AXES, pairs)]
    ppermute x10 -> x8, waiting for transfers between devices: 8.58 us -> 7.37 us  [across(): return lax.ppermute(value, AXES, pairs)]
    ppermute x0 -> x1, waiting for transfers between devices: none -> 0.94 us  [both_ways(): return lax.ppermute(value, AXES, pairs)]
    ppermute x0 -> x1, starting transfers between devices: none -> 0.72 us  [both_ways(): return lax.ppermute(value, AXES, pairs)]
    ppermute x8, starting transfers between devices: 4.69 us -> 4.26 us  [swap_cores(): return lax.ppermute(value, AXES, pairs)]
    ppermute x8, waiting for transfers between devices: 1.37 us -> 1.02 us  [swap_cores(): return lax.ppermute(value, AXES, pairs)]
  transfers between devices with their start and end apart: 18 -> 17, of which waited for: 8 -> 8; matrix products, arithmetic and copies ran while one was open for 0% -> 0% of each run, Pallas kernels for 20% -> 21%
where the time goes in v4:
time: 30.5 us; the launch traced here: 30.4 us
  starting transfers between devices  12.4 us (41%)
  waiting for transfers between devices  9.34 us (31%)
  Pallas kernels  7.83 us (26%)
  between operations  0.72 us (2%)
    ppermute x8, starting transfers between devices, across(): return lax.ppermute(value, AXES, pairs)  7.43 us
    ppermute x8, waiting for transfers between devices, across(): return lax.ppermute(value, AXES, pairs)  7.37 us
    ppermute x8, starting transfers between devices, swap_cores(): return lax.ppermute(value, AXES, pairs)  4.26 us
    pallas_call x1, Pallas kernels, per_device_chips(): run(functools.partial(last_kernel, ITERS - 2), [VMEM], [update, update],...  2.95 us
    pallas_call x1, Pallas kernels, per_device_chips(): run(functools.partial(middle_kernel, 2), [VMEM], [whole], moved=2 ** 20)  2.02 us
    pallas_call x1, Pallas kernels, per_device_chips(): run(load_kernel, [ANY] * 3, [near, moment, moment, table], scratch=[pltpu...  1.34 us
    ppermute x8, waiting for transfers between devices, swap_cores(): return lax.ppermute(value, AXES, pairs)  1.02 us
    pallas_call x1, Pallas kernels, per_device_chips(): run(finish_kernel, [VMEM] * 13, [jax.ShapeDtypeStruct((mats, half, width)...  0.95 us
  transfers between devices with their start and end apart: 17, of which 8 were waited for; matrix products, arithmetic and copies ran while one was open for 0% of the time, Pallas kernels for 21%

profile of v4, /device:TPU:0, one launch (start us, length us, event | category | flops | bytes accessed | tf_op | source)
XLA Modules:
  0.0 30.4 jit_solution(1348736704237894463)
XLA Ops:
  0.6 0.5 %collective-permute-start = (bf16[1,256,512]{2,1,0:T(8,128)(2,1)}, bf16[1,256,512]{2,1,0:T(8,128)(2,1)S(1)}, u32[]{:S(2)}, u32[]{:S(2)}) collective-permute-start(bf16[1,256,512]{2,1,0:T(8,128)(2,1)} %momentum.1), channel_id=1, source_target_pairs={{0,8},{8,0},{1,9},{9,1},{16,24},{24,16},{17,25},{25,17},{2,10},{10... | collective-permute-start | bytes 786440 | tf_op jit(solution)/shard_map/ppermute | solution.py:317
  1.2 1.3 %shard_map.50 = (f32[4,128,512]{2,1,0:T(8,128)S(1)}, bf16[256,512]{1,0:T(8,128)(2,1)S(1)}, bf16[256,512]{1,0:T(8,128)(2,1)S(1)}, s32[8,128]{1,0:T(8,128)S(1)}) custom-call(f32[1,4,128,512]{3,2,1,0:T(8,128)} %grads.1, bf16[1,256,512]{2,1,0:T(8,128)(2,1)} %momentum.1, s32[4]{0:T(128)} %slots.1), custom_call_target="tpu_custom_call" | custom-call | bytes 2097152 | tf_op jit(solution)/shard_map/pallas_call | solution.py:361
  2.5 0.4 %collective-permute-start.3 = (f32[1,4,128,512]{3,2,1,0:T(8,128)S(1)}, f32[1,4,128,512]{3,2,1,0:T(8,128)S(1)}, u32[]{:S(2)}, u32[]{:S(2)}) collective-permute-start(f32[1,4,128,512]{3,2,1,0:T(8,128)S(1)} %copy-done), channel_id=1, source_target_pairs={{0,8},{8,0},{1,9},{9,1},{16,24},{24,16},{17,25},{25,17},{2,10},{10... | collective-permute-start | bytes 3145736 | tf_op jit(solution)/shard_map/ppermute | solution.py:317
  3.2 2.5 %collective-permute-start.2 = (bf16[256,512]{1,0:T(8,128)(2,1)S(1)}, bf16[256,512]{1,0:T(8,128)(2,1)S(1)}, u32[]{:S(2)}, u32[]{:S(2)}) collective-permute-start(bf16[256,512]{1,0:T(8,128)(2,1)S(1)} %shard_map.51), channel_id=1, source_target_pairs={{8,1},{9,0},{24,17},{25,16},{0,8},{1,9},{16,24},{17,25},{10,3},{11... | collective-permute-start | bytes 786440 | tf_op jit(solution)/shard_map/ppermute | solution.py:326
  5.7 0.6 %collective-permute-start.4 = (f32[128,512]{1,0:T(8,128)S(1)}, f32[128,512]{1,0:T(8,128)S(1)}, u32[]{:S(2)}, u32[]{:S(2)}) collective-permute-start(f32[128,512]{1,0:T(8,128)S(1)} %get-tuple-element.25), channel_id=1, source_target_pairs={{8,17},{9,16},{24,1},{25,0},{0,8},{1,9},{16,24},{17,25},{10,19},{1... | collective-permute-start | bytes 786440 | tf_op jit(solution)/shard_map/ppermute | solution.py:326
  6.3 2.8 %collective-permute-start.5 = (f32[128,512]{1,0:T(8,128)S(1)}, f32[128,512]{1,0:T(8,128)S(1)}, u32[]{:S(2)}, u32[]{:S(2)}) collective-permute-start(f32[128,512]{1,0:T(8,128)S(1)} %get-tuple-element.26), channel_id=1, source_target_pairs={{8,16},{9,17},{24,0},{25,1},{0,8},{1,9},{16,24},{17,25},{10,18},{1... | collective-permute-start | bytes 786440 | tf_op jit(solution)/shard_map/ppermute | solution.py:326
  9.1 0.6 %collective-permute-done.1.mom_x = bf16[256,512]{1,0:T(8,128)(2,1)S(1)} collective-permute-done((bf16[256,512]{1,0:T(8,128)(2,1)S(1)}, bf16[256,512]{1,0:T(8,128)(2,1)S(1)}, u32[]{:S(2)}, u32[]{:S(2)}) %collective-permute-start.1) | collective-permute-done | bytes 262176 | tf_op jit(solution)/shard_map/ppermute | solution.py:326
  9.7 1.2 %collective-permute-done.2.mom_y = bf16[256,512]{1,0:T(8,128)(2,1)S(1)} collective-permute-done((bf16[256,512]{1,0:T(8,128)(2,1)S(1)}, bf16[256,512]{1,0:T(8,128)(2,1)S(1)}, u32[]{:S(2)}, u32[]{:S(2)}) %collective-permute-start.2) | collective-permute-done | bytes 262176 | tf_op jit(solution)/shard_map/ppermute | solution.py:326
  10.9 2.9 %collective-permute-done.4.in_d = f32[128,512]{1,0:T(8,128)S(1)} collective-permute-done((f32[128,512]{1,0:T(8,128)S(1)}, f32[128,512]{1,0:T(8,128)S(1)}, u32[]{:S(2)}, u32[]{:S(2)}) %collective-permute-start.4) | collective-permute-done | bytes 262176 | tf_op jit(solution)/shard_map/ppermute | solution.py:326
  13.8 2.4 %collective-permute-done.5.in_x = f32[128,512]{1,0:T(8,128)S(1)} collective-permute-done((f32[128,512]{1,0:T(8,128)S(1)}, f32[128,512]{1,0:T(8,128)S(1)}, u32[]{:S(2)}, u32[]{:S(2)}) %collective-permute-start.5) | collective-permute-done | bytes 262176 | tf_op jit(solution)/shard_map/ppermute | solution.py:326
  16.2 0.3 %collective-permute-done.6.in_y = f32[128,512]{1,0:T(8,128)S(1)} collective-permute-done((f32[128,512]{1,0:T(8,128)S(1)}, f32[128,512]{1,0:T(8,128)S(1)}, u32[]{:S(2)}, u32[]{:S(2)}) %collective-permute-start.6) | collective-permute-done | bytes 262176 | tf_op jit(solution)/shard_map/ppermute | solution.py:326
  16.5 0.6 %shard_map.53 = (bf16[256,512]{1,0:T(8,128)(2,1)S(1)}, f32[256,512]{1,0:T(8,128)S(1)}) custom-call(s32[8,128]{1,0:T(8,128)S(1)} %get-tuple-element.19.plan, bf16[1,256,512]{2,1,0:T(8,128)(2,1)S(1)} %collective-permute-done.mom_other, bf16[256,512]{1,0:T(8,128)(2,1)S(1)} %collective-permute-done.1.mom_x, bf16[256,512]{1,0:T(8,128)(2,1)S(1)} %collective-permute-done.2.mom_y, ...), custom_call_target="tpu_custom_call" | custom-call | bytes 1048576 | tf_op jit(solution)/shard_map/pallas_call | solution.py:379
  17.2 2.0 %shard_map.54.start = f32[256,512]{1,0:T(8,128)S(1)} custom-call(f32[256,512]{1,0:T(8,128)S(1)} %get-tuple-element.29.before), custom_call_target="tpu_custom_call" | custom-call | bytes 1048576 | tf_op jit(solution)/shard_map/pallas_call | solution.py:383
  19.2 0.7 %collective-permute-start.8 = (bf16[256,512]{1,0:T(8,128)(2,1)S(1)}, bf16[256,512]{1,0:T(8,128)(2,1)S(1)}, u32[]{:S(2)}, u32[]{:S(2)}) collective-permute-start(bf16[256,512]{1,0:T(8,128)(2,1)S(1)} %broadcast_select_fusion.new), channel_id=1, source_target_pairs={{0,24},{1,25},{16,8},{17,9},{8,1},{9,0},{24,17},{25,16},{2,26},{3,... | collective-permute-start | bytes 786440 | tf_op jit(solution)/shard_map/ppermute | solution.py:332
  20.0 2.9 %shard_map.55 = (bf16[128,512]{1,0:T(8,128)(2,1)S(1)}, bf16[128,512]{1,0:T(8,128)(2,1)S(1)}) custom-call(f32[256,512]{1,0:T(8,128)S(1)} %shard_map.54.start), custom_call_target="tpu_custom_call" | custom-call | bytes 1048576 | tf_op jit(solution)/shard_map/pallas_call | solution.py:387
  23.0 0.9 %collective-permute-start.11 = (bf16[128,512]{1,0:T(8,128)(2,1)S(1)}, bf16[128,512]{1,0:T(8,128)(2,1)S(1)}, u32[]{:S(2)}, u32[]{:S(2)}) collective-permute-start(bf16[128,512]{1,0:T(8,128)(2,1)S(1)} %get-tuple-element.33.mine), channel_id=1, source_target_pairs={{0,24},{1,25},{16,8},{17,9},{8,0},{9,1},{24,16},{25,17},{2,26},{3,... | collective-permute-start | bytes 393224 | tf_op jit(solution)/shard_map/ppermute | solution.py:326
  24.2 0.9 %collective-permute-done.8.back = bf16[256,512]{1,0:T(8,128)(2,1)S(1)} collective-permute-done((bf16[256,512]{1,0:T(8,128)(2,1)S(1)}, bf16[256,512]{1,0:T(8,128)(2,1)S(1)}, u32[]{:S(2)}, u32[]{:S(2)}) %collective-permute-start.8) | collective-permute-done | bytes 262176 | tf_op jit(solution)/shard_map/ppermute | solution.py:332
  25.2 0.4 %collective-permute-start.13 = (bf16[128,512]{1,0:T(8,128)(2,1)S(1)}, bf16[128,512]{1,0:T(8,128)(2,1)S(1)}, u32[]{:S(2)}, u32[]{:S(2)}) collective-permute-start(bf16[128,512]{1,0:T(8,128)(2,1)S(1)} %get-tuple-element.33.mine), channel_id=1, source_target_pairs={{0,8},{8,0},{1,9},{9,1},{16,24},{24,16},{17,25},{25,17},{2,10},{10... | collective-permute-start | bytes 393224 | tf_op jit(solution)/shard_map/ppermute | solution.py:317
  25.6 1.4 %collective-permute-start.14 = (bf16[128,512]{1,0:T(8,128)(2,1)S(1)}, bf16[128,512]{1,0:T(8,128)(2,1)S(1)}, u32[]{:S(2)}, u32[]{:S(2)}) collective-permute-start(bf16[128,512]{1,0:T(8,128)(2,1)S(1)} %collective-permute-done.10.up_d), channel_id=1, source_target_pairs={{0,8},{8,0},{1,9},{9,1},{16,24},{24,16},{17,25},{25,17},{2,10},{10... | collective-permute-start | bytes 393224 | tf_op jit(solution)/shard_map/ppermute | solution.py:317
  27.1 0.9 %collective-permute-start.15 = (bf16[128,512]{1,0:T(8,128)(2,1)S(1)}, bf16[128,512]{1,0:T(8,128)(2,1)S(1)}, u32[]{:S(2)}, u32[]{:S(2)}) collective-permute-start(bf16[128,512]{1,0:T(8,128)(2,1)S(1)} %collective-permute-done.11.up_x), channel_id=1, source_target_pairs={{0,8},{8,0},{1,9},{9,1},{16,24},{24,16},{17,25},{25,17},{2,10},{10... | collective-permute-start | bytes 393224 | tf_op jit(solution)/shard_map/ppermute | solution.py:317
  28.0 0.4 %collective-permute-start.16 = (bf16[128,512]{1,0:T(8,128)(2,1)S(1)}, bf16[128,512]{1,0:T(8,128)(2,1)S(1)}, u32[]{:S(2)}, u32[]{:S(2)}) collective-permute-start(bf16[128,512]{1,0:T(8,128)(2,1)S(1)} %collective-permute-done.12.up_y), channel_id=1, source_target_pairs={{0,8},{8,0},{1,9},{9,1},{16,24},{24,16},{17,25},{25,17},{2,10},{10... | collective-permute-start | bytes 393224 | tf_op jit(solution)/shard_map/ppermute | solution.py:317
  28.4 0.5 %collective-permute-done.15.in_x = bf16[128,512]{1,0:T(8,128)(2,1)S(1)} collective-permute-done((bf16[128,512]{1,0:T(8,128)(2,1)S(1)}, bf16[128,512]{1,0:T(8,128)(2,1)S(1)}, u32[]{:S(2)}, u32[]{:S(2)}) %collective-permute-start.15) | collective-permute-done | bytes 131104 | tf_op jit(solution)/shard_map/ppermute | solution.py:317
  29.0 0.4 %collective-permute-done.16.in_y = bf16[128,512]{1,0:T(8,128)(2,1)S(1)} collective-permute-done((bf16[128,512]{1,0:T(8,128)(2,1)S(1)}, bf16[128,512]{1,0:T(8,128)(2,1)S(1)}, u32[]{:S(2)}, u32[]{:S(2)}) %collective-permute-start.16) | collective-permute-done | bytes 131104 | tf_op jit(solution)/shard_map/ppermute | solution.py:317
  29.4 1.0 %shard_map.56 = (bf16[4,128,512]{2,1,0:T(8,128)(2,1)}, bf16[1,256,512]{2,1,0:T(8,128)(2,1)}) custom-call(s32[8,128]{1,0:T(8,128)S(1)} %get-tuple-element.19.plan, bf16[256,512]{1,0:T(8,128)(2,1)S(1)} %get-tuple-element.20.faded, bf16[256,512]{1,0:T(8,128)(2,1)S(1)} %broadcast_select_fusion.new, bf16[256,512]{1,0:T(8,128)(2,1)S(1)} %collective-permute-done.8.back, ...), custom_call_target="tpu_custom_call" | custom-call | bytes 1048576 | tf_op jit(solution)/shard_map/pallas_call | solution.py:396
  (20 shorter events, 0.9 us)
Async XLA Ops:
  0.6 1.9 %copy-start = (f32[1,4,128,512]{3,2,1,0:T(8,128)S(1)}, f32[1,4,128,512]{3,2,1,0:T(8,128)}, u32[]{:S(2)}) copy-start(f32[1,4,128,512]{3,2,1,0:T(8,128)} %grads.1) | copy-start | bytes 3145732
  0.6 1.9 %collective-permute-start = (bf16[1,256,512]{2,1,0:T(8,128)(2,1)}, bf16[1,256,512]{2,1,0:T(8,128)(2,1)S(1)}, u32[]{:S(2)}, u32[]{:S(2)}) collective-permute-start(bf16[1,256,512]{2,1,0:T(8,128)(2,1)} %momentum.1), channel_id=1, source_target_pairs={{0,8},{8,0},{1,9},{9,1},{16,24},{24,16},{17,25},{25,17},{2,10},{10... | collective-permute-start | bytes 786440 | tf_op jit(solution)/shard_map/ppermute | solution.py:317
  2.5 3.2 %collective-permute-start.3 = (f32[1,4,128,512]{3,2,1,0:T(8,128)S(1)}, f32[1,4,128,512]{3,2,1,0:T(8,128)S(1)}, u32[]{:S(2)}, u32[]{:S(2)}) collective-permute-start(f32[1,4,128,512]{3,2,1,0:T(8,128)S(1)} %copy-done), channel_id=1, source_target_pairs={{0,8},{8,0},{1,9},{9,1},{16,24},{24,16},{17,25},{25,17},{2,10},{10... | collective-permute-start | bytes 3145736 | tf_op jit(solution)/shard_map/ppermute | solution.py:317
  2.9 6.8 %collective-permute-start.1 = (bf16[256,512]{1,0:T(8,128)(2,1)S(1)}, bf16[256,512]{1,0:T(8,128)(2,1)S(1)}, u32[]{:S(2)}, u32[]{:S(2)}) collective-permute-start(bf16[256,512]{1,0:T(8,128)(2,1)S(1)} %shard_map.51), channel_id=1, source_target_pairs={{8,16},{9,17},{24,0},{25,1},{0,8},{1,9},{16,24},{17,25},{10,18},{1... | collective-permute-start | bytes 786440 | tf_op jit(solution)/shard_map/ppermute | solution.py:326
  3.2 7.7 %collective-permute-start.2 = (bf16[256,512]{1,0:T(8,128)(2,1)S(1)}, bf16[256,512]{1,0:T(8,128)(2,1)S(1)}, u32[]{:S(2)}, u32[]{:S(2)}) collective-permute-start(bf16[256,512]{1,0:T(8,128)(2,1)S(1)} %shard_map.51), channel_id=1, source_target_pairs={{8,1},{9,0},{24,17},{25,16},{0,8},{1,9},{16,24},{17,25},{10,3},{11... | collective-permute-start | bytes 786440 | tf_op jit(solution)/shard_map/ppermute | solution.py:326
  5.7 8.1 %collective-permute-start.4 = (f32[128,512]{1,0:T(8,128)S(1)}, f32[128,512]{1,0:T(8,128)S(1)}, u32[]{:S(2)}, u32[]{:S(2)}) collective-permute-start(f32[128,512]{1,0:T(8,128)S(1)} %get-tuple-element.25), channel_id=1, source_target_pairs={{8,17},{9,16},{24,1},{25,0},{0,8},{1,9},{16,24},{17,25},{10,19},{1... | collective-permute-start | bytes 786440 | tf_op jit(solution)/shard_map/ppermute | solution.py:326
  6.3 9.8 %collective-permute-start.5 = (f32[128,512]{1,0:T(8,128)S(1)}, f32[128,512]{1,0:T(8,128)S(1)}, u32[]{:S(2)}, u32[]{:S(2)}) collective-permute-start(f32[128,512]{1,0:T(8,128)S(1)} %get-tuple-element.26), channel_id=1, source_target_pairs={{8,16},{9,17},{24,0},{25,1},{0,8},{1,9},{16,24},{17,25},{10,18},{1... | collective-permute-start | bytes 786440 | tf_op jit(solution)/shard_map/ppermute | solution.py:326
  9.1 7.4 %collective-permute-start.6 = (f32[128,512]{1,0:T(8,128)S(1)}, f32[128,512]{1,0:T(8,128)S(1)}, u32[]{:S(2)}, u32[]{:S(2)}) collective-permute-start(f32[128,512]{1,0:T(8,128)S(1)} %get-tuple-element.27), channel_id=1, source_target_pairs={{8,1},{9,0},{24,17},{25,16},{0,8},{1,9},{16,24},{17,25},{10,3},{11... | collective-permute-start | bytes 786440 | tf_op jit(solution)/shard_map/ppermute | solution.py:326
  17.1 2.1 %collective-permute-start.7 = (bf16[256,512]{1,0:T(8,128)(2,1)S(1)}, bf16[256,512]{1,0:T(8,128)(2,1)S(1)}, u32[]{:S(2)}, u32[]{:S(2)}) collective-permute-start(bf16[256,512]{1,0:T(8,128)(2,1)S(1)} %get-tuple-element.28), channel_id=1, source_target_pairs={{0,8},{8,0},{1,9},{9,1},{16,24},{24,16},{17,25},{25,17},{2,10},{10... | collective-permute-start | bytes 786440 | tf_op jit(solution)/shard_map/ppermute | solution.py:317
  19.2 5.8 %collective-permute-start.8 = (bf16[256,512]{1,0:T(8,128)(2,1)S(1)}, bf16[256,512]{1,0:T(8,128)(2,1)S(1)}, u32[]{:S(2)}, u32[]{:S(2)}) collective-permute-start(bf16[256,512]{1,0:T(8,128)(2,1)S(1)} %broadcast_select_fusion.new), channel_id=1, source_target_pairs={{0,24},{1,25},{16,8},{17,9},{8,1},{9,0},{24,17},{25,16},{2,26},{3,... | collective-permute-start | bytes 786440 | tf_op jit(solution)/shard_map/ppermute | solution.py:332
  22.9 2.7 %collective-permute-start.10 = (bf16[128,512]{1,0:T(8,128)(2,1)S(1)}, bf16[128,512]{1,0:T(8,128)(2,1)S(1)}, u32[]{:S(2)}, u32[]{:S(2)}) collective-permute-start(bf16[128,512]{1,0:T(8,128)(2,1)S(1)} %get-tuple-element.32), channel_id=1, source_target_pairs={{0,25},{1,24},{16,9},{17,8},{8,0},{9,1},{24,16},{25,17},{2,27},{3,... | collective-permute-start | bytes 393224 | tf_op jit(solution)/shard_map/ppermute | solution.py:326
  23.0 4.1 %collective-permute-start.11 = (bf16[128,512]{1,0:T(8,128)(2,1)S(1)}, bf16[128,512]{1,0:T(8,128)(2,1)S(1)}, u32[]{:S(2)}, u32[]{:S(2)}) collective-permute-start(bf16[128,512]{1,0:T(8,128)(2,1)S(1)} %get-tuple-element.33.mine), channel_id=1, source_target_pairs={{0,24},{1,25},{16,8},{17,9},{8,0},{9,1},{24,16},{25,17},{2,26},{3,... | collective-permute-start | bytes 393224 | tf_op jit(solution)/shard_map/ppermute | solution.py:326
  23.9 4.1 %collective-permute-start.12 = (bf16[128,512]{1,0:T(8,128)(2,1)S(1)}, bf16[128,512]{1,0:T(8,128)(2,1)S(1)}, u32[]{:S(2)}, u32[]{:S(2)}) collective-permute-start(bf16[128,512]{1,0:T(8,128)(2,1)S(1)} %get-tuple-element.32), channel_id=1, source_target_pairs={{0,9},{1,8},{16,25},{17,24},{8,0},{9,1},{24,16},{25,17},{2,11},{3,... | collective-permute-start | bytes 393224 | tf_op jit(solution)/shard_map/ppermute | solution.py:326
  25.1 4.3 %collective-permute-start.9 = (bf16[256,512]{1,0:T(8,128)(2,1)S(1)}, bf16[256,512]{1,0:T(8,128)(2,1)S(1)}, u32[]{:S(2)}, u32[]{:S(2)}) collective-permute-start(bf16[256,512]{1,0:T(8,128)(2,1)S(1)} %collective-permute-done.8.back), channel_id=1, source_target_pairs={{0,8},{8,0},{1,9},{9,1},{16,24},{24,16},{17,25},{25,17},{2,10},{10... | collective-permute-start | bytes 786440 | tf_op jit(solution)/shard_map/ppermute | solution.py:317
  25.2 3.2 %collective-permute-start.13 = (bf16[128,512]{1,0:T(8,128)(2,1)S(1)}, bf16[128,512]{1,0:T(8,128)(2,1)S(1)}, u32[]{:S(2)}, u32[]{:S(2)}) collective-permute-start(bf16[128,512]{1,0:T(8,128)(2,1)S(1)} %get-tuple-element.33.mine), channel_id=1, source_target_pairs={{0,8},{8,0},{1,9},{9,1},{16,24},{24,16},{17,25},{25,17},{2,10},{10... | collective-permute-start | bytes 393224 | tf_op jit(solution)/shard_map/ppermute | solution.py:317
  25.6 2.8 %collective-permute-start.14 = (bf16[128,512]{1,0:T(8,128)(2,1)S(1)}, bf16[128,512]{1,0:T(8,128)(2,1)S(1)}, u32[]{:S(2)}, u32[]{:S(2)}) collective-permute-start(bf16[128,512]{1,0:T(8,128)(2,1)S(1)} %collective-permute-done.10.up_d), channel_id=1, source_target_pairs={{0,8},{8,0},{1,9},{9,1},{16,24},{24,16},{17,25},{25,17},{2,10},{10... | collective-permute-start | bytes 393224 | tf_op jit(solution)/shard_map/ppermute | solution.py:317
  27.1 1.9 %collective-permute-start.15 = (bf16[128,512]{1,0:T(8,128)(2,1)S(1)}, bf16[128,512]{1,0:T(8,128)(2,1)S(1)}, u32[]{:S(2)}, u32[]{:S(2)}) collective-permute-start(bf16[128,512]{1,0:T(8,128)(2,1)S(1)} %collective-permute-done.11.up_x), channel_id=1, source_target_pairs={{0,8},{8,0},{1,9},{9,1},{16,24},{24,16},{17,25},{25,17},{2,10},{10... | collective-permute-start | bytes 393224 | tf_op jit(solution)/shard_map/ppermute | solution.py:317
  28.0 1.4 %collective-permute-start.16 = (bf16[128,512]{1,0:T(8,128)(2,1)S(1)}, bf16[128,512]{1,0:T(8,128)(2,1)S(1)}, u32[]{:S(2)}, u32[]{:S(2)}) collective-permute-start(bf16[128,512]{1,0:T(8,128)(2,1)S(1)} %collective-permute-done.12.up_y), channel_id=1, source_target_pairs={{0,8},{8,0},{1,9},{9,1},{16,24},{24,16},{17,25},{25,17},{2,10},{10... | collective-permute-start | bytes 393224 | tf_op jit(solution)/shard_map/ppermute | solution.py:317

commit v5 on v4

--- a/solution.py
+++ b/solution.py
@@ -200,8 +200,8 @@
     dot = functools.partial(lax.dot_general, preferred_element_type=jnp.float32)
     plain, turned = (((1,), (0,)), ((), ())), (((1,), (1,)), ((), ()))
     high, low = parts_of(current)
-    mixed = dot(high, low, turned)
-    gram = dot(high, high, turned) + (mixed + mixed.T)
+    mixed = dot(high, low, turned).astype(jnp.bfloat16)
+    gram = dot(high, high, turned) + (mixed.astype(jnp.float32) + mixed.T.astype(jnp.float32))
     gram_high, gram_low = parts_of(gram)
     rows = current.shape[0] // 2
     blocks = []
@@ -218,9 +218,7 @@
     return jnp.concatenate(blocks, axis=0)
 
 
-def nesterov_kernel(
-    plan, mom_other, mom_x, mom_y, other, in_d, in_x, in_y, own, mom, new, current
-):
+def ready_kernel(plan, mom_other, mom_x, mom_y, other, own, mom, base, held):
     _, c, y = here()
     half = own.shape[1]
 
@@ -228,31 +226,40 @@
     def _():
         m = plan[0, 0]
         source = plan[SOURCE, 0]
-        squares = jnp.float32(0)
-        pieces = []
+        base[...] = own[m] + other[0, m]
         for part, start in enumerate((y * half, (1 - y) * half)):
             rows = pl.ds(pl.multiple_of(start, half), half)
-            if part == 0:
-                total = (own[m] + other[0, m]) + in_x[...]
-            else:
-                total = in_y[...] + in_d[...]
-            held = pick([mom[rows], mom_other[0, rows], mom_x[rows], mom_y[rows]], source)
-            buffer = MOMENT * held.astype(jnp.float32) + total
+            held[part * half : (part + 1) * half] = pick(
+                [mom[rows], mom_other[0, rows], mom_x[rows], mom_y[rows]], source
+            )
+
+
+def nesterov_kernel(base, held, in_d, in_x, in_y, new, nesterov, scale):
+    _, c, y = here()
+    half = base.shape[0]
+
+    @pl.when(c == 0)
+    def _():
+        squares = jnp.zeros((1, base.shape[1]), jnp.float32)
+        for part, start in enumerate((y * half, (1 - y) * half)):
+            rows = pl.ds(pl.multiple_of(start, half), half)
+            local = slice(part * half, (part + 1) * half)
+            total = base[...] + in_x[...] if part == 0 else in_y[...] + in_d[...]
+            buffer = MOMENT * held[local].astype(jnp.float32) + total
             new[rows] = buffer.astype(jnp.bfloat16)
             piece = total + MOMENT * buffer
-            squares = squares + jnp.sum(piece * piece)
-            pieces.append(piece)
-        norm = jnp.sqrt(squares) + 1e-07
-        for part in (0, 1):
-            current[part * half : (part + 1) * half] = pieces[part] / norm
-
-
-def middle_kernel(steps, before, after):
+            nesterov[local] = piece
+            squares = squares + jnp.sum(piece * piece, axis=0, keepdims=True)
+        norm = jnp.sqrt(jnp.sum(squares, axis=1, keepdims=True)) + 1e-07
+        scale[...] = jnp.broadcast_to(1.0 / norm, scale.shape)
+
+
+def middle_kernel(steps, scale, before, after):
     _, c, _ = here()
 
     @pl.when(c == 0)
     def _():
-        value = before[...]
+        value = before[...] * scale[0:1, 0:1]
         for _ in range(steps):
             value = polynomial_step(value)
         after[...] = value
@@ -272,19 +279,28 @@
         others[...] = value[half:]
 
 
+def place(plan, core, pieces, updates, sems):
+    _, c, _ = here()
+
+    @pl.when(c == core)
+    def _():
+        for k, (flip, source) in enumerate(pieces):
+            pltpu.make_async_copy(source, updates.at[plan[flip, 0]], sems.at[k]).start()
+
+
+def early_kernel(plan, up_d, up_l, in_d, mine, updates, sems):
+    place(plan, 0, ((0, mine), (3, in_d)), updates, sems)
+    place(plan, 1, ((0, up_l), (3, up_d)), updates, sems)
+    for k in (0, 1):
+        pltpu.make_async_copy(mine, updates.at[k], sems.at[k]).wait()
+
+
 def finish_kernel(
-    plan, faded, new, back, back_in, up_d, up_x, up_y, up_l, in_d, in_x, in_y, mine,
-    updates, moment, sems,
+    plan, faded, new, back, back_in, up_x, up_y, in_x, in_y, _, updates, moment, sems
 ):
     _, c, _ = here()
-    for core, sources in ((0, (mine, in_y, in_x, in_d)), (1, (up_l, up_y, up_x, up_d))):
-
-        @pl.when(c == core)
-        def _():
-            for flip, source in enumerate(sources):
-                m = plan[flip, 0]
-                pltpu.make_async_copy(source, updates.at[m], sems.at[flip]).start()
-
+    place(plan, 0, ((2, in_x), (1, in_y)), updates, sems)
+    place(plan, 1, ((2, up_x), (1, up_y)), updates, sems)
     slot = plan[SLOT, 0]
     handed = (slot == 3) & (c == 1)
     for chosen, source in (
@@ -296,11 +312,11 @@
 
         @pl.when(chosen)
         def _():
-            pltpu.make_async_copy(source, moment.at[0], sems.at[4]).start()
-
-    for flip in range(4):
-        pltpu.make_async_copy(mine, updates.at[flip], sems.at[flip]).wait()
-    pltpu.make_async_copy(faded, moment.at[0], sems.at[4]).wait()
+            pltpu.make_async_copy(source, moment.at[0], sems.at[2]).start()
+
+    for k in (0, 1):
+        pltpu.make_async_copy(up_x, updates.at[k], sems.at[k]).wait()
+    pltpu.make_async_copy(faded, moment.at[0], sems.at[2]).wait()
 
 
 def chip_device(x, c, y):
@@ -332,15 +348,16 @@
     return lax.ppermute(value, AXES, pairs)
 
 
-def run(kernel, in_specs, out_shapes, out_specs=None, scratch=(), flops=0, moved=0):
+def run(kernel, in_specs, out_shapes, out_specs=None, scratch=(), moved=0, aliases={}):
     return pl.pallas_call(
         kernel,
         in_specs=in_specs,
         out_shape=out_shapes,
         out_specs=out_specs if out_specs is not None else [VMEM] * len(out_shapes),
         scratch_shapes=list(scratch),
+        input_output_aliases=aliases,
         compiler_params=pltpu.CompilerParams(vmem_limit_bytes=24 * 2**20),
-        cost_estimate=pl.CostEstimate(flops=flops, bytes_accessed=moved, transcendentals=0),
+        cost_estimate=pl.CostEstimate(flops=0, bytes_accessed=moved, transcendentals=0),
     )
 
 
@@ -376,11 +393,19 @@
     in_d = across(to_d, 1, 1, 1)
     in_x = across(to_x, 1, 1, 0)
     in_y = across(to_y, 1, 0, 1)
-    new, current = run(nesterov_kernel, [VMEM] * 10, [moment, whole], moved=2**20)(
-        plan, mom_other, mom_x, mom_y, grads_other, in_d, in_x, in_y, own, mom
-    )
+    base, held = run(ready_kernel, [VMEM] * 7, [piece, moment], moved=2**20)(
+        plan, mom_other, mom_x, mom_y, grads_other, own, mom
+    )
+    new, current, scale = run(
+        nesterov_kernel,
+        [VMEM] * 5,
+        [moment, whole, jax.ShapeDtypeStruct((8, 128), f32)],
+        moved=2**20,
+    )(base, held, in_d, in_x, in_y)
     new_l = swap_cores(new)
-    (current,) = run(functools.partial(middle_kernel, 2), [VMEM], [whole], moved=2**20)(current)
+    (current,) = run(functools.partial(middle_kernel, 2), [VMEM] * 2, [whole], moved=2**20)(
+        scale, current
+    )
     new_l, current = lax.optimization_barrier((new_l, current))
     new = jnp.where(lax.axis_index("dp") % 2 == 0, new, new_l)
     back = both_ways(new)
@@ -393,14 +418,24 @@
     up_l = swap_cores(mine)
     back_in = swap_cores(back)
     over_d, over_x, over_y = swap_cores(up_d), swap_cores(up_x), swap_cores(up_y)
+    whole_updates = jax.ShapeDtypeStruct((mats, half, width), bf16)
+    (updates,) = run(
+        early_kernel,
+        [VMEM] * 5,
+        [whole_updates],
+        out_specs=[ANY],
+        scratch=[pltpu.SemaphoreType.DMA((2,))],
+        moved=2**19,
+    )(plan, up_d, up_l, over_d, mine)
     updates, new_momentum = run(
         finish_kernel,
-        [VMEM] * 13,
-        [jax.ShapeDtypeStruct((mats, half, width), bf16), jax.ShapeDtypeStruct(momentum.shape, bf16)],
+        [VMEM] * 9 + [ANY],
+        [whole_updates, jax.ShapeDtypeStruct(momentum.shape, bf16)],
         out_specs=[ANY, ANY],
-        scratch=[pltpu.SemaphoreType.DMA((5,))],
+        scratch=[pltpu.SemaphoreType.DMA((3,))],
         moved=2**20,
-    )(plan, faded, new, back, back_in, up_d, up_x, up_y, up_l, over_d, over_x, over_y, mine)
+        aliases={9: 0},
+    )(plan, faded, new, back, back_in, up_x, up_y, over_x, over_y, updates)
     return (updates, new_momentum)
 
 

time: 30.5 us -> 29.9 us (0.980)
  waiting for transfers between devices: 9.34 us -> 8.49 us
  Pallas kernels: 7.83 us -> 8.21 us
    ppermute x8, waiting for transfers between devices: 1.02 us -> 0.25 us  [swap_cores(): return lax.ppermute(value, AXES, pairs)]
    pallas_call x3 -> x5, Pallas kernels: 3.54 us -> 4.01 us  [the longest x1 1.99 us: per_device_chips(): run(functools.partial(middle_kernel, 2), [VMEM] * 2, [whole], moved=2 ** 20)]
  transfers between devices with their start and end apart: 17 -> 17, of which waited for: 8 -> 7; matrix products, arithmetic and copies ran while one was open for 0% -> 0% of each run, Pallas kernels for 21% -> 24%
where the time goes in v5:
time: 29.9 us; the launch traced here: 29.8 us
  starting transfers between devices  12.3 us (41%)
  waiting for transfers between devices  8.49 us (28%)
  Pallas kernels  8.21 us (27%)
  between operations  0.73 us (2%)
    ppermute x8, starting transfers between devices, across(): return lax.ppermute(value, AXES, pairs)  7.43 us
    ppermute x8, waiting for transfers between devices, across(): return lax.ppermute(value, AXES, pairs)  7.25 us
    ppermute x8, starting transfers between devices, swap_cores(): return lax.ppermute(value, AXES, pairs)  4.1 us
    pallas_call x1, Pallas kernels, per_device_chips(): run(functools.partial(last_kernel, ITERS - 2), [VMEM], [update, update],...  2.85 us
    pallas_call x1, Pallas kernels, per_device_chips(): run(functools.partial(middle_kernel, 2), [VMEM] * 2, [whole], moved=2 ** 20)  1.99 us
    pallas_call x1, Pallas kernels, per_device_chips(): run(load_kernel, [ANY] * 3, [near, moment, moment, table], scratch=[pltpu...  1.34 us
    ppermute x1, waiting for transfers between devices, both_ways(): return lax.ppermute(value, AXES, pairs)  0.99 us
    pallas_call x1, Pallas kernels, per_device_chips(): run(finish_kernel, [VMEM] * 9 + [ANY], [whole_updates, jax.ShapeDtypeStru...  0.85 us
  transfers between devices with their start and end apart: 17, of which 7 were waited for; matrix products, arithmetic and copies ran while one was open for 0% of the time, Pallas kernels for 24%

profile of v5, /device:TPU:0, one launch (start us, length us, event | category | flops | bytes accessed | tf_op | source)
XLA Modules:
  0.0 29.8 jit_solution(337166922856306029)
XLA Ops:
  0.6 0.5 %collective-permute-start = (bf16[1,256,512]{2,1,0:T(8,128)(2,1)}, bf16[1,256,512]{2,1,0:T(8,128)(2,1)S(1)}, u32[]{:S(2)}, u32[]{:S(2)}) collective-permute-start(bf16[1,256,512]{2,1,0:T(8,128)(2,1)} %momentum.1), channel_id=1, source_target_pairs={{0,8},{8,0},{1,9},{9,1},{16,24},{24,16},{17,25},{25,17},{2,10},{10... | collective-permute-start | bytes 786440 | tf_op jit(solution)/shard_map/ppermute | solution.py:333
  1.2 1.3 %shard_map.50 = (f32[4,128,512]{2,1,0:T(8,128)S(1)}, bf16[256,512]{1,0:T(8,128)(2,1)S(1)}, bf16[256,512]{1,0:T(8,128)(2,1)S(1)}, s32[8,128]{1,0:T(8,128)S(1)}) custom-call(f32[1,4,128,512]{3,2,1,0:T(8,128)} %grads.1, bf16[1,256,512]{2,1,0:T(8,128)(2,1)} %momentum.1, s32[4]{0:T(128)} %slots.1), custom_call_target="tpu_custom_call" | custom-call | bytes 2097152 | tf_op jit(solution)/shard_map/pallas_call | solution.py:378
  2.5 0.4 %collective-permute-start.3 = (f32[1,4,128,512]{3,2,1,0:T(8,128)S(1)}, f32[1,4,128,512]{3,2,1,0:T(8,128)S(1)}, u32[]{:S(2)}, u32[]{:S(2)}) collective-permute-start(f32[1,4,128,512]{3,2,1,0:T(8,128)S(1)} %copy-done), channel_id=1, source_target_pairs={{0,8},{8,0},{1,9},{9,1},{16,24},{24,16},{17,25},{25,17},{2,10},{10... | collective-permute-start | bytes 3145736 | tf_op jit(solution)/shard_map/ppermute | solution.py:333
  2.9 0.3 %collective-permute-start.1 = (bf16[256,512]{1,0:T(8,128)(2,1)S(1)}, bf16[256,512]{1,0:T(8,128)(2,1)S(1)}, u32[]{:S(2)}, u32[]{:S(2)}) collective-permute-start(bf16[256,512]{1,0:T(8,128)(2,1)S(1)} %shard_map.51), channel_id=1, source_target_pairs={{8,16},{9,17},{24,0},{25,1},{0,8},{1,9},{16,24},{17,25},{10,18},{1... | collective-permute-start | bytes 786440 | tf_op jit(solution)/shard_map/ppermute | solution.py:342
  3.2 2.5 %collective-permute-start.2 = (bf16[256,512]{1,0:T(8,128)(2,1)S(1)}, bf16[256,512]{1,0:T(8,128)(2,1)S(1)}, u32[]{:S(2)}, u32[]{:S(2)}) collective-permute-start(bf16[256,512]{1,0:T(8,128)(2,1)S(1)} %shard_map.51), channel_id=1, source_target_pairs={{8,1},{9,0},{24,17},{25,16},{0,8},{1,9},{16,24},{17,25},{10,3},{11... | collective-permute-start | bytes 786440 | tf_op jit(solution)/shard_map/ppermute | solution.py:342
  5.7 0.6 %collective-permute-start.4 = (f32[128,512]{1,0:T(8,128)S(1)}, f32[128,512]{1,0:T(8,128)S(1)}, u32[]{:S(2)}, u32[]{:S(2)}) collective-permute-start(f32[128,512]{1,0:T(8,128)S(1)} %get-tuple-element.30), channel_id=1, source_target_pairs={{8,17},{9,16},{24,1},{25,0},{0,8},{1,9},{16,24},{17,25},{10,19},{1... | collective-permute-start | bytes 786440 | tf_op jit(solution)/shard_map/ppermute | solution.py:342
  6.3 2.8 %collective-permute-start.5 = (f32[128,512]{1,0:T(8,128)S(1)}, f32[128,512]{1,0:T(8,128)S(1)}, u32[]{:S(2)}, u32[]{:S(2)}) collective-permute-start(f32[128,512]{1,0:T(8,128)S(1)} %get-tuple-element.31), channel_id=1, source_target_pairs={{8,16},{9,17},{24,0},{25,1},{0,8},{1,9},{16,24},{17,25},{10,18},{1... | collective-permute-start | bytes 786440 | tf_op jit(solution)/shard_map/ppermute | solution.py:342
  9.1 0.6 %collective-permute-done.1.mom_x = bf16[256,512]{1,0:T(8,128)(2,1)S(1)} collective-permute-done((bf16[256,512]{1,0:T(8,128)(2,1)S(1)}, bf16[256,512]{1,0:T(8,128)(2,1)S(1)}, u32[]{:S(2)}, u32[]{:S(2)}) %collective-permute-start.1) | collective-permute-done | bytes 262176 | tf_op jit(solution)/shard_map/ppermute | solution.py:342
  9.7 1.2 %collective-permute-done.2.mom_y = bf16[256,512]{1,0:T(8,128)(2,1)S(1)} collective-permute-done((bf16[256,512]{1,0:T(8,128)(2,1)S(1)}, bf16[256,512]{1,0:T(8,128)(2,1)S(1)}, u32[]{:S(2)}, u32[]{:S(2)}) %collective-permute-start.2) | collective-permute-done | bytes 262176 | tf_op jit(solution)/shard_map/ppermute | solution.py:342
  11.0 2.7 %collective-permute-done.4.in_d = f32[128,512]{1,0:T(8,128)S(1)} collective-permute-done((f32[128,512]{1,0:T(8,128)S(1)}, f32[128,512]{1,0:T(8,128)S(1)}, u32[]{:S(2)}, u32[]{:S(2)}) %collective-permute-start.4) | collective-permute-done | bytes 262176 | tf_op jit(solution)/shard_map/ppermute | solution.py:342
  13.8 2.4 %collective-permute-done.5.in_x = f32[128,512]{1,0:T(8,128)S(1)} collective-permute-done((f32[128,512]{1,0:T(8,128)S(1)}, f32[128,512]{1,0:T(8,128)S(1)}, u32[]{:S(2)}, u32[]{:S(2)}) %collective-permute-start.5) | collective-permute-done | bytes 262176 | tf_op jit(solution)/shard_map/ppermute | solution.py:342
  16.2 0.3 %collective-permute-done.6.in_y = f32[128,512]{1,0:T(8,128)S(1)} collective-permute-done((f32[128,512]{1,0:T(8,128)S(1)}, f32[128,512]{1,0:T(8,128)S(1)}, u32[]{:S(2)}, u32[]{:S(2)}) %collective-permute-start.6) | collective-permute-done | bytes 262176 | tf_op jit(solution)/shard_map/ppermute | solution.py:342
  16.5 0.3 %shard_map.54 = (bf16[256,512]{1,0:T(8,128)(2,1)S(1)}, f32[256,512]{1,0:T(8,128)S(1)}, f32[8,128]{1,0:T(8,128)S(1)}) custom-call(f32[128,512]{1,0:T(8,128)S(1)} %get-tuple-element.28.base, bf16[256,512]{1,0:T(8,128)(2,1)S(1)} %get-tuple-element.29.held, f32[128,512]{1,0:T(8,128)S(1)} %collective-permute-done.4.in_d, ...), custom_call_target="tpu_custom_call" | custom-call | bytes 1048576 | tf_op jit(solution)/shard_map/pallas_call | solution.py:399
  16.8 2.0 %shard_map.55.start = f32[256,512]{1,0:T(8,128)S(1)} custom-call(f32[8,128]{1,0:T(8,128)S(1)} %get-tuple-element.34.scale, f32[256,512]{1,0:T(8,128)S(1)} %get-tuple-element.35.before), custom_call_target="tpu_custom_call" | custom-call | bytes 1048576 | tf_op jit(solution)/shard_map/pallas_call | solution.py:406
  18.9 0.8 %collective-permute-start.8 = (bf16[256,512]{1,0:T(8,128)(2,1)S(1)}, bf16[256,512]{1,0:T(8,128)(2,1)S(1)}, u32[]{:S(2)}, u32[]{:S(2)}) collective-permute-start(bf16[256,512]{1,0:T(8,128)(2,1)S(1)} %broadcast_select_fusion.new), channel_id=1, source_target_pairs={{0,24},{1,25},{16,8},{17,9},{8,1},{9,0},{24,17},{25,16},{2,26},{3,... | collective-permute-start | bytes 786440 | tf_op jit(solution)/shard_map/ppermute | solution.py:348
  19.6 2.9 %shard_map.56 = (bf16[128,512]{1,0:T(8,128)(2,1)S(1)}, bf16[128,512]{1,0:T(8,128)(2,1)S(1)}) custom-call(f32[256,512]{1,0:T(8,128)S(1)} %shard_map.55.start), custom_call_target="tpu_custom_call" | custom-call | bytes 1048576 | tf_op jit(solution)/shard_map/pallas_call | solution.py:412
  22.6 0.9 %collective-permute-start.10 = (bf16[128,512]{1,0:T(8,128)(2,1)S(1)}, bf16[128,512]{1,0:T(8,128)(2,1)S(1)}, u32[]{:S(2)}, u32[]{:S(2)}) collective-permute-start(bf16[128,512]{1,0:T(8,128)(2,1)S(1)} %get-tuple-element.38.mine), channel_id=1, source_target_pairs={{0,24},{1,25},{16,8},{17,9},{8,0},{9,1},{24,16},{25,17},{2,26},{3,... | collective-permute-start | bytes 393224 | tf_op jit(solution)/shard_map/ppermute | solution.py:342
  23.7 1.0 %collective-permute-done.8.back = bf16[256,512]{1,0:T(8,128)(2,1)S(1)} collective-permute-done((bf16[256,512]{1,0:T(8,128)(2,1)S(1)}, bf16[256,512]{1,0:T(8,128)(2,1)S(1)}, u32[]{:S(2)}, u32[]{:S(2)}) %collective-permute-start.8) | collective-permute-done | bytes 262176 | tf_op jit(solution)/shard_map/ppermute | solution.py:348
  24.8 0.4 %collective-permute-start.15 = (bf16[128,512]{1,0:T(8,128)(2,1)S(1)}, bf16[128,512]{1,0:T(8,128)(2,1)S(1)}, u32[]{:S(2)}, u32[]{:S(2)}) collective-permute-start(bf16[128,512]{1,0:T(8,128)(2,1)S(1)} %get-tuple-element.38.mine), channel_id=1, source_target_pairs={{0,8},{8,0},{1,9},{9,1},{16,24},{24,16},{17,25},{25,17},{2,10},{10... | collective-permute-start | bytes 393224 | tf_op jit(solution)/shard_map/ppermute | solution.py:333
  25.2 1.3 %collective-permute-start.16 = (bf16[128,512]{1,0:T(8,128)(2,1)S(1)}, bf16[128,512]{1,0:T(8,128)(2,1)S(1)}, u32[]{:S(2)}, u32[]{:S(2)}) collective-permute-start(bf16[128,512]{1,0:T(8,128)(2,1)S(1)} %collective-permute-done.14.up_d), channel_id=1, source_target_pairs={{0,8},{8,0},{1,9},{9,1},{16,24},{24,16},{17,25},{25,17},{2,10},{10... | collective-permute-start | bytes 393224 | tf_op jit(solution)/shard_map/ppermute | solution.py:333
  26.6 0.9 %collective-permute-start.12 = (bf16[128,512]{1,0:T(8,128)(2,1)S(1)}, bf16[128,512]{1,0:T(8,128)(2,1)S(1)}, u32[]{:S(2)}, u32[]{:S(2)}) collective-permute-start(bf16[128,512]{1,0:T(8,128)(2,1)S(1)} %collective-permute-done.10.up_x), channel_id=1, source_target_pairs={{0,8},{8,0},{1,9},{9,1},{16,24},{24,16},{17,25},{25,17},{2,10},{10... | collective-permute-start | bytes 393224 | tf_op jit(solution)/shard_map/ppermute | solution.py:333
  27.5 0.4 %collective-permute-start.13 = (bf16[128,512]{1,0:T(8,128)(2,1)S(1)}, bf16[128,512]{1,0:T(8,128)(2,1)S(1)}, u32[]{:S(2)}, u32[]{:S(2)}) collective-permute-start(bf16[128,512]{1,0:T(8,128)(2,1)S(1)} %collective-permute-done.11.up_y), channel_id=1, source_target_pairs={{0,8},{8,0},{1,9},{9,1},{16,24},{24,16},{17,25},{25,17},{2,10},{10... | collective-permute-start | bytes 393224 | tf_op jit(solution)/shard_map/ppermute | solution.py:333
  27.9 0.8 %shard_map.57._ = bf16[4,128,512]{2,1,0:T(8,128)(2,1)} custom-call(s32[8,128]{1,0:T(8,128)S(1)} %get-tuple-element.22.plan, bf16[128,512]{1,0:T(8,128)(2,1)S(1)} %collective-permute-done.14.up_d, bf16[128,512]{1,0:T(8,128)(2,1)S(1)} %collective-permute-done.15.up_l, bf16[128,512]{1,0:T(8,128)(2,1)S(1)} %collective-permute-done.16.in_d, ...), custom_call_target="tpu_custom_call" | custom-call | bytes 524288 | tf_op jit(solution)/shard_map/pallas_call | solution.py:422
  28.9 0.8 %shard_map.58 = (bf16[4,128,512]{2,1,0:T(8,128)(2,1)}, bf16[1,256,512]{2,1,0:T(8,128)(2,1)}) custom-call(s32[8,128]{1,0:T(8,128)S(1)} %get-tuple-element.22.plan, bf16[256,512]{1,0:T(8,128)(2,1)S(1)} %get-tuple-element.23.faded, bf16[256,512]{1,0:T(8,128)(2,1)S(1)} %broadcast_select_fusion.new, ...), custom_call_target="tpu_custom_call", output_to_operand_aliasing={{0}: (9, {})} | custom-call | bytes 1048576 | tf_op jit(solution)/shard_map/pallas_call | solution.py:430
  (22 shorter events, 0.9 us)
Async XLA Ops:
  0.6 1.9 %copy-start = (f32[1,4,128,512]{3,2,1,0:T(8,128)S(1)}, f32[1,4,128,512]{3,2,1,0:T(8,128)}, u32[]{:S(2)}) copy-start(f32[1,4,128,512]{3,2,1,0:T(8,128)} %grads.1) | copy-start | bytes 3145732
  0.6 1.9 %collective-permute-start = (bf16[1,256,512]{2,1,0:T(8,128)(2,1)}, bf16[1,256,512]{2,1,0:T(8,128)(2,1)S(1)}, u32[]{:S(2)}, u32[]{:S(2)}) collective-permute-start(bf16[1,256,512]{2,1,0:T(8,128)(2,1)} %momentum.1), channel_id=1, source_target_pairs={{0,8},{8,0},{1,9},{9,1},{16,24},{24,16},{17,25},{25,17},{2,10},{10... | collective-permute-start | bytes 786440 | tf_op jit(solution)/shard_map/ppermute | solution.py:333
  2.5 3.2 %collective-permute-start.3 = (f32[1,4,128,512]{3,2,1,0:T(8,128)S(1)}, f32[1,4,128,512]{3,2,1,0:T(8,128)S(1)}, u32[]{:S(2)}, u32[]{:S(2)}) collective-permute-start(f32[1,4,128,512]{3,2,1,0:T(8,128)S(1)} %copy-done), channel_id=1, source_target_pairs={{0,8},{8,0},{1,9},{9,1},{16,24},{24,16},{17,25},{25,17},{2,10},{10... | collective-permute-start | bytes 3145736 | tf_op jit(solution)/shard_map/ppermute | solution.py:333
  2.9 6.8 %collective-permute-start.1 = (bf16[256,512]{1,0:T(8,128)(2,1)S(1)}, bf16[256,512]{1,0:T(8,128)(2,1)S(1)}, u32[]{:S(2)}, u32[]{:S(2)}) collective-permute-start(bf16[256,512]{1,0:T(8,128)(2,1)S(1)} %shard_map.51), channel_id=1, source_target_pairs={{8,16},{9,17},{24,0},{25,1},{0,8},{1,9},{16,24},{17,25},{10,18},{1... | collective-permute-start | bytes 786440 | tf_op jit(solution)/shard_map/ppermute | solution.py:342
  3.2 7.7 %collective-permute-start.2 = (bf16[256,512]{1,0:T(8,128)(2,1)S(1)}, bf16[256,512]{1,0:T(8,128)(2,1)S(1)}, u32[]{:S(2)}, u32[]{:S(2)}) collective-permute-start(bf16[256,512]{1,0:T(8,128)(2,1)S(1)} %shard_map.51), channel_id=1, source_target_pairs={{8,1},{9,0},{24,17},{25,16},{0,8},{1,9},{16,24},{17,25},{10,3},{11... | collective-permute-start | bytes 786440 | tf_op jit(solution)/shard_map/ppermute | solution.py:342
  5.7 8.1 %collective-permute-start.4 = (f32[128,512]{1,0:T(8,128)S(1)}, f32[128,512]{1,0:T(8,128)S(1)}, u32[]{:S(2)}, u32[]{:S(2)}) collective-permute-start(f32[128,512]{1,0:T(8,128)S(1)} %get-tuple-element.30), channel_id=1, source_target_pairs={{8,17},{9,16},{24,1},{25,0},{0,8},{1,9},{16,24},{17,25},{10,19},{1... | collective-permute-start | bytes 786440 | tf_op jit(solution)/shard_map/ppermute | solution.py:342
  6.3 9.8 %collective-permute-start.5 = (f32[128,512]{1,0:T(8,128)S(1)}, f32[128,512]{1,0:T(8,128)S(1)}, u32[]{:S(2)}, u32[]{:S(2)}) collective-permute-start(f32[128,512]{1,0:T(8,128)S(1)} %get-tuple-element.31), channel_id=1, source_target_pairs={{8,16},{9,17},{24,0},{25,1},{0,8},{1,9},{16,24},{17,25},{10,18},{1... | collective-permute-start | bytes 786440 | tf_op jit(solution)/shard_map/ppermute | solution.py:342
  9.1 7.4 %collective-permute-start.6 = (f32[128,512]{1,0:T(8,128)S(1)}, f32[128,512]{1,0:T(8,128)S(1)}, u32[]{:S(2)}, u32[]{:S(2)}) collective-permute-start(f32[128,512]{1,0:T(8,128)S(1)} %get-tuple-element.32), channel_id=1, source_target_pairs={{8,1},{9,0},{24,17},{25,16},{0,8},{1,9},{16,24},{17,25},{10,3},{11... | collective-permute-start | bytes 786440 | tf_op jit(solution)/shard_map/ppermute | solution.py:342
  16.8 2.0 %collective-permute-start.7 = (bf16[256,512]{1,0:T(8,128)(2,1)S(1)}, bf16[256,512]{1,0:T(8,128)(2,1)S(1)}, u32[]{:S(2)}, u32[]{:S(2)}) collective-permute-start(bf16[256,512]{1,0:T(8,128)(2,1)S(1)} %get-tuple-element.33), channel_id=1, source_target_pairs={{0,8},{8,0},{1,9},{9,1},{16,24},{24,16},{17,25},{25,17},{2,10},{10... | collective-permute-start | bytes 786440 | tf_op jit(solution)/shard_map/ppermute | solution.py:333
  18.9 5.8 %collective-permute-start.8 = (bf16[256,512]{1,0:T(8,128)(2,1)S(1)}, bf16[256,512]{1,0:T(8,128)(2,1)S(1)}, u32[]{:S(2)}, u32[]{:S(2)}) collective-permute-start(bf16[256,512]{1,0:T(8,128)(2,1)S(1)} %broadcast_select_fusion.new), channel_id=1, source_target_pairs={{0,24},{1,25},{16,8},{17,9},{8,1},{9,0},{24,17},{25,16},{2,26},{3,... | collective-permute-start | bytes 786440 | tf_op jit(solution)/shard_map/ppermute | solution.py:348
  22.5 2.7 %collective-permute-start.14 = (bf16[128,512]{1,0:T(8,128)(2,1)S(1)}, bf16[128,512]{1,0:T(8,128)(2,1)S(1)}, u32[]{:S(2)}, u32[]{:S(2)}) collective-permute-start(bf16[128,512]{1,0:T(8,128)(2,1)S(1)} %get-tuple-element.39), channel_id=1, source_target_pairs={{0,25},{1,24},{16,9},{17,8},{8,0},{9,1},{24,16},{25,17},{2,27},{3,... | collective-permute-start | bytes 393224 | tf_op jit(solution)/shard_map/ppermute | solution.py:342
  22.6 4.0 %collective-permute-start.10 = (bf16[128,512]{1,0:T(8,128)(2,1)S(1)}, bf16[128,512]{1,0:T(8,128)(2,1)S(1)}, u32[]{:S(2)}, u32[]{:S(2)}) collective-permute-start(bf16[128,512]{1,0:T(8,128)(2,1)S(1)} %get-tuple-element.38.mine), channel_id=1, source_target_pairs={{0,24},{1,25},{16,8},{17,9},{8,0},{9,1},{24,16},{25,17},{2,26},{3,... | collective-permute-start | bytes 393224 | tf_op jit(solution)/shard_map/ppermute | solution.py:342
  23.4 4.1 %collective-permute-start.11 = (bf16[128,512]{1,0:T(8,128)(2,1)S(1)}, bf16[128,512]{1,0:T(8,128)(2,1)S(1)}, u32[]{:S(2)}, u32[]{:S(2)}) collective-permute-start(bf16[128,512]{1,0:T(8,128)(2,1)S(1)} %get-tuple-element.39), channel_id=1, source_target_pairs={{0,9},{1,8},{16,25},{17,24},{8,0},{9,1},{24,16},{25,17},{2,11},{3,... | collective-permute-start | bytes 393224 | tf_op jit(solution)/shard_map/ppermute | solution.py:342
  24.7 4.2 %collective-permute-start.9 = (bf16[256,512]{1,0:T(8,128)(2,1)S(1)}, bf16[256,512]{1,0:T(8,128)(2,1)S(1)}, u32[]{:S(2)}, u32[]{:S(2)}) collective-permute-start(bf16[256,512]{1,0:T(8,128)(2,1)S(1)} %collective-permute-done.8.back), channel_id=1, source_target_pairs={{0,8},{8,0},{1,9},{9,1},{16,24},{24,16},{17,25},{25,17},{2,10},{10... | collective-permute-start | bytes 786440 | tf_op jit(solution)/shard_map/ppermute | solution.py:333
  24.8 3.1 %collective-permute-start.15 = (bf16[128,512]{1,0:T(8,128)(2,1)S(1)}, bf16[128,512]{1,0:T(8,128)(2,1)S(1)}, u32[]{:S(2)}, u32[]{:S(2)}) collective-permute-start(bf16[128,512]{1,0:T(8,128)(2,1)S(1)} %get-tuple-element.38.mine), channel_id=1, source_target_pairs={{0,8},{8,0},{1,9},{9,1},{16,24},{24,16},{17,25},{25,17},{2,10},{10... | collective-permute-start | bytes 393224 | tf_op jit(solution)/shard_map/ppermute | solution.py:333
  25.2 2.7 %collective-permute-start.16 = (bf16[128,512]{1,0:T(8,128)(2,1)S(1)}, bf16[128,512]{1,0:T(8,128)(2,1)S(1)}, u32[]{:S(2)}, u32[]{:S(2)}) collective-permute-start(bf16[128,512]{1,0:T(8,128)(2,1)S(1)} %collective-permute-done.14.up_d), channel_id=1, source_target_pairs={{0,8},{8,0},{1,9},{9,1},{16,24},{24,16},{17,25},{25,17},{2,10},{10... | collective-permute-start | bytes 393224 | tf_op jit(solution)/shard_map/ppermute | solution.py:333
  26.6 2.1 %collective-permute-start.12 = (bf16[128,512]{1,0:T(8,128)(2,1)S(1)}, bf16[128,512]{1,0:T(8,128)(2,1)S(1)}, u32[]{:S(2)}, u32[]{:S(2)}) collective-permute-start(bf16[128,512]{1,0:T(8,128)(2,1)S(1)} %collective-permute-done.10.up_x), channel_id=1, source_target_pairs={{0,8},{8,0},{1,9},{9,1},{16,24},{24,16},{17,25},{25,17},{2,10},{10... | collective-permute-start | bytes 393224 | tf_op jit(solution)/shard_map/ppermute | solution.py:333
  27.5 1.4 %collective-permute-start.13 = (bf16[128,512]{1,0:T(8,128)(2,1)S(1)}, bf16[128,512]{1,0:T(8,128)(2,1)S(1)}, u32[]{:S(2)}, u32[]{:S(2)}) collective-permute-start(bf16[128,512]{1,0:T(8,128)(2,1)S(1)} %collective-permute-done.11.up_y), channel_id=1, source_target_pairs={{0,8},{8,0},{1,9},{9,1},{16,24},{24,16},{17,25},{25,17},{2,10},{10... | collective-permute-start | bytes 393224 | tf_op jit(solution)/shard_map/ppermute | solution.py:333

commit v6 on v5

--- a/solution.py
+++ b/solution.py
@@ -196,12 +196,21 @@
     return high, (value - high.astype(jnp.float32)).astype(jnp.bfloat16)
 
 
-def polynomial_step(current):
+def gram_of(high, low):
     dot = functools.partial(lax.dot_general, preferred_element_type=jnp.float32)
-    plain, turned = (((1,), (0,)), ((), ())), (((1,), (1,)), ((), ()))
+    turned = (((1,), (1,)), ((), ()))
+    mixed = dot(high, low, turned).astype(jnp.bfloat16)
+    return dot(high, high, turned) + (mixed.astype(jnp.float32) + mixed.T.astype(jnp.float32))
+
+
+def polynomial_step(current, norm=None):
+    dot = functools.partial(lax.dot_general, preferred_element_type=jnp.float32)
+    plain = (((1,), (0,)), ((), ()))
     high, low = parts_of(current)
-    mixed = dot(high, low, turned).astype(jnp.bfloat16)
-    gram = dot(high, high, turned) + (mixed.astype(jnp.float32) + mixed.T.astype(jnp.float32))
+    gram = gram_of(high, low)
+    if norm is not None:
+        inverse = 1.0 / norm
+        gram = gram * (inverse * inverse)
     gram_high, gram_low = parts_of(gram)
     rows = current.shape[0] // 2
     blocks = []
@@ -214,7 +223,8 @@
         change = dot(poly_high, high, plain) + (
             dot(poly_high, low, plain) + dot(poly_low, high, plain)
         )
-        blocks.append(COEF_A * current[block] + change)
+        result = COEF_A * current[block] + change
+        blocks.append(result if norm is None else result * inverse)
     return jnp.concatenate(blocks, axis=0)
 
 
@@ -234,33 +244,31 @@
             )
 
 
-def nesterov_kernel(base, held, in_d, in_x, in_y, new, nesterov, scale):
+def nesterov_kernel(base, held, in_d, in_x, in_y, new, nesterov):
     _, c, y = here()
     half = base.shape[0]
 
     @pl.when(c == 0)
     def _():
-        squares = jnp.zeros((1, base.shape[1]), jnp.float32)
         for part, start in enumerate((y * half, (1 - y) * half)):
             rows = pl.ds(pl.multiple_of(start, half), half)
             local = slice(part * half, (part + 1) * half)
             total = base[...] + in_x[...] if part == 0 else in_y[...] + in_d[...]
             buffer = MOMENT * held[local].astype(jnp.float32) + total
             new[rows] = buffer.astype(jnp.bfloat16)
-            piece = total + MOMENT * buffer
-            nesterov[local] = piece
-            squares = squares + jnp.sum(piece * piece, axis=0, keepdims=True)
+            nesterov[local] = total + MOMENT * buffer
+
+
+def first_kernel(steps, nesterov, after):
+    _, c, _ = here()
+
+    @pl.when(c == 0)
+    def _():
+        value = nesterov[...]
+        squares = jnp.sum(value * value, axis=0, keepdims=True)
         norm = jnp.sqrt(jnp.sum(squares, axis=1, keepdims=True)) + 1e-07
-        scale[...] = jnp.broadcast_to(1.0 / norm, scale.shape)
-
-
-def middle_kernel(steps, scale, before, after):
-    _, c, _ = here()
-
-    @pl.when(c == 0)
-    def _():
-        value = before[...] * scale[0:1, 0:1]
-        for _ in range(steps):
+        value = polynomial_step(value, norm)
+        for _ in range(steps - 1):
             value = polynomial_step(value)
         after[...] = value
 
@@ -396,16 +404,11 @@
     base, held = run(ready_kernel, [VMEM] * 7, [piece, moment], moved=2**20)(
         plan, mom_other, mom_x, mom_y, grads_other, own, mom
     )
-    new, current, scale = run(
-        nesterov_kernel,
-        [VMEM] * 5,
-        [moment, whole, jax.ShapeDtypeStruct((8, 128), f32)],
-        moved=2**20,
-    )(base, held, in_d, in_x, in_y)
+    new, current = run(nesterov_kernel, [VMEM] * 5, [moment, whole], moved=2**20)(
+        base, held, in_d, in_x, in_y
+    )
     new_l = swap_cores(new)
-    (current,) = run(functools.partial(middle_kernel, 2), [VMEM] * 2, [whole], moved=2**20)(
-        scale, current
-    )
+    (current,) = run(functools.partial(first_kernel, 2), [VMEM], [whole], moved=2**20)(current)
     new_l, current = lax.optimization_barrier((new_l, current))
     new = jnp.where(lax.axis_index("dp") % 2 == 0, new, new_l)
     back = both_ways(new)

time: 29.9 us -> 29.8 us (level)
  no operation moved by 1% of the time
where the time goes in v6:
time: 29.8 us; the launch traced here: 29.7 us
  starting transfers between devices  12.4 us (42%)
  waiting for transfers between devices  8.5 us (29%)
  Pallas kernels  8.04 us (27%)
  between operations  0.74 us (2%)
    ppermute x8, starting transfers between devices, across(): return lax.ppermute(value, AXES, pairs)  7.43 us
    ppermute x8, waiting for transfers between devices, across(): return lax.ppermute(value, AXES, pairs)  7.25 us
    ppermute x8, starting transfers between devices, swap_cores(): return lax.ppermute(value, AXES, pairs)  4.15 us
    pallas_call x1, Pallas kernels, per_device_chips(): run(functools.partial(last_kernel, ITERS - 2), [VMEM], [update, update],...  2.85 us
    pallas_call x1, Pallas kernels, per_device_chips(): run(functools.partial(first_kernel, 2), [VMEM], [whole], moved=2 ** 20)  1.98 us
    pallas_call x1, Pallas kernels, per_device_chips(): run(load_kernel, [ANY] * 3, [near, moment, moment, table], scratch=[pltpu...  1.34 us
    ppermute x1, waiting for transfers between devices, both_ways(): return lax.ppermute(value, AXES, pairs)  0.99 us
    pallas_call x1, Pallas kernels, per_device_chips(): run(finish_kernel, [VMEM] * 9 + [ANY], [whole_updates, jax.ShapeDtypeStru...  0.85 us
  transfers between devices with their start and end apart: 17, of which 7 were waited for; matrix products, arithmetic and copies ran while one was open for 0% of the time, Pallas kernels for 24%

profile of v6, /device:TPU:0, one launch (start us, length us, event | category | flops | bytes accessed | tf_op | source)
XLA Modules:
  0.0 29.7 jit_solution(7300393173706667339)
XLA Ops:
  0.6 0.5 %collective-permute-start = (bf16[1,256,512]{2,1,0:T(8,128)(2,1)}, bf16[1,256,512]{2,1,0:T(8,128)(2,1)S(1)}, u32[]{:S(2)}, u32[]{:S(2)}) collective-permute-start(bf16[1,256,512]{2,1,0:T(8,128)(2,1)} %momentum.1), channel_id=1, source_target_pairs={{0,8},{8,0},{1,9},{9,1},{16,24},{24,16},{17,25},{25,17},{2,10},{10... | collective-permute-start | bytes 786440 | tf_op jit(solution)/shard_map/ppermute | solution.py:341
  1.2 1.3 %shard_map.50 = (f32[4,128,512]{2,1,0:T(8,128)S(1)}, bf16[256,512]{1,0:T(8,128)(2,1)S(1)}, bf16[256,512]{1,0:T(8,128)(2,1)S(1)}, s32[8,128]{1,0:T(8,128)S(1)}) custom-call(f32[1,4,128,512]{3,2,1,0:T(8,128)} %grads.1, bf16[1,256,512]{2,1,0:T(8,128)(2,1)} %momentum.1, s32[4]{0:T(128)} %slots.1), custom_call_target="tpu_custom_call" | custom-call | bytes 2097152 | tf_op jit(solution)/shard_map/pallas_call | solution.py:386
  2.5 0.4 %collective-permute-start.3 = (f32[1,4,128,512]{3,2,1,0:T(8,128)S(1)}, f32[1,4,128,512]{3,2,1,0:T(8,128)S(1)}, u32[]{:S(2)}, u32[]{:S(2)}) collective-permute-start(f32[1,4,128,512]{3,2,1,0:T(8,128)S(1)} %copy-done), channel_id=1, source_target_pairs={{0,8},{8,0},{1,9},{9,1},{16,24},{24,16},{17,25},{25,17},{2,10},{10... | collective-permute-start | bytes 3145736 | tf_op jit(solution)/shard_map/ppermute | solution.py:341
  2.9 0.3 %collective-permute-start.1 = (bf16[256,512]{1,0:T(8,128)(2,1)S(1)}, bf16[256,512]{1,0:T(8,128)(2,1)S(1)}, u32[]{:S(2)}, u32[]{:S(2)}) collective-permute-start(bf16[256,512]{1,0:T(8,128)(2,1)S(1)} %shard_map.51), channel_id=1, source_target_pairs={{8,16},{9,17},{24,0},{25,1},{0,8},{1,9},{16,24},{17,25},{10,18},{1... | collective-permute-start | bytes 786440 | tf_op jit(solution)/shard_map/ppermute | solution.py:350
  3.2 2.5 %collective-permute-start.2 = (bf16[256,512]{1,0:T(8,128)(2,1)S(1)}, bf16[256,512]{1,0:T(8,128)(2,1)S(1)}, u32[]{:S(2)}, u32[]{:S(2)}) collective-permute-start(bf16[256,512]{1,0:T(8,128)(2,1)S(1)} %shard_map.51), channel_id=1, source_target_pairs={{8,1},{9,0},{24,17},{25,16},{0,8},{1,9},{16,24},{17,25},{10,3},{11... | collective-permute-start | bytes 786440 | tf_op jit(solution)/shard_map/ppermute | solution.py:350
  5.7 0.6 %collective-permute-start.4 = (f32[128,512]{1,0:T(8,128)S(1)}, f32[128,512]{1,0:T(8,128)S(1)}, u32[]{:S(2)}, u32[]{:S(2)}) collective-permute-start(f32[128,512]{1,0:T(8,128)S(1)} %get-tuple-element.29), channel_id=1, source_target_pairs={{8,17},{9,16},{24,1},{25,0},{0,8},{1,9},{16,24},{17,25},{10,19},{1... | collective-permute-start | bytes 786440 | tf_op jit(solution)/shard_map/ppermute | solution.py:350
  6.3 2.8 %collective-permute-start.5 = (f32[128,512]{1,0:T(8,128)S(1)}, f32[128,512]{1,0:T(8,128)S(1)}, u32[]{:S(2)}, u32[]{:S(2)}) collective-permute-start(f32[128,512]{1,0:T(8,128)S(1)} %get-tuple-element.30), channel_id=1, source_target_pairs={{8,16},{9,17},{24,0},{25,1},{0,8},{1,9},{16,24},{17,25},{10,18},{1... | collective-permute-start | bytes 786440 | tf_op jit(solution)/shard_map/ppermute | solution.py:350
  9.1 0.6 %collective-permute-done.1.mom_x = bf16[256,512]{1,0:T(8,128)(2,1)S(1)} collective-permute-done((bf16[256,512]{1,0:T(8,128)(2,1)S(1)}, bf16[256,512]{1,0:T(8,128)(2,1)S(1)}, u32[]{:S(2)}, u32[]{:S(2)}) %collective-permute-start.1) | collective-permute-done | bytes 262176 | tf_op jit(solution)/shard_map/ppermute | solution.py:350
  9.7 1.2 %collective-permute-done.2.mom_y = bf16[256,512]{1,0:T(8,128)(2,1)S(1)} collective-permute-done((bf16[256,512]{1,0:T(8,128)(2,1)S(1)}, bf16[256,512]{1,0:T(8,128)(2,1)S(1)}, u32[]{:S(2)}, u32[]{:S(2)}) %collective-permute-start.2) | collective-permute-done | bytes 262176 | tf_op jit(solution)/shard_map/ppermute | solution.py:350
  11.0 2.8 %collective-permute-done.4.in_d = f32[128,512]{1,0:T(8,128)S(1)} collective-permute-done((f32[128,512]{1,0:T(8,128)S(1)}, f32[128,512]{1,0:T(8,128)S(1)}, u32[]{:S(2)}, u32[]{:S(2)}) %collective-permute-start.4) | collective-permute-done | bytes 262176 | tf_op jit(solution)/shard_map/ppermute | solution.py:350
  13.8 2.4 %collective-permute-done.5.in_x = f32[128,512]{1,0:T(8,128)S(1)} collective-permute-done((f32[128,512]{1,0:T(8,128)S(1)}, f32[128,512]{1,0:T(8,128)S(1)}, u32[]{:S(2)}, u32[]{:S(2)}) %collective-permute-start.5) | collective-permute-done | bytes 262176 | tf_op jit(solution)/shard_map/ppermute | solution.py:350
  16.2 0.3 %collective-permute-done.6.in_y = f32[128,512]{1,0:T(8,128)S(1)} collective-permute-done((f32[128,512]{1,0:T(8,128)S(1)}, f32[128,512]{1,0:T(8,128)S(1)}, u32[]{:S(2)}, u32[]{:S(2)}) %collective-permute-start.6) | collective-permute-done | bytes 262176 | tf_op jit(solution)/shard_map/ppermute | solution.py:350
  16.7 2.0 %shard_map.55.start = f32[256,512]{1,0:T(8,128)S(1)} custom-call(f32[256,512]{1,0:T(8,128)S(1)} %get-tuple-element.33.nesterov), custom_call_target="tpu_custom_call" | custom-call | bytes 1048576 | tf_op jit(solution)/shard_map/pallas_call | solution.py:411
  18.8 0.8 %collective-permute-start.8 = (bf16[256,512]{1,0:T(8,128)(2,1)S(1)}, bf16[256,512]{1,0:T(8,128)(2,1)S(1)}, u32[]{:S(2)}, u32[]{:S(2)}) collective-permute-start(bf16[256,512]{1,0:T(8,128)(2,1)S(1)} %broadcast_select_fusion.new), channel_id=1, source_target_pairs={{0,24},{1,25},{16,8},{17,9},{8,1},{9,0},{24,17},{25,16},{2,26},{3,... | collective-permute-start | bytes 786440 | tf_op jit(solution)/shard_map/ppermute | solution.py:356
  19.5 2.9 %shard_map.56 = (bf16[128,512]{1,0:T(8,128)(2,1)S(1)}, bf16[128,512]{1,0:T(8,128)(2,1)S(1)}) custom-call(f32[256,512]{1,0:T(8,128)S(1)} %shard_map.55.start), custom_call_target="tpu_custom_call" | custom-call | bytes 1048576 | tf_op jit(solution)/shard_map/pallas_call | solution.py:415
  22.5 0.9 %collective-permute-start.10 = (bf16[128,512]{1,0:T(8,128)(2,1)S(1)}, bf16[128,512]{1,0:T(8,128)(2,1)S(1)}, u32[]{:S(2)}, u32[]{:S(2)}) collective-permute-start(bf16[128,512]{1,0:T(8,128)(2,1)S(1)} %get-tuple-element.36.mine), channel_id=1, source_target_pairs={{0,24},{1,25},{16,8},{17,9},{8,0},{9,1},{24,16},{25,17},{2,26},{3,... | collective-permute-start | bytes 393224 | tf_op jit(solution)/shard_map/ppermute | solution.py:350
  23.3 0.3 collective-permute-start.11
  23.6 1.0 %collective-permute-done.8.back = bf16[256,512]{1,0:T(8,128)(2,1)S(1)} collective-permute-done((bf16[256,512]{1,0:T(8,128)(2,1)S(1)}, bf16[256,512]{1,0:T(8,128)(2,1)S(1)}, u32[]{:S(2)}, u32[]{:S(2)}) %collective-permute-start.8) | collective-permute-done | bytes 262176 | tf_op jit(solution)/shard_map/ppermute | solution.py:356
  24.7 0.4 %collective-permute-start.15 = (bf16[128,512]{1,0:T(8,128)(2,1)S(1)}, bf16[128,512]{1,0:T(8,128)(2,1)S(1)}, u32[]{:S(2)}, u32[]{:S(2)}) collective-permute-start(bf16[128,512]{1,0:T(8,128)(2,1)S(1)} %get-tuple-element.36.mine), channel_id=1, source_target_pairs={{0,8},{8,0},{1,9},{9,1},{16,24},{24,16},{17,25},{25,17},{2,10},{10... | collective-permute-start | bytes 393224 | tf_op jit(solution)/shard_map/ppermute | solution.py:341
  25.1 1.3 %collective-permute-start.16 = (bf16[128,512]{1,0:T(8,128)(2,1)S(1)}, bf16[128,512]{1,0:T(8,128)(2,1)S(1)}, u32[]{:S(2)}, u32[]{:S(2)}) collective-permute-start(bf16[128,512]{1,0:T(8,128)(2,1)S(1)} %collective-permute-done.14.up_d), channel_id=1, source_target_pairs={{0,8},{8,0},{1,9},{9,1},{16,24},{24,16},{17,25},{25,17},{2,10},{10... | collective-permute-start | bytes 393224 | tf_op jit(solution)/shard_map/ppermute | solution.py:341
  26.5 0.9 %collective-permute-start.12 = (bf16[128,512]{1,0:T(8,128)(2,1)S(1)}, bf16[128,512]{1,0:T(8,128)(2,1)S(1)}, u32[]{:S(2)}, u32[]{:S(2)}) collective-permute-start(bf16[128,512]{1,0:T(8,128)(2,1)S(1)} %collective-permute-done.10.up_x), channel_id=1, source_target_pairs={{0,8},{8,0},{1,9},{9,1},{16,24},{24,16},{17,25},{25,17},{2,10},{10... | collective-permute-start | bytes 393224 | tf_op jit(solution)/shard_map/ppermute | solution.py:341
  27.4 0.4 %collective-permute-start.13 = (bf16[128,512]{1,0:T(8,128)(2,1)S(1)}, bf16[128,512]{1,0:T(8,128)(2,1)S(1)}, u32[]{:S(2)}, u32[]{:S(2)}) collective-permute-start(bf16[128,512]{1,0:T(8,128)(2,1)S(1)} %collective-permute-done.11.up_y), channel_id=1, source_target_pairs={{0,8},{8,0},{1,9},{9,1},{16,24},{24,16},{17,25},{25,17},{2,10},{10... | collective-permute-start | bytes 393224 | tf_op jit(solution)/shard_map/ppermute | solution.py:341
  27.8 0.8 %shard_map.57._ = bf16[4,128,512]{2,1,0:T(8,128)(2,1)} custom-call(s32[8,128]{1,0:T(8,128)S(1)} %get-tuple-element.21.plan, bf16[128,512]{1,0:T(8,128)(2,1)S(1)} %collective-permute-done.14.up_d, bf16[128,512]{1,0:T(8,128)(2,1)S(1)} %collective-permute-done.15.up_l, bf16[128,512]{1,0:T(8,128)(2,1)S(1)} %collective-permute-done.16.in_d, ...), custom_call_target="tpu_custom_call" | custom-call | bytes 524288 | tf_op jit(solution)/shard_map/pallas_call | solution.py:425
  28.8 0.8 %shard_map.58 = (bf16[4,128,512]{2,1,0:T(8,128)(2,1)}, bf16[1,256,512]{2,1,0:T(8,128)(2,1)}) custom-call(s32[8,128]{1,0:T(8,128)S(1)} %get-tuple-element.21.plan, bf16[256,512]{1,0:T(8,128)(2,1)S(1)} %get-tuple-element.22.faded, bf16[256,512]{1,0:T(8,128)(2,1)S(1)} %broadcast_select_fusion.new, ...), custom_call_target="tpu_custom_call", output_to_operand_aliasing={{0}: (9, {})} | custom-call | bytes 1048576 | tf_op jit(solution)/shard_map/pallas_call | solution.py:433
  (22 shorter events, 0.8 us)
Async XLA Ops:
  0.6 1.9 %copy-start = (f32[1,4,128,512]{3,2,1,0:T(8,128)S(1)}, f32[1,4,128,512]{3,2,1,0:T(8,128)}, u32[]{:S(2)}) copy-start(f32[1,4,128,512]{3,2,1,0:T(8,128)} %grads.1) | copy-start | bytes 3145732
  0.6 1.9 %collective-permute-start = (bf16[1,256,512]{2,1,0:T(8,128)(2,1)}, bf16[1,256,512]{2,1,0:T(8,128)(2,1)S(1)}, u32[]{:S(2)}, u32[]{:S(2)}) collective-permute-start(bf16[1,256,512]{2,1,0:T(8,128)(2,1)} %momentum.1), channel_id=1, source_target_pairs={{0,8},{8,0},{1,9},{9,1},{16,24},{24,16},{17,25},{25,17},{2,10},{10... | collective-permute-start | bytes 786440 | tf_op jit(solution)/shard_map/ppermute | solution.py:341
  2.5 3.2 %collective-permute-start.3 = (f32[1,4,128,512]{3,2,1,0:T(8,128)S(1)}, f32[1,4,128,512]{3,2,1,0:T(8,128)S(1)}, u32[]{:S(2)}, u32[]{:S(2)}) collective-permute-start(f32[1,4,128,512]{3,2,1,0:T(8,128)S(1)} %copy-done), channel_id=1, source_target_pairs={{0,8},{8,0},{1,9},{9,1},{16,24},{24,16},{17,25},{25,17},{2,10},{10... | collective-permute-start | bytes 3145736 | tf_op jit(solution)/shard_map/ppermute | solution.py:341
  2.9 6.8 %collective-permute-start.1 = (bf16[256,512]{1,0:T(8,128)(2,1)S(1)}, bf16[256,512]{1,0:T(8,128)(2,1)S(1)}, u32[]{:S(2)}, u32[]{:S(2)}) collective-permute-start(bf16[256,512]{1,0:T(8,128)(2,1)S(1)} %shard_map.51), channel_id=1, source_target_pairs={{8,16},{9,17},{24,0},{25,1},{0,8},{1,9},{16,24},{17,25},{10,18},{1... | collective-permute-start | bytes 786440 | tf_op jit(solution)/shard_map/ppermute | solution.py:350
  3.2 7.7 %collective-permute-start.2 = (bf16[256,512]{1,0:T(8,128)(2,1)S(1)}, bf16[256,512]{1,0:T(8,128)(2,1)S(1)}, u32[]{:S(2)}, u32[]{:S(2)}) collective-permute-start(bf16[256,512]{1,0:T(8,128)(2,1)S(1)} %shard_map.51), channel_id=1, source_target_pairs={{8,1},{9,0},{24,17},{25,16},{0,8},{1,9},{16,24},{17,25},{10,3},{11... | collective-permute-start | bytes 786440 | tf_op jit(solution)/shard_map/ppermute | solution.py:350
  5.7 8.1 %collective-permute-start.4 = (f32[128,512]{1,0:T(8,128)S(1)}, f32[128,512]{1,0:T(8,128)S(1)}, u32[]{:S(2)}, u32[]{:S(2)}) collective-permute-start(f32[128,512]{1,0:T(8,128)S(1)} %get-tuple-element.29), channel_id=1, source_target_pairs={{8,17},{9,16},{24,1},{25,0},{0,8},{1,9},{16,24},{17,25},{10,19},{1... | collective-permute-start | bytes 786440 | tf_op jit(solution)/shard_map/ppermute | solution.py:350
  6.3 9.8 %collective-permute-start.5 = (f32[128,512]{1,0:T(8,128)S(1)}, f32[128,512]{1,0:T(8,128)S(1)}, u32[]{:S(2)}, u32[]{:S(2)}) collective-permute-start(f32[128,512]{1,0:T(8,128)S(1)} %get-tuple-element.30), channel_id=1, source_target_pairs={{8,16},{9,17},{24,0},{25,1},{0,8},{1,9},{16,24},{17,25},{10,18},{1... | collective-permute-start | bytes 786440 | tf_op jit(solution)/shard_map/ppermute | solution.py:350
  9.1 7.4 %collective-permute-start.6 = (f32[128,512]{1,0:T(8,128)S(1)}, f32[128,512]{1,0:T(8,128)S(1)}, u32[]{:S(2)}, u32[]{:S(2)}) collective-permute-start(f32[128,512]{1,0:T(8,128)S(1)} %get-tuple-element.31), channel_id=1, source_target_pairs={{8,1},{9,0},{24,17},{25,16},{0,8},{1,9},{16,24},{17,25},{10,3},{11... | collective-permute-start | bytes 786440 | tf_op jit(solution)/shard_map/ppermute | solution.py:350
  16.7 2.1 %collective-permute-start.7 = (bf16[256,512]{1,0:T(8,128)(2,1)S(1)}, bf16[256,512]{1,0:T(8,128)(2,1)S(1)}, u32[]{:S(2)}, u32[]{:S(2)}) collective-permute-start(bf16[256,512]{1,0:T(8,128)(2,1)S(1)} %get-tuple-element.32), channel_id=1, source_target_pairs={{0,8},{8,0},{1,9},{9,1},{16,24},{24,16},{17,25},{25,17},{2,10},{10... | collective-permute-start | bytes 786440 | tf_op jit(solution)/shard_map/ppermute | solution.py:341
  18.8 5.8 %collective-permute-start.8 = (bf16[256,512]{1,0:T(8,128)(2,1)S(1)}, bf16[256,512]{1,0:T(8,128)(2,1)S(1)}, u32[]{:S(2)}, u32[]{:S(2)}) collective-permute-start(bf16[256,512]{1,0:T(8,128)(2,1)S(1)} %broadcast_select_fusion.new), channel_id=1, source_target_pairs={{0,24},{1,25},{16,8},{17,9},{8,1},{9,0},{24,17},{25,16},{2,26},{3,... | collective-permute-start | bytes 786440 | tf_op jit(solution)/shard_map/ppermute | solution.py:356
  22.4 2.7 %collective-permute-start.14 = (bf16[128,512]{1,0:T(8,128)(2,1)S(1)}, bf16[128,512]{1,0:T(8,128)(2,1)S(1)}, u32[]{:S(2)}, u32[]{:S(2)}) collective-permute-start(bf16[128,512]{1,0:T(8,128)(2,1)S(1)} %get-tuple-element.37), channel_id=1, source_target_pairs={{0,25},{1,24},{16,9},{17,8},{8,0},{9,1},{24,16},{25,17},{2,27},{3,... | collective-permute-start | bytes 393224 | tf_op jit(solution)/shard_map/ppermute | solution.py:350
  22.5 4.0 %collective-permute-start.10 = (bf16[128,512]{1,0:T(8,128)(2,1)S(1)}, bf16[128,512]{1,0:T(8,128)(2,1)S(1)}, u32[]{:S(2)}, u32[]{:S(2)}) collective-permute-start(bf16[128,512]{1,0:T(8,128)(2,1)S(1)} %get-tuple-element.36.mine), channel_id=1, source_target_pairs={{0,24},{1,25},{16,8},{17,9},{8,0},{9,1},{24,16},{25,17},{2,26},{3,... | collective-permute-start | bytes 393224 | tf_op jit(solution)/shard_map/ppermute | solution.py:350
  23.3 4.1 %collective-permute-start.11 = (bf16[128,512]{1,0:T(8,128)(2,1)S(1)}, bf16[128,512]{1,0:T(8,128)(2,1)S(1)}, u32[]{:S(2)}, u32[]{:S(2)}) collective-permute-start(bf16[128,512]{1,0:T(8,128)(2,1)S(1)} %get-tuple-element.37), channel_id=1, source_target_pairs={{0,9},{1,8},{16,25},{17,24},{8,0},{9,1},{24,16},{25,17},{2,11},{3,... | collective-permute-start | bytes 393224 | tf_op jit(solution)/shard_map/ppermute | solution.py:350
  24.6 4.2 %collective-permute-start.9 = (bf16[256,512]{1,0:T(8,128)(2,1)S(1)}, bf16[256,512]{1,0:T(8,128)(2,1)S(1)}, u32[]{:S(2)}, u32[]{:S(2)}) collective-permute-start(bf16[256,512]{1,0:T(8,128)(2,1)S(1)} %collective-permute-done.8.back), channel_id=1, source_target_pairs={{0,8},{8,0},{1,9},{9,1},{16,24},{24,16},{17,25},{25,17},{2,10},{10... | collective-permute-start | bytes 786440 | tf_op jit(solution)/shard_map/ppermute | solution.py:341
  24.7 3.1 %collective-permute-start.15 = (bf16[128,512]{1,0:T(8,128)(2,1)S(1)}, bf16[128,512]{1,0:T(8,128)(2,1)S(1)}, u32[]{:S(2)}, u32[]{:S(2)}) collective-permute-start(bf16[128,512]{1,0:T(8,128)(2,1)S(1)} %get-tuple-element.36.mine), channel_id=1, source_target_pairs={{0,8},{8,0},{1,9},{9,1},{16,24},{24,16},{17,25},{25,17},{2,10},{10... | collective-permute-start | bytes 393224 | tf_op jit(solution)/shard_map/ppermute | solution.py:341
  25.1 2.7 %collective-permute-start.16 = (bf16[128,512]{1,0:T(8,128)(2,1)S(1)}, bf16[128,512]{1,0:T(8,128)(2,1)S(1)}, u32[]{:S(2)}, u32[]{:S(2)}) collective-permute-start(bf16[128,512]{1,0:T(8,128)(2,1)S(1)} %collective-permute-done.14.up_d), channel_id=1, source_target_pairs={{0,8},{8,0},{1,9},{9,1},{16,24},{24,16},{17,25},{25,17},{2,10},{10... | collective-permute-start | bytes 393224 | tf_op jit(solution)/shard_map/ppermute | solution.py:341
  26.5 2.1 %collective-permute-start.12 = (bf16[128,512]{1,0:T(8,128)(2,1)S(1)}, bf16[128,512]{1,0:T(8,128)(2,1)S(1)}, u32[]{:S(2)}, u32[]{:S(2)}) collective-permute-start(bf16[128,512]{1,0:T(8,128)(2,1)S(1)} %collective-permute-done.10.up_x), channel_id=1, source_target_pairs={{0,8},{8,0},{1,9},{9,1},{16,24},{24,16},{17,25},{25,17},{2,10},{10... | collective-permute-start | bytes 393224 | tf_op jit(solution)/shard_map/ppermute | solution.py:341
  27.4 1.4 %collective-permute-start.13 = (bf16[128,512]{1,0:T(8,128)(2,1)S(1)}, bf16[128,512]{1,0:T(8,128)(2,1)S(1)}, u32[]{:S(2)}, u32[]{:S(2)}) collective-permute-start(bf16[128,512]{1,0:T(8,128)(2,1)S(1)} %collective-permute-done.11.up_y), channel_id=1, source_target_pairs={{0,8},{8,0},{1,9},{9,1},{16,24},{24,16},{17,25},{25,17},{2,10},{10... | collective-permute-start | bytes 393224 | tf_op jit(solution)/shard_map/ppermute | solution.py:341

commit v7 on v6

--- a/solution.py
+++ b/solution.py
@@ -20,6 +20,7 @@
 FACTOR = 0.2 * math.sqrt(max(R, C))
 
 AXES = ("dp", "fsdp")
+SMEM = pl.BlockSpec(memory_space=pltpu.SMEM)
 VMEM = pl.BlockSpec(memory_space=pltpu.VMEM)
 ANY = pl.BlockSpec(memory_space=pl.ANY)
 
@@ -159,11 +160,8 @@
     entries.append(jnp.where(comes_y, 3, jnp.where(comes_x, 2, jnp.where(at_0, zero, one))))
     entries.append(jnp.where(at_1, one, zero))
     entries.append(jnp.where(mine, one + away, zero))
-    row = lax.broadcasted_iota(jnp.int32, plan.shape, 0)
-    table = jnp.zeros(plan.shape, jnp.int32)
     for k, entry in enumerate(entries):
-        table = jnp.where(row == k, entry, table)
-    plan[...] = table
+        plan[k] = entry
     copies[1].wait()
     faded[...] = (MOMENT * momentum_near[...].astype(jnp.float32)).astype(jnp.bfloat16)
     copies[2].wait()
@@ -177,7 +175,7 @@
 
     @pl.when(c == 1)
     def _():
-        mine = plan[GIVER, 0] == 1
+        mine = plan[GIVER] == 1
         mom_out[...] = jnp.where(mine, mom[...], mom_other[0])
 
 
@@ -187,7 +185,7 @@
     @pl.when(c == 1)
     def _():
         for out, flip in ((to_d, 3), (to_x, 2), (to_y, 1)):
-            m = plan[flip, 0]
+            m = plan[flip]
             out[...] = own[m] + other[0, m]
 
 
@@ -234,8 +232,8 @@
 
     @pl.when(c == 0)
     def _():
-        m = plan[0, 0]
-        source = plan[SOURCE, 0]
+        m = plan[0]
+        source = plan[SOURCE]
         base[...] = own[m] + other[0, m]
         for part, start in enumerate((y * half, (1 - y) * half)):
             rows = pl.ds(pl.multiple_of(start, half), half)
@@ -293,7 +291,7 @@
     @pl.when(c == core)
     def _():
         for k, (flip, source) in enumerate(pieces):
-            pltpu.make_async_copy(source, updates.at[plan[flip, 0]], sems.at[k]).start()
+            pltpu.make_async_copy(source, updates.at[plan[flip]], sems.at[k]).start()
 
 
 def early_kernel(plan, up_d, up_l, in_d, mine, updates, sems):
@@ -309,7 +307,7 @@
     _, c, _ = here()
     place(plan, 0, ((2, in_x), (1, in_y)), updates, sems)
     place(plan, 1, ((2, up_x), (1, up_y)), updates, sems)
-    slot = plan[SLOT, 0]
+    slot = plan[SLOT]
     handed = (slot == 3) & (c == 1)
     for chosen, source in (
         (slot == 0, faded),
@@ -379,7 +377,7 @@
     update = jax.ShapeDtypeStruct((half, width), bf16)
 
     near = jax.ShapeDtypeStruct((mats, half, width), f32)
-    table = jax.ShapeDtypeStruct((8, 128), jnp.int32)
+    table = pltpu.SMEM((8,), jnp.int32)
 
     mom_other = swap_cores(momentum)
     far = functools.partial(pltpu.with_memory_space_constraint, memory_space=pltpu.HBM)
@@ -387,22 +385,24 @@
         load_kernel,
         [ANY] * 3,
         [near, moment, moment, table],
+        out_specs=[VMEM, VMEM, VMEM, SMEM],
         scratch=[pltpu.SMEM((mats,), jnp.int32), pltpu.SemaphoreType.DMA((3,))],
         moved=2**21,
     )(far(grads), far(momentum), far(owner_slot))
+    plan_s = functools.partial(pltpu.with_memory_space_constraint, memory_space=pltpu.SMEM)
     mom_other, plan, grads = lax.optimization_barrier((mom_other, plan, grads))
     grads_other = swap_cores(grads)
-    (mom_out,) = run(give_kernel, [VMEM] * 3, [moment], moved=2**18)(plan, mom, mom_other)
+    (mom_out,) = run(give_kernel, [SMEM] + [VMEM] * 2, [moment], moved=2**18)(plan_s(plan), mom, mom_other)
     mom_x = across(mom_out, 1, 1, 0)
     mom_y = across(mom_out, 1, 0, 1)
-    to_d, to_x, to_y = run(sum_kernel, [VMEM] * 3, [piece, piece, piece], moved=2**20)(
-        plan, own, grads_other
+    to_d, to_x, to_y = run(sum_kernel, [SMEM] + [VMEM] * 2, [piece, piece, piece], moved=2**20)(
+        plan_s(plan), own, grads_other
     )
     in_d = across(to_d, 1, 1, 1)
     in_x = across(to_x, 1, 1, 0)
     in_y = across(to_y, 1, 0, 1)
-    base, held = run(ready_kernel, [VMEM] * 7, [piece, moment], moved=2**20)(
-        plan, mom_other, mom_x, mom_y, grads_other, own, mom
+    base, held = run(ready_kernel, [SMEM] + [VMEM] * 6, [piece, moment], moved=2**20)(
+        plan_s(plan), mom_other, mom_x, mom_y, grads_other, own, mom
     )
     new, current = run(nesterov_kernel, [VMEM] * 5, [moment, whole], moved=2**20)(
         base, held, in_d, in_x, in_y
@@ -424,21 +424,21 @@
     whole_updates = jax.ShapeDtypeStruct((mats, half, width), bf16)
     (updates,) = run(
         early_kernel,
-        [VMEM] * 5,
+        [SMEM] + [VMEM] * 4,
         [whole_updates],
         out_specs=[ANY],
         scratch=[pltpu.SemaphoreType.DMA((2,))],
         moved=2**19,
-    )(plan, up_d, up_l, over_d, mine)
+    )(plan_s(plan), up_d, up_l, over_d, mine)
     updates, new_momentum = run(
         finish_kernel,
-        [VMEM] * 9 + [ANY],
+        [SMEM] + [VMEM] * 8 + [ANY],
         [whole_updates, jax.ShapeDtypeStruct(momentum.shape, bf16)],
         out_specs=[ANY, ANY],
         scratch=[pltpu.SemaphoreType.DMA((3,))],
         moved=2**20,
         aliases={9: 0},
-    )(plan, faded, new, back, back_in, up_x, up_y, over_x, over_y, updates)
+    )(plan_s(plan), faded, new, back, back_in, up_x, up_y, over_x, over_y, updates)
     return (updates, new_momentum)
 
 

time: 29.8 us -> 29.7 us (level)
  no operation moved by 1% of the time
where the time goes in v7:
time: 29.7 us; the launch traced here: 29.6 us
  starting transfers between devices  12.3 us (41%)
  waiting for transfers between devices  8.61 us (29%)
  Pallas kernels  7.91 us (27%)
  between operations  0.75 us (3%)
    ppermute x8, starting transfers between devices, across(): return lax.ppermute(value, AXES, pairs)  7.41 us
    ppermute x8, waiting for transfers between devices, across(): return lax.ppermute(value, AXES, pairs)  7.3 us
    ppermute x8, starting transfers between devices, swap_cores(): return lax.ppermute(value, AXES, pairs)  4.13 us
    pallas_call x1, Pallas kernels, per_device_chips(): run(functools.partial(last_kernel, ITERS - 2), [VMEM], [update, update],...  2.85 us
    pallas_call x1, Pallas kernels, per_device_chips(): run(functools.partial(first_kernel, 2), [VMEM], [whole], moved=2 ** 20)  1.98 us
    pallas_call x1, Pallas kernels, per_device_chips(): run(load_kernel, [ANY] * 3, [near, moment, moment, table], out_specs=[VME...  1.34 us
    ppermute x1, waiting for transfers between devices, both_ways(): return lax.ppermute(value, AXES, pairs)  1.03 us
    pallas_call x1, Pallas kernels, per_device_chips(): run(finish_kernel, [SMEM] + [VMEM] * 8 + [ANY], [whole_updates, jax.Shape...  0.81 us
  transfers between devices with their start and end apart: 17, of which 7 were waited for; matrix products, arithmetic and copies ran while one was open for 0% of the time, Pallas kernels for 24%

profile of v7, /device:TPU:0, one launch (start us, length us, event | category | flops | bytes accessed | tf_op | source)
XLA Modules:
  0.0 29.6 jit_solution(10422649790145390164)
XLA Ops:
  0.6 0.5 %collective-permute-start = (bf16[1,256,512]{2,1,0:T(8,128)(2,1)}, bf16[1,256,512]{2,1,0:T(8,128)(2,1)S(1)}, u32[]{:S(2)}, u32[]{:S(2)}) collective-permute-start(bf16[1,256,512]{2,1,0:T(8,128)(2,1)} %momentum.1), channel_id=1, source_target_pairs={{0,8},{8,0},{1,9},{9,1},{16,24},{24,16},{17,25},{25,17},{2,10},{10... | collective-permute-start | bytes 786440 | tf_op jit(solution)/shard_map/ppermute | solution.py:339
  1.2 1.3 %shard_map.50 = (f32[4,128,512]{2,1,0:T(8,128)S(1)}, bf16[256,512]{1,0:T(8,128)(2,1)S(1)}, bf16[256,512]{1,0:T(8,128)(2,1)S(1)}, s32[8]{0:T(128)S(4)}) custom-call(f32[1,4,128,512]{3,2,1,0:T(8,128)} %grads.1, bf16[1,256,512]{2,1,0:T(8,128)(2,1)} %momentum.1, s32[4]{0:T(128)} %slots.1), custom_call_target="tpu_custom_call" | custom-call | bytes 2097152 | tf_op jit(solution)/shard_map/pallas_call | solution.py:384
  2.5 0.4 %collective-permute-start.3 = (f32[1,4,128,512]{3,2,1,0:T(8,128)S(1)}, f32[1,4,128,512]{3,2,1,0:T(8,128)S(1)}, u32[]{:S(2)}, u32[]{:S(2)}) collective-permute-start(f32[1,4,128,512]{3,2,1,0:T(8,128)S(1)} %copy-done), channel_id=1, source_target_pairs={{0,8},{8,0},{1,9},{9,1},{16,24},{24,16},{17,25},{25,17},{2,10},{10... | collective-permute-start | bytes 3145736 | tf_op jit(solution)/shard_map/ppermute | solution.py:339
  2.9 0.3 collective-permute-start.1
  3.2 2.5 %collective-permute-start.2 = (bf16[256,512]{1,0:T(8,128)(2,1)S(1)}, bf16[256,512]{1,0:T(8,128)(2,1)S(1)}, u32[]{:S(2)}, u32[]{:S(2)}) collective-permute-start(bf16[256,512]{1,0:T(8,128)(2,1)S(1)} %shard_map.51), channel_id=1, source_target_pairs={{8,1},{9,0},{24,17},{25,16},{0,8},{1,9},{16,24},{17,25},{10,3},{11... | collective-permute-start | bytes 786440 | tf_op jit(solution)/shard_map/ppermute | solution.py:348
  5.7 0.6 %collective-permute-start.4 = (f32[128,512]{1,0:T(8,128)S(1)}, f32[128,512]{1,0:T(8,128)S(1)}, u32[]{:S(2)}, u32[]{:S(2)}) collective-permute-start(f32[128,512]{1,0:T(8,128)S(1)} %get-tuple-element.29), channel_id=1, source_target_pairs={{8,17},{9,16},{24,1},{25,0},{0,8},{1,9},{16,24},{17,25},{10,19},{1... | collective-permute-start | bytes 786440 | tf_op jit(solution)/shard_map/ppermute | solution.py:348
  6.3 2.9 %collective-permute-start.5 = (f32[128,512]{1,0:T(8,128)S(1)}, f32[128,512]{1,0:T(8,128)S(1)}, u32[]{:S(2)}, u32[]{:S(2)}) collective-permute-start(f32[128,512]{1,0:T(8,128)S(1)} %get-tuple-element.30), channel_id=1, source_target_pairs={{8,16},{9,17},{24,0},{25,1},{0,8},{1,9},{16,24},{17,25},{10,18},{1... | collective-permute-start | bytes 786440 | tf_op jit(solution)/shard_map/ppermute | solution.py:348
  9.1 0.5 %collective-permute-done.1.mom_x = bf16[256,512]{1,0:T(8,128)(2,1)S(1)} collective-permute-done((bf16[256,512]{1,0:T(8,128)(2,1)S(1)}, bf16[256,512]{1,0:T(8,128)(2,1)S(1)}, u32[]{:S(2)}, u32[]{:S(2)}) %collective-permute-start.1) | collective-permute-done | bytes 262176 | tf_op jit(solution)/shard_map/ppermute | solution.py:348
  9.7 1.2 %collective-permute-done.2.mom_y = bf16[256,512]{1,0:T(8,128)(2,1)S(1)} collective-permute-done((bf16[256,512]{1,0:T(8,128)(2,1)S(1)}, bf16[256,512]{1,0:T(8,128)(2,1)S(1)}, u32[]{:S(2)}, u32[]{:S(2)}) %collective-permute-start.2) | collective-permute-done | bytes 262176 | tf_op jit(solution)/shard_map/ppermute | solution.py:348
  11.0 2.8 %collective-permute-done.4.in_d = f32[128,512]{1,0:T(8,128)S(1)} collective-permute-done((f32[128,512]{1,0:T(8,128)S(1)}, f32[128,512]{1,0:T(8,128)S(1)}, u32[]{:S(2)}, u32[]{:S(2)}) %collective-permute-start.4) | collective-permute-done | bytes 262176 | tf_op jit(solution)/shard_map/ppermute | solution.py:348
  13.8 2.4 %collective-permute-done.5.in_x = f32[128,512]{1,0:T(8,128)S(1)} collective-permute-done((f32[128,512]{1,0:T(8,128)S(1)}, f32[128,512]{1,0:T(8,128)S(1)}, u32[]{:S(2)}, u32[]{:S(2)}) %collective-permute-start.5) | collective-permute-done | bytes 262176 | tf_op jit(solution)/shard_map/ppermute | solution.py:348
  16.2 0.3 %collective-permute-done.6.in_y = f32[128,512]{1,0:T(8,128)S(1)} collective-permute-done((f32[128,512]{1,0:T(8,128)S(1)}, f32[128,512]{1,0:T(8,128)S(1)}, u32[]{:S(2)}, u32[]{:S(2)}) %collective-permute-start.6) | collective-permute-done | bytes 262176 | tf_op jit(solution)/shard_map/ppermute | solution.py:348
  16.7 2.0 %shard_map.55.start = f32[256,512]{1,0:T(8,128)S(1)} custom-call(f32[256,512]{1,0:T(8,128)S(1)} %get-tuple-element.33.nesterov), custom_call_target="tpu_custom_call" | custom-call | bytes 1048576 | tf_op jit(solution)/shard_map/pallas_call | solution.py:411
  18.8 0.8 %collective-permute-start.8 = (bf16[256,512]{1,0:T(8,128)(2,1)S(1)}, bf16[256,512]{1,0:T(8,128)(2,1)S(1)}, u32[]{:S(2)}, u32[]{:S(2)}) collective-permute-start(bf16[256,512]{1,0:T(8,128)(2,1)S(1)} %broadcast_select_fusion.new), channel_id=1, source_target_pairs={{0,24},{1,25},{16,8},{17,9},{8,1},{9,0},{24,17},{25,16},{2,26},{3,... | collective-permute-start | bytes 786440 | tf_op jit(solution)/shard_map/ppermute | solution.py:354
  19.5 2.9 %shard_map.56 = (bf16[128,512]{1,0:T(8,128)(2,1)S(1)}, bf16[128,512]{1,0:T(8,128)(2,1)S(1)}) custom-call(f32[256,512]{1,0:T(8,128)S(1)} %shard_map.55.start), custom_call_target="tpu_custom_call" | custom-call | bytes 1048576 | tf_op jit(solution)/shard_map/pallas_call | solution.py:415
  22.4 0.9 %collective-permute-start.10 = (bf16[128,512]{1,0:T(8,128)(2,1)S(1)}, bf16[128,512]{1,0:T(8,128)(2,1)S(1)}, u32[]{:S(2)}, u32[]{:S(2)}) collective-permute-start(bf16[128,512]{1,0:T(8,128)(2,1)S(1)} %get-tuple-element.36.mine), channel_id=1, source_target_pairs={{0,24},{1,25},{16,8},{17,9},{8,0},{9,1},{24,16},{25,17},{2,26},{3,... | collective-permute-start | bytes 393224 | tf_op jit(solution)/shard_map/ppermute | solution.py:348
  23.3 0.3 collective-permute-start.11
  23.6 1.0 %collective-permute-done.8.back = bf16[256,512]{1,0:T(8,128)(2,1)S(1)} collective-permute-done((bf16[256,512]{1,0:T(8,128)(2,1)S(1)}, bf16[256,512]{1,0:T(8,128)(2,1)S(1)}, u32[]{:S(2)}, u32[]{:S(2)}) %collective-permute-start.8) | collective-permute-done | bytes 262176 | tf_op jit(solution)/shard_map/ppermute | solution.py:354
  24.7 0.4 %collective-permute-start.15 = (bf16[128,512]{1,0:T(8,128)(2,1)S(1)}, bf16[128,512]{1,0:T(8,128)(2,1)S(1)}, u32[]{:S(2)}, u32[]{:S(2)}) collective-permute-start(bf16[128,512]{1,0:T(8,128)(2,1)S(1)} %get-tuple-element.36.mine), channel_id=1, source_target_pairs={{0,8},{8,0},{1,9},{9,1},{16,24},{24,16},{17,25},{25,17},{2,10},{10... | collective-permute-start | bytes 393224 | tf_op jit(solution)/shard_map/ppermute | solution.py:339
  25.1 1.3 %collective-permute-start.16 = (bf16[128,512]{1,0:T(8,128)(2,1)S(1)}, bf16[128,512]{1,0:T(8,128)(2,1)S(1)}, u32[]{:S(2)}, u32[]{:S(2)}) collective-permute-start(bf16[128,512]{1,0:T(8,128)(2,1)S(1)} %collective-permute-done.14.up_d), channel_id=1, source_target_pairs={{0,8},{8,0},{1,9},{9,1},{16,24},{24,16},{17,25},{25,17},{2,10},{10... | collective-permute-start | bytes 393224 | tf_op jit(solution)/shard_map/ppermute | solution.py:339
  26.4 1.0 %collective-permute-start.12 = (bf16[128,512]{1,0:T(8,128)(2,1)S(1)}, bf16[128,512]{1,0:T(8,128)(2,1)S(1)}, u32[]{:S(2)}, u32[]{:S(2)}) collective-permute-start(bf16[128,512]{1,0:T(8,128)(2,1)S(1)} %collective-permute-done.10.up_x), channel_id=1, source_target_pairs={{0,8},{8,0},{1,9},{9,1},{16,24},{24,16},{17,25},{25,17},{2,10},{10... | collective-permute-start | bytes 393224 | tf_op jit(solution)/shard_map/ppermute | solution.py:339
  27.4 0.4 %collective-permute-start.13 = (bf16[128,512]{1,0:T(8,128)(2,1)S(1)}, bf16[128,512]{1,0:T(8,128)(2,1)S(1)}, u32[]{:S(2)}, u32[]{:S(2)}) collective-permute-start(bf16[128,512]{1,0:T(8,128)(2,1)S(1)} %collective-permute-done.11.up_y), channel_id=1, source_target_pairs={{0,8},{8,0},{1,9},{9,1},{16,24},{24,16},{17,25},{25,17},{2,10},{10... | collective-permute-start | bytes 393224 | tf_op jit(solution)/shard_map/ppermute | solution.py:339
  27.8 0.7 %shard_map.57._ = bf16[4,128,512]{2,1,0:T(8,128)(2,1)} custom-call(s32[8]{0:T(128)S(4)} %get-tuple-element.21.plan, bf16[128,512]{1,0:T(8,128)(2,1)S(1)} %collective-permute-done.14.up_d, bf16[128,512]{1,0:T(8,128)(2,1)S(1)} %collective-permute-done.15.up_l, bf16[128,512]{1,0:T(8,128)(2,1)S(1)} %collective-permute-done.16.in_d, ...), custom_call_target="tpu_custom_call" | custom-call | bytes 524288 | tf_op jit(solution)/shard_map/pallas_call | solution.py:425
  28.8 0.8 %shard_map.58 = (bf16[4,128,512]{2,1,0:T(8,128)(2,1)}, bf16[1,256,512]{2,1,0:T(8,128)(2,1)}) custom-call(s32[8]{0:T(128)S(4)} %get-tuple-element.21.plan, bf16[256,512]{1,0:T(8,128)(2,1)S(1)} %get-tuple-element.22.faded, bf16[256,512]{1,0:T(8,128)(2,1)S(1)} %broadcast_select_fusion.new, ...), custom_call_target="tpu_custom_call", output_to_operand_aliasing={{0}: (9, {})} | custom-call | bytes 1048576 | tf_op jit(solution)/shard_map/pallas_call | solution.py:433
  (22 shorter events, 0.8 us)
Async XLA Ops:
  0.6 1.9 %copy-start = (f32[1,4,128,512]{3,2,1,0:T(8,128)S(1)}, f32[1,4,128,512]{3,2,1,0:T(8,128)}, u32[]{:S(2)}) copy-start(f32[1,4,128,512]{3,2,1,0:T(8,128)} %grads.1) | copy-start | bytes 3145732
  0.6 1.9 %collective-permute-start = (bf16[1,256,512]{2,1,0:T(8,128)(2,1)}, bf16[1,256,512]{2,1,0:T(8,128)(2,1)S(1)}, u32[]{:S(2)}, u32[]{:S(2)}) collective-permute-start(bf16[1,256,512]{2,1,0:T(8,128)(2,1)} %momentum.1), channel_id=1, source_target_pairs={{0,8},{8,0},{1,9},{9,1},{16,24},{24,16},{17,25},{25,17},{2,10},{10... | collective-permute-start | bytes 786440 | tf_op jit(solution)/shard_map/ppermute | solution.py:339
  2.5 3.2 %collective-permute-start.3 = (f32[1,4,128,512]{3,2,1,0:T(8,128)S(1)}, f32[1,4,128,512]{3,2,1,0:T(8,128)S(1)}, u32[]{:S(2)}, u32[]{:S(2)}) collective-permute-start(f32[1,4,128,512]{3,2,1,0:T(8,128)S(1)} %copy-done), channel_id=1, source_target_pairs={{0,8},{8,0},{1,9},{9,1},{16,24},{24,16},{17,25},{25,17},{2,10},{10... | collective-permute-start | bytes 3145736 | tf_op jit(solution)/shard_map/ppermute | solution.py:339
  2.9 6.7 %collective-permute-start.1 = (bf16[256,512]{1,0:T(8,128)(2,1)S(1)}, bf16[256,512]{1,0:T(8,128)(2,1)S(1)}, u32[]{:S(2)}, u32[]{:S(2)}) collective-permute-start(bf16[256,512]{1,0:T(8,128)(2,1)S(1)} %shard_map.51), channel_id=1, source_target_pairs={{8,16},{9,17},{24,0},{25,1},{0,8},{1,9},{16,24},{17,25},{10,18},{1... | collective-permute-start | bytes 786440 | tf_op jit(solution)/shard_map/ppermute | solution.py:348
  3.2 7.7 %collective-permute-start.2 = (bf16[256,512]{1,0:T(8,128)(2,1)S(1)}, bf16[256,512]{1,0:T(8,128)(2,1)S(1)}, u32[]{:S(2)}, u32[]{:S(2)}) collective-permute-start(bf16[256,512]{1,0:T(8,128)(2,1)S(1)} %shard_map.51), channel_id=1, source_target_pairs={{8,1},{9,0},{24,17},{25,16},{0,8},{1,9},{16,24},{17,25},{10,3},{11... | collective-permute-start | bytes 786440 | tf_op jit(solution)/shard_map/ppermute | solution.py:348
  5.7 8.1 %collective-permute-start.4 = (f32[128,512]{1,0:T(8,128)S(1)}, f32[128,512]{1,0:T(8,128)S(1)}, u32[]{:S(2)}, u32[]{:S(2)}) collective-permute-start(f32[128,512]{1,0:T(8,128)S(1)} %get-tuple-element.29), channel_id=1, source_target_pairs={{8,17},{9,16},{24,1},{25,0},{0,8},{1,9},{16,24},{17,25},{10,19},{1... | collective-permute-start | bytes 786440 | tf_op jit(solution)/shard_map/ppermute | solution.py:348
  6.3 9.9 %collective-permute-start.5 = (f32[128,512]{1,0:T(8,128)S(1)}, f32[128,512]{1,0:T(8,128)S(1)}, u32[]{:S(2)}, u32[]{:S(2)}) collective-permute-start(f32[128,512]{1,0:T(8,128)S(1)} %get-tuple-element.30), channel_id=1, source_target_pairs={{8,16},{9,17},{24,0},{25,1},{0,8},{1,9},{16,24},{17,25},{10,18},{1... | collective-permute-start | bytes 786440 | tf_op jit(solution)/shard_map/ppermute | solution.py:348
  9.1 7.4 %collective-permute-start.6 = (f32[128,512]{1,0:T(8,128)S(1)}, f32[128,512]{1,0:T(8,128)S(1)}, u32[]{:S(2)}, u32[]{:S(2)}) collective-permute-start(f32[128,512]{1,0:T(8,128)S(1)} %get-tuple-element.31), channel_id=1, source_target_pairs={{8,1},{9,0},{24,17},{25,16},{0,8},{1,9},{16,24},{17,25},{10,3},{11... | collective-permute-start | bytes 786440 | tf_op jit(solution)/shard_map/ppermute | solution.py:348
  16.6 2.1 %collective-permute-start.7 = (bf16[256,512]{1,0:T(8,128)(2,1)S(1)}, bf16[256,512]{1,0:T(8,128)(2,1)S(1)}, u32[]{:S(2)}, u32[]{:S(2)}) collective-permute-start(bf16[256,512]{1,0:T(8,128)(2,1)S(1)} %get-tuple-element.32), channel_id=1, source_target_pairs={{0,8},{8,0},{1,9},{9,1},{16,24},{24,16},{17,25},{25,17},{2,10},{10... | collective-permute-start | bytes 786440 | tf_op jit(solution)/shard_map/ppermute | solution.py:339
  18.8 5.8 %collective-permute-start.8 = (bf16[256,512]{1,0:T(8,128)(2,1)S(1)}, bf16[256,512]{1,0:T(8,128)(2,1)S(1)}, u32[]{:S(2)}, u32[]{:S(2)}) collective-permute-start(bf16[256,512]{1,0:T(8,128)(2,1)S(1)} %broadcast_select_fusion.new), channel_id=1, source_target_pairs={{0,24},{1,25},{16,8},{17,9},{8,1},{9,0},{24,17},{25,16},{2,26},{3,... | collective-permute-start | bytes 786440 | tf_op jit(solution)/shard_map/ppermute | solution.py:354
  22.4 2.7 %collective-permute-start.14 = (bf16[128,512]{1,0:T(8,128)(2,1)S(1)}, bf16[128,512]{1,0:T(8,128)(2,1)S(1)}, u32[]{:S(2)}, u32[]{:S(2)}) collective-permute-start(bf16[128,512]{1,0:T(8,128)(2,1)S(1)} %get-tuple-element.37), channel_id=1, source_target_pairs={{0,25},{1,24},{16,9},{17,8},{8,0},{9,1},{24,16},{25,17},{2,27},{3,... | collective-permute-start | bytes 393224 | tf_op jit(solution)/shard_map/ppermute | solution.py:348
  22.4 4.0 %collective-permute-start.10 = (bf16[128,512]{1,0:T(8,128)(2,1)S(1)}, bf16[128,512]{1,0:T(8,128)(2,1)S(1)}, u32[]{:S(2)}, u32[]{:S(2)}) collective-permute-start(bf16[128,512]{1,0:T(8,128)(2,1)S(1)} %get-tuple-element.36.mine), channel_id=1, source_target_pairs={{0,24},{1,25},{16,8},{17,9},{8,0},{9,1},{24,16},{25,17},{2,26},{3,... | collective-permute-start | bytes 393224 | tf_op jit(solution)/shard_map/ppermute | solution.py:348
  23.3 4.1 %collective-permute-start.11 = (bf16[128,512]{1,0:T(8,128)(2,1)S(1)}, bf16[128,512]{1,0:T(8,128)(2,1)S(1)}, u32[]{:S(2)}, u32[]{:S(2)}) collective-permute-start(bf16[128,512]{1,0:T(8,128)(2,1)S(1)} %get-tuple-element.37), channel_id=1, source_target_pairs={{0,9},{1,8},{16,25},{17,24},{8,0},{9,1},{24,16},{25,17},{2,11},{3,... | collective-permute-start | bytes 393224 | tf_op jit(solution)/shard_map/ppermute | solution.py:348
  24.6 4.2 %collective-permute-start.9 = (bf16[256,512]{1,0:T(8,128)(2,1)S(1)}, bf16[256,512]{1,0:T(8,128)(2,1)S(1)}, u32[]{:S(2)}, u32[]{:S(2)}) collective-permute-start(bf16[256,512]{1,0:T(8,128)(2,1)S(1)} %collective-permute-done.8.back), channel_id=1, source_target_pairs={{0,8},{8,0},{1,9},{9,1},{16,24},{24,16},{17,25},{25,17},{2,10},{10... | collective-permute-start | bytes 786440 | tf_op jit(solution)/shard_map/ppermute | solution.py:339
  24.7 3.1 %collective-permute-start.15 = (bf16[128,512]{1,0:T(8,128)(2,1)S(1)}, bf16[128,512]{1,0:T(8,128)(2,1)S(1)}, u32[]{:S(2)}, u32[]{:S(2)}) collective-permute-start(bf16[128,512]{1,0:T(8,128)(2,1)S(1)} %get-tuple-element.36.mine), channel_id=1, source_target_pairs={{0,8},{8,0},{1,9},{9,1},{16,24},{24,16},{17,25},{25,17},{2,10},{10... | collective-permute-start | bytes 393224 | tf_op jit(solution)/shard_map/ppermute | solution.py:339
  25.1 2.7 %collective-permute-start.16 = (bf16[128,512]{1,0:T(8,128)(2,1)S(1)}, bf16[128,512]{1,0:T(8,128)(2,1)S(1)}, u32[]{:S(2)}, u32[]{:S(2)}) collective-permute-start(bf16[128,512]{1,0:T(8,128)(2,1)S(1)} %collective-permute-done.14.up_d), channel_id=1, source_target_pairs={{0,8},{8,0},{1,9},{9,1},{16,24},{24,16},{17,25},{25,17},{2,10},{10... | collective-permute-start | bytes 393224 | tf_op jit(solution)/shard_map/ppermute | solution.py:339
  26.4 2.1 %collective-permute-start.12 = (bf16[128,512]{1,0:T(8,128)(2,1)S(1)}, bf16[128,512]{1,0:T(8,128)(2,1)S(1)}, u32[]{:S(2)}, u32[]{:S(2)}) collective-permute-start(bf16[128,512]{1,0:T(8,128)(2,1)S(1)} %collective-permute-done.10.up_x), channel_id=1, source_target_pairs={{0,8},{8,0},{1,9},{9,1},{16,24},{24,16},{17,25},{25,17},{2,10},{10... | collective-permute-start | bytes 393224 | tf_op jit(solution)/shard_map/ppermute | solution.py:339
  27.4 1.4 %collective-permute-start.13 = (bf16[128,512]{1,0:T(8,128)(2,1)S(1)}, bf16[128,512]{1,0:T(8,128)(2,1)S(1)}, u32[]{:S(2)}, u32[]{:S(2)}) collective-permute-start(bf16[128,512]{1,0:T(8,128)(2,1)S(1)} %collective-permute-done.11.up_y), channel_id=1, source_target_pairs={{0,8},{8,0},{1,9},{9,1},{16,24},{24,16},{17,25},{25,17},{2,10},{10... | collective-permute-start | bytes 393224 | tf_op jit(solution)/shard_map/ppermute | solution.py:339

commit v8 on v7

--- a/solution.py
+++ b/solution.py
@@ -186,7 +186,7 @@
     def _():
         for out, flip in ((to_d, 3), (to_x, 2), (to_y, 1)):
             m = plan[flip]
-            out[...] = own[m] + other[0, m]
+            out[...] = own[m] + other[m]
 
 
 def parts_of(value):
@@ -197,8 +197,9 @@
 def gram_of(high, low):
     dot = functools.partial(lax.dot_general, preferred_element_type=jnp.float32)
     turned = (((1,), (1,)), ((), ()))
+    main = dot(high, high, turned)
     mixed = dot(high, low, turned).astype(jnp.bfloat16)
-    return dot(high, high, turned) + (mixed.astype(jnp.float32) + mixed.T.astype(jnp.float32))
+    return main + (mixed.astype(jnp.float32) + mixed.T.astype(jnp.float32))
 
 
 def polynomial_step(current, norm=None):
@@ -234,7 +235,7 @@
     def _():
         m = plan[0]
         source = plan[SOURCE]
-        base[...] = own[m] + other[0, m]
+        base[...] = own[m] + other[m]
         for part, start in enumerate((y * half, (1 - y) * half)):
             rows = pl.ds(pl.multiple_of(start, half), half)
             held[part * half : (part + 1) * half] = pick(
@@ -390,8 +391,8 @@
         moved=2**21,
     )(far(grads), far(momentum), far(owner_slot))
     plan_s = functools.partial(pltpu.with_memory_space_constraint, memory_space=pltpu.SMEM)
-    mom_other, plan, grads = lax.optimization_barrier((mom_other, plan, grads))
-    grads_other = swap_cores(grads)
+    mom_other, plan, own = lax.optimization_barrier((mom_other, plan, own))
+    grads_other = swap_cores(own)
     (mom_out,) = run(give_kernel, [SMEM] + [VMEM] * 2, [moment], moved=2**18)(plan_s(plan), mom, mom_other)
     mom_x = across(mom_out, 1, 1, 0)
     mom_y = across(mom_out, 1, 0, 1)

time: 29.7 us -> 29.7 us (level)
  transfers between devices with their start and end apart: 17 -> 17, of which waited for: 7 -> 7; matrix products, arithmetic and copies ran while one was open for 0% -> 0% of each run, Pallas kernels for 24% -> 23%
where the time goes in v8:
time: 29.7 us; the launch traced here: 29.6 us
  starting transfers between devices  12.3 us (41%)
  waiting for transfers between devices  8.59 us (29%)
  Pallas kernels  7.9 us (27%)
  between operations  0.74 us (2%)
    ppermute x8, starting transfers between devices, across(): return lax.ppermute(value, AXES, pairs)  7.41 us
    ppermute x8, waiting for transfers between devices, across(): return lax.ppermute(value, AXES, pairs)  7.29 us
    ppermute x8, starting transfers between devices, swap_cores(): return lax.ppermute(value, AXES, pairs)  4.14 us
    pallas_call x1, Pallas kernels, per_device_chips(): run(functools.partial(last_kernel, ITERS - 2), [VMEM], [update, update],...  2.85 us
    pallas_call x1, Pallas kernels, per_device_chips(): run(functools.partial(first_kernel, 2), [VMEM], [whole], moved=2 ** 20)  1.97 us
    pallas_call x1, Pallas kernels, per_device_chips(): run(load_kernel, [ANY] * 3, [near, moment, moment, table], out_specs=[VME...  1.34 us
    ppermute x1, waiting for transfers between devices, both_ways(): return lax.ppermute(value, AXES, pairs)  1.02 us
    pallas_call x1, Pallas kernels, per_device_chips(): run(finish_kernel, [SMEM] + [VMEM] * 8 + [ANY], [whole_updates, jax.Shape...  0.81 us
  transfers between devices with their start and end apart: 17, of which 7 were waited for; matrix products, arithmetic and copies ran while one was open for 0% of the time, Pallas kernels for 23%

profile of v8, /device:TPU:0, one launch (start us, length us, event | category | flops | bytes accessed | tf_op | source)
XLA Modules:
  0.0 29.6 jit_solution(709473085744762572)
XLA Ops:
  0.6 0.5 %collective-permute-start = (bf16[1,256,512]{2,1,0:T(8,128)(2,1)}, bf16[1,256,512]{2,1,0:T(8,128)(2,1)S(1)}, u32[]{:S(2)}, u32[]{:S(2)}) collective-permute-start(bf16[1,256,512]{2,1,0:T(8,128)(2,1)} %momentum.1), channel_id=1, source_target_pairs={{0,8},{8,0},{1,9},{9,1},{16,24},{24,16},{17,25},{25,17},{2,10},{10... | collective-permute-start | bytes 786440 | tf_op jit(solution)/shard_map/ppermute | solution.py:340
  1.1 1.3 %shard_map.50 = (f32[4,128,512]{2,1,0:T(8,128)S(1)}, bf16[256,512]{1,0:T(8,128)(2,1)S(1)}, bf16[256,512]{1,0:T(8,128)(2,1)S(1)}, s32[8]{0:T(128)S(4)}) custom-call(f32[1,4,128,512]{3,2,1,0:T(8,128)} %grads.1, bf16[1,256,512]{2,1,0:T(8,128)(2,1)} %momentum.1, s32[4]{0:T(128)} %slots.1), custom_call_target="tpu_custom_call" | custom-call | bytes 2097152 | tf_op jit(solution)/shard_map/pallas_call | solution.py:385
  2.5 0.4 %collective-permute-start.3 = (f32[4,128,512]{2,1,0:T(8,128)S(1)}, f32[4,128,512]{2,1,0:T(8,128)S(1)}, u32[]{:S(2)}, u32[]{:S(2)}) collective-permute-start(f32[4,128,512]{2,1,0:T(8,128)S(1)} %get-tuple-element.26.own), channel_id=1, source_target_pairs={{0,8},{8,0},{1,9},{9,1},{16,24},{24,16},{17,25},{25,17},{2,10},{10... | collective-permute-start | bytes 3145736 | tf_op jit(solution)/shard_map/ppermute | solution.py:340
  2.9 0.3 collective-permute-start.1
  3.2 2.5 %collective-permute-start.2 = (bf16[256,512]{1,0:T(8,128)(2,1)S(1)}, bf16[256,512]{1,0:T(8,128)(2,1)S(1)}, u32[]{:S(2)}, u32[]{:S(2)}) collective-permute-start(bf16[256,512]{1,0:T(8,128)(2,1)S(1)} %shard_map.51), channel_id=1, source_target_pairs={{8,1},{9,0},{24,17},{25,16},{0,8},{1,9},{16,24},{17,25},{10,3},{11... | collective-permute-start | bytes 786440 | tf_op jit(solution)/shard_map/ppermute | solution.py:349
  5.7 0.6 %collective-permute-start.4 = (f32[128,512]{1,0:T(8,128)S(1)}, f32[128,512]{1,0:T(8,128)S(1)}, u32[]{:S(2)}, u32[]{:S(2)}) collective-permute-start(f32[128,512]{1,0:T(8,128)S(1)} %get-tuple-element.29), channel_id=1, source_target_pairs={{8,17},{9,16},{24,1},{25,0},{0,8},{1,9},{16,24},{17,25},{10,19},{1... | collective-permute-start | bytes 786440 | tf_op jit(solution)/shard_map/ppermute | solution.py:349
  6.3 2.9 %collective-permute-start.5 = (f32[128,512]{1,0:T(8,128)S(1)}, f32[128,512]{1,0:T(8,128)S(1)}, u32[]{:S(2)}, u32[]{:S(2)}) collective-permute-start(f32[128,512]{1,0:T(8,128)S(1)} %get-tuple-element.30), channel_id=1, source_target_pairs={{8,16},{9,17},{24,0},{25,1},{0,8},{1,9},{16,24},{17,25},{10,18},{1... | collective-permute-start | bytes 786440 | tf_op jit(solution)/shard_map/ppermute | solution.py:349
  9.1 0.5 %collective-permute-done.1.mom_x = bf16[256,512]{1,0:T(8,128)(2,1)S(1)} collective-permute-done((bf16[256,512]{1,0:T(8,128)(2,1)S(1)}, bf16[256,512]{1,0:T(8,128)(2,1)S(1)}, u32[]{:S(2)}, u32[]{:S(2)}) %collective-permute-start.1) | collective-permute-done | bytes 262176 | tf_op jit(solution)/shard_map/ppermute | solution.py:349
  9.6 1.2 %collective-permute-done.2.mom_y = bf16[256,512]{1,0:T(8,128)(2,1)S(1)} collective-permute-done((bf16[256,512]{1,0:T(8,128)(2,1)S(1)}, bf16[256,512]{1,0:T(8,128)(2,1)S(1)}, u32[]{:S(2)}, u32[]{:S(2)}) %collective-permute-start.2) | collective-permute-done | bytes 262176 | tf_op jit(solution)/shard_map/ppermute | solution.py:349
  11.0 2.8 %collective-permute-done.4.in_d = f32[128,512]{1,0:T(8,128)S(1)} collective-permute-done((f32[128,512]{1,0:T(8,128)S(1)}, f32[128,512]{1,0:T(8,128)S(1)}, u32[]{:S(2)}, u32[]{:S(2)}) %collective-permute-start.4) | collective-permute-done | bytes 262176 | tf_op jit(solution)/shard_map/ppermute | solution.py:349
  13.7 2.4 %collective-permute-done.5.in_x = f32[128,512]{1,0:T(8,128)S(1)} collective-permute-done((f32[128,512]{1,0:T(8,128)S(1)}, f32[128,512]{1,0:T(8,128)S(1)}, u32[]{:S(2)}, u32[]{:S(2)}) %collective-permute-start.5) | collective-permute-done | bytes 262176 | tf_op jit(solution)/shard_map/ppermute | solution.py:349
  16.2 0.3 %collective-permute-done.6.in_y = f32[128,512]{1,0:T(8,128)S(1)} collective-permute-done((f32[128,512]{1,0:T(8,128)S(1)}, f32[128,512]{1,0:T(8,128)S(1)}, u32[]{:S(2)}, u32[]{:S(2)}) %collective-permute-start.6) | collective-permute-done | bytes 262176 | tf_op jit(solution)/shard_map/ppermute | solution.py:349
  16.7 2.0 %shard_map.55.start = f32[256,512]{1,0:T(8,128)S(1)} custom-call(f32[256,512]{1,0:T(8,128)S(1)} %get-tuple-element.33.nesterov), custom_call_target="tpu_custom_call" | custom-call | bytes 1048576 | tf_op jit(solution)/shard_map/pallas_call | solution.py:412
  18.7 0.8 %collective-permute-start.8 = (bf16[256,512]{1,0:T(8,128)(2,1)S(1)}, bf16[256,512]{1,0:T(8,128)(2,1)S(1)}, u32[]{:S(2)}, u32[]{:S(2)}) collective-permute-start(bf16[256,512]{1,0:T(8,128)(2,1)S(1)} %broadcast_select_fusion.new), channel_id=1, source_target_pairs={{0,24},{1,25},{16,8},{17,9},{8,1},{9,0},{24,17},{25,16},{2,26},{3,... | collective-permute-start | bytes 786440 | tf_op jit(solution)/shard_map/ppermute | solution.py:355
  19.5 2.9 %shard_map.56 = (bf16[128,512]{1,0:T(8,128)(2,1)S(1)}, bf16[128,512]{1,0:T(8,128)(2,1)S(1)}) custom-call(f32[256,512]{1,0:T(8,128)S(1)} %shard_map.55.start), custom_call_target="tpu_custom_call" | custom-call | bytes 1048576 | tf_op jit(solution)/shard_map/pallas_call | solution.py:416
  22.4 0.9 %collective-permute-start.10 = (bf16[128,512]{1,0:T(8,128)(2,1)S(1)}, bf16[128,512]{1,0:T(8,128)(2,1)S(1)}, u32[]{:S(2)}, u32[]{:S(2)}) collective-permute-start(bf16[128,512]{1,0:T(8,128)(2,1)S(1)} %get-tuple-element.36.mine), channel_id=1, source_target_pairs={{0,24},{1,25},{16,8},{17,9},{8,0},{9,1},{24,16},{25,17},{2,26},{3,... | collective-permute-start | bytes 393224 | tf_op jit(solution)/shard_map/ppermute | solution.py:349
  23.3 0.3 collective-permute-start.11
  23.6 1.0 %collective-permute-done.8.back = bf16[256,512]{1,0:T(8,128)(2,1)S(1)} collective-permute-done((bf16[256,512]{1,0:T(8,128)(2,1)S(1)}, bf16[256,512]{1,0:T(8,128)(2,1)S(1)}, u32[]{:S(2)}, u32[]{:S(2)}) %collective-permute-start.8) | collective-permute-done | bytes 262176 | tf_op jit(solution)/shard_map/ppermute | solution.py:355
  24.7 0.4 %collective-permute-start.15 = (bf16[128,512]{1,0:T(8,128)(2,1)S(1)}, bf16[128,512]{1,0:T(8,128)(2,1)S(1)}, u32[]{:S(2)}, u32[]{:S(2)}) collective-permute-start(bf16[128,512]{1,0:T(8,128)(2,1)S(1)} %get-tuple-element.36.mine), channel_id=1, source_target_pairs={{0,8},{8,0},{1,9},{9,1},{16,24},{24,16},{17,25},{25,17},{2,10},{10... | collective-permute-start | bytes 393224 | tf_op jit(solution)/shard_map/ppermute | solution.py:340
  25.1 1.3 %collective-permute-start.16 = (bf16[128,512]{1,0:T(8,128)(2,1)S(1)}, bf16[128,512]{1,0:T(8,128)(2,1)S(1)}, u32[]{:S(2)}, u32[]{:S(2)}) collective-permute-start(bf16[128,512]{1,0:T(8,128)(2,1)S(1)} %collective-permute-done.14.up_d), channel_id=1, source_target_pairs={{0,8},{8,0},{1,9},{9,1},{16,24},{24,16},{17,25},{25,17},{2,10},{10... | collective-permute-start | bytes 393224 | tf_op jit(solution)/shard_map/ppermute | solution.py:340
  26.4 1.0 %collective-permute-start.12 = (bf16[128,512]{1,0:T(8,128)(2,1)S(1)}, bf16[128,512]{1,0:T(8,128)(2,1)S(1)}, u32[]{:S(2)}, u32[]{:S(2)}) collective-permute-start(bf16[128,512]{1,0:T(8,128)(2,1)S(1)} %collective-permute-done.10.up_x), channel_id=1, source_target_pairs={{0,8},{8,0},{1,9},{9,1},{16,24},{24,16},{17,25},{25,17},{2,10},{10... | collective-permute-start | bytes 393224 | tf_op jit(solution)/shard_map/ppermute | solution.py:340
  27.4 0.4 %collective-permute-start.13 = (bf16[128,512]{1,0:T(8,128)(2,1)S(1)}, bf16[128,512]{1,0:T(8,128)(2,1)S(1)}, u32[]{:S(2)}, u32[]{:S(2)}) collective-permute-start(bf16[128,512]{1,0:T(8,128)(2,1)S(1)} %collective-permute-done.11.up_y), channel_id=1, source_target_pairs={{0,8},{8,0},{1,9},{9,1},{16,24},{24,16},{17,25},{25,17},{2,10},{10... | collective-permute-start | bytes 393224 | tf_op jit(solution)/shard_map/ppermute | solution.py:340
  27.8 0.7 %shard_map.57._ = bf16[4,128,512]{2,1,0:T(8,128)(2,1)} custom-call(s32[8]{0:T(128)S(4)} %get-tuple-element.22.plan, bf16[128,512]{1,0:T(8,128)(2,1)S(1)} %collective-permute-done.14.up_d, bf16[128,512]{1,0:T(8,128)(2,1)S(1)} %collective-permute-done.15.up_l, bf16[128,512]{1,0:T(8,128)(2,1)S(1)} %collective-permute-done.16.in_d, ...), custom_call_target="tpu_custom_call" | custom-call | bytes 524288 | tf_op jit(solution)/shard_map/pallas_call | solution.py:426
  28.8 0.8 %shard_map.58 = (bf16[4,128,512]{2,1,0:T(8,128)(2,1)}, bf16[1,256,512]{2,1,0:T(8,128)(2,1)}) custom-call(s32[8]{0:T(128)S(4)} %get-tuple-element.22.plan, bf16[256,512]{1,0:T(8,128)(2,1)S(1)} %get-tuple-element.23.faded, bf16[256,512]{1,0:T(8,128)(2,1)S(1)} %broadcast_select_fusion.new, ...), custom_call_target="tpu_custom_call", output_to_operand_aliasing={{0}: (9, {})} | custom-call | bytes 1048576 | tf_op jit(solution)/shard_map/pallas_call | solution.py:434
  (20 shorter events, 0.8 us)
Async XLA Ops:
  0.6 1.9 %collective-permute-start = (bf16[1,256,512]{2,1,0:T(8,128)(2,1)}, bf16[1,256,512]{2,1,0:T(8,128)(2,1)S(1)}, u32[]{:S(2)}, u32[]{:S(2)}) collective-permute-start(bf16[1,256,512]{2,1,0:T(8,128)(2,1)} %momentum.1), channel_id=1, source_target_pairs={{0,8},{8,0},{1,9},{9,1},{16,24},{24,16},{17,25},{25,17},{2,10},{10... | collective-permute-start | bytes 786440 | tf_op jit(solution)/shard_map/ppermute | solution.py:340
  2.5 3.2 %collective-permute-start.3 = (f32[4,128,512]{2,1,0:T(8,128)S(1)}, f32[4,128,512]{2,1,0:T(8,128)S(1)}, u32[]{:S(2)}, u32[]{:S(2)}) collective-permute-start(f32[4,128,512]{2,1,0:T(8,128)S(1)} %get-tuple-element.26.own), channel_id=1, source_target_pairs={{0,8},{8,0},{1,9},{9,1},{16,24},{24,16},{17,25},{25,17},{2,10},{10... | collective-permute-start | bytes 3145736 | tf_op jit(solution)/shard_map/ppermute | solution.py:340
  2.9 6.7 %collective-permute-start.1 = (bf16[256,512]{1,0:T(8,128)(2,1)S(1)}, bf16[256,512]{1,0:T(8,128)(2,1)S(1)}, u32[]{:S(2)}, u32[]{:S(2)}) collective-permute-start(bf16[256,512]{1,0:T(8,128)(2,1)S(1)} %shard_map.51), channel_id=1, source_target_pairs={{8,16},{9,17},{24,0},{25,1},{0,8},{1,9},{16,24},{17,25},{10,18},{1... | collective-permute-start | bytes 786440 | tf_op jit(solution)/shard_map/ppermute | solution.py:349
  3.2 7.7 %collective-permute-start.2 = (bf16[256,512]{1,0:T(8,128)(2,1)S(1)}, bf16[256,512]{1,0:T(8,128)(2,1)S(1)}, u32[]{:S(2)}, u32[]{:S(2)}) collective-permute-start(bf16[256,512]{1,0:T(8,128)(2,1)S(1)} %shard_map.51), channel_id=1, source_target_pairs={{8,1},{9,0},{24,17},{25,16},{0,8},{1,9},{16,24},{17,25},{10,3},{11... | collective-permute-start | bytes 786440 | tf_op jit(solution)/shard_map/ppermute | solution.py:349
  5.7 8.1 %collective-permute-start.4 = (f32[128,512]{1,0:T(8,128)S(1)}, f32[128,512]{1,0:T(8,128)S(1)}, u32[]{:S(2)}, u32[]{:S(2)}) collective-permute-start(f32[128,512]{1,0:T(8,128)S(1)} %get-tuple-element.29), channel_id=1, source_target_pairs={{8,17},{9,16},{24,1},{25,0},{0,8},{1,9},{16,24},{17,25},{10,19},{1... | collective-permute-start | bytes 786440 | tf_op jit(solution)/shard_map/ppermute | solution.py:349
  6.3 9.9 %collective-permute-start.5 = (f32[128,512]{1,0:T(8,128)S(1)}, f32[128,512]{1,0:T(8,128)S(1)}, u32[]{:S(2)}, u32[]{:S(2)}) collective-permute-start(f32[128,512]{1,0:T(8,128)S(1)} %get-tuple-element.30), channel_id=1, source_target_pairs={{8,16},{9,17},{24,0},{25,1},{0,8},{1,9},{16,24},{17,25},{10,18},{1... | collective-permute-start | bytes 786440 | tf_op jit(solution)/shard_map/ppermute | solution.py:349
  9.1 7.4 %collective-permute-start.6 = (f32[128,512]{1,0:T(8,128)S(1)}, f32[128,512]{1,0:T(8,128)S(1)}, u32[]{:S(2)}, u32[]{:S(2)}) collective-permute-start(f32[128,512]{1,0:T(8,128)S(1)} %get-tuple-element.31), channel_id=1, source_target_pairs={{8,1},{9,0},{24,17},{25,16},{0,8},{1,9},{16,24},{17,25},{10,3},{11... | collective-permute-start | bytes 786440 | tf_op jit(solution)/shard_map/ppermute | solution.py:349
  16.6 2.1 %collective-permute-start.7 = (bf16[256,512]{1,0:T(8,128)(2,1)S(1)}, bf16[256,512]{1,0:T(8,128)(2,1)S(1)}, u32[]{:S(2)}, u32[]{:S(2)}) collective-permute-start(bf16[256,512]{1,0:T(8,128)(2,1)S(1)} %get-tuple-element.32), channel_id=1, source_target_pairs={{0,8},{8,0},{1,9},{9,1},{16,24},{24,16},{17,25},{25,17},{2,10},{10... | collective-permute-start | bytes 786440 | tf_op jit(solution)/shard_map/ppermute | solution.py:340
  18.7 5.8 %collective-permute-start.8 = (bf16[256,512]{1,0:T(8,128)(2,1)S(1)}, bf16[256,512]{1,0:T(8,128)(2,1)S(1)}, u32[]{:S(2)}, u32[]{:S(2)}) collective-permute-start(bf16[256,512]{1,0:T(8,128)(2,1)S(1)} %broadcast_select_fusion.new), channel_id=1, source_target_pairs={{0,24},{1,25},{16,8},{17,9},{8,1},{9,0},{24,17},{25,16},{2,26},{3,... | collective-permute-start | bytes 786440 | tf_op jit(solution)/shard_map/ppermute | solution.py:355
  22.4 2.7 %collective-permute-start.14 = (bf16[128,512]{1,0:T(8,128)(2,1)S(1)}, bf16[128,512]{1,0:T(8,128)(2,1)S(1)}, u32[]{:S(2)}, u32[]{:S(2)}) collective-permute-start(bf16[128,512]{1,0:T(8,128)(2,1)S(1)} %get-tuple-element.37), channel_id=1, source_target_pairs={{0,25},{1,24},{16,9},{17,8},{8,0},{9,1},{24,16},{25,17},{2,27},{3,... | collective-permute-start | bytes 393224 | tf_op jit(solution)/shard_map/ppermute | solution.py:349
  22.4 4.0 %collective-permute-start.10 = (bf16[128,512]{1,0:T(8,128)(2,1)S(1)}, bf16[128,512]{1,0:T(8,128)(2,1)S(1)}, u32[]{:S(2)}, u32[]{:S(2)}) collective-permute-start(bf16[128,512]{1,0:T(8,128)(2,1)S(1)} %get-tuple-element.36.mine), channel_id=1, source_target_pairs={{0,24},{1,25},{16,8},{17,9},{8,0},{9,1},{24,16},{25,17},{2,26},{3,... | collective-permute-start | bytes 393224 | tf_op jit(solution)/shard_map/ppermute | solution.py:349
  23.3 4.1 %collective-permute-start.11 = (bf16[128,512]{1,0:T(8,128)(2,1)S(1)}, bf16[128,512]{1,0:T(8,128)(2,1)S(1)}, u32[]{:S(2)}, u32[]{:S(2)}) collective-permute-start(bf16[128,512]{1,0:T(8,128)(2,1)S(1)} %get-tuple-element.37), channel_id=1, source_target_pairs={{0,9},{1,8},{16,25},{17,24},{8,0},{9,1},{24,16},{25,17},{2,11},{3,... | collective-permute-start | bytes 393224 | tf_op jit(solution)/shard_map/ppermute | solution.py:349
  24.6 4.2 %collective-permute-start.9 = (bf16[256,512]{1,0:T(8,128)(2,1)S(1)}, bf16[256,512]{1,0:T(8,128)(2,1)S(1)}, u32[]{:S(2)}, u32[]{:S(2)}) collective-permute-start(bf16[256,512]{1,0:T(8,128)(2,1)S(1)} %collective-permute-done.8.back), channel_id=1, source_target_pairs={{0,8},{8,0},{1,9},{9,1},{16,24},{24,16},{17,25},{25,17},{2,10},{10... | collective-permute-start | bytes 786440 | tf_op jit(solution)/shard_map/ppermute | solution.py:340
  24.7 3.1 %collective-permute-start.15 = (bf16[128,512]{1,0:T(8,128)(2,1)S(1)}, bf16[128,512]{1,0:T(8,128)(2,1)S(1)}, u32[]{:S(2)}, u32[]{:S(2)}) collective-permute-start(bf16[128,512]{1,0:T(8,128)(2,1)S(1)} %get-tuple-element.36.mine), channel_id=1, source_target_pairs={{0,8},{8,0},{1,9},{9,1},{16,24},{24,16},{17,25},{25,17},{2,10},{10... | collective-permute-start | bytes 393224 | tf_op jit(solution)/shard_map/ppermute | solution.py:340
  25.1 2.7 %collective-permute-start.16 = (bf16[128,512]{1,0:T(8,128)(2,1)S(1)}, bf16[128,512]{1,0:T(8,128)(2,1)S(1)}, u32[]{:S(2)}, u32[]{:S(2)}) collective-permute-start(bf16[128,512]{1,0:T(8,128)(2,1)S(1)} %collective-permute-done.14.up_d), channel_id=1, source_target_pairs={{0,8},{8,0},{1,9},{9,1},{16,24},{24,16},{17,25},{25,17},{2,10},{10... | collective-permute-start | bytes 393224 | tf_op jit(solution)/shard_map/ppermute | solution.py:340
  26.4 2.1 %collective-permute-start.12 = (bf16[128,512]{1,0:T(8,128)(2,1)S(1)}, bf16[128,512]{1,0:T(8,128)(2,1)S(1)}, u32[]{:S(2)}, u32[]{:S(2)}) collective-permute-start(bf16[128,512]{1,0:T(8,128)(2,1)S(1)} %collective-permute-done.10.up_x), channel_id=1, source_target_pairs={{0,8},{8,0},{1,9},{9,1},{16,24},{24,16},{17,25},{25,17},{2,10},{10... | collective-permute-start | bytes 393224 | tf_op jit(solution)/shard_map/ppermute | solution.py:340
  27.4 1.4 %collective-permute-start.13 = (bf16[128,512]{1,0:T(8,128)(2,1)S(1)}, bf16[128,512]{1,0:T(8,128)(2,1)S(1)}, u32[]{:S(2)}, u32[]{:S(2)}) collective-permute-start(bf16[128,512]{1,0:T(8,128)(2,1)S(1)} %collective-permute-done.11.up_y), channel_id=1, source_target_pairs={{0,8},{8,0},{1,9},{9,1},{16,24},{24,16},{17,25},{25,17},{2,10},{10... | collective-permute-start | bytes 393224 | tf_op jit(solution)/shard_map/ppermute | solution.py:340

commit v9 on v8

--- a/solution.py
+++ b/solution.py
@@ -394,7 +394,7 @@
     mom_other, plan, own = lax.optimization_barrier((mom_other, plan, own))
     grads_other = swap_cores(own)
     (mom_out,) = run(give_kernel, [SMEM] + [VMEM] * 2, [moment], moved=2**18)(plan_s(plan), mom, mom_other)
-    mom_x = across(mom_out, 1, 1, 0)
+    mom_x = across(mom, 1, 1, 0)
     mom_y = across(mom_out, 1, 0, 1)
     to_d, to_x, to_y = run(sum_kernel, [SMEM] + [VMEM] * 2, [piece, piece, piece], moved=2**20)(
         plan_s(plan), own, grads_other

time: 29.7 us -> 29.7 us (level)
  starting transfers between devices: 12.3 us -> 12 us
  waiting for transfers between devices: 8.59 us -> 8.89 us
  transfers between devices with their start and end apart: 17 -> 17, of which waited for: 7 -> 6; matrix products, arithmetic and copies ran while one was open for 0% -> 0% of each run, Pallas kernels for 23% -> 24%
where the time goes in v9:
time: 29.7 us; the launch traced here: 29.5 us
  starting transfers between devices  12 us (40%)
  waiting for transfers between devices  8.89 us (30%)
  Pallas kernels  7.89 us (27%)
  between operations  0.74 us (2%)
    ppermute x8, waiting for transfers between devices, across(): return lax.ppermute(value, AXES, pairs)  7.37 us
    ppermute x8, starting transfers between devices, across(): return lax.ppermute(value, AXES, pairs)  7.33 us
    ppermute x8, starting transfers between devices, swap_cores(): return lax.ppermute(value, AXES, pairs)  3.97 us
    pallas_call x1, Pallas kernels, per_device_chips(): run(functools.partial(last_kernel, ITERS - 2), [VMEM], [update, update],...  2.85 us
    pallas_call x1, Pallas kernels, per_device_chips(): run(functools.partial(first_kernel, 2), [VMEM], [whole], moved=2 ** 20)  1.97 us
    pallas_call x1, Pallas kernels, per_device_chips(): run(load_kernel, [ANY] * 3, [near, moment, moment, table], out_specs=[VME...  1.34 us
    ppermute x1, waiting for transfers between devices, both_ways(): return lax.ppermute(value, AXES, pairs)  1.19 us
    pallas_call x1, Pallas kernels, per_device_chips(): run(finish_kernel, [SMEM] + [VMEM] * 8 + [ANY], [whole_updates, jax.Shape...  0.81 us
  transfers between devices with their start and end apart: 17, of which 6 were waited for; matrix products, arithmetic and copies ran while one was open for 0% of the time, Pallas kernels for 24%

profile of v9, /device:TPU:0, one launch (start us, length us, event | category | flops | bytes accessed | tf_op | source)
XLA Modules:
  0.0 29.5 jit_solution(7963945298163868713)
XLA Ops:
  0.6 0.5 %collective-permute-start = (bf16[1,256,512]{2,1,0:T(8,128)(2,1)}, bf16[1,256,512]{2,1,0:T(8,128)(2,1)S(1)}, u32[]{:S(2)}, u32[]{:S(2)}) collective-permute-start(bf16[1,256,512]{2,1,0:T(8,128)(2,1)} %momentum.1), channel_id=1, source_target_pairs={{0,8},{8,0},{1,9},{9,1},{16,24},{24,16},{17,25},{25,17},{2,10},{10... | collective-permute-start | bytes 786440 | tf_op jit(solution)/shard_map/ppermute | solution.py:340
  1.1 1.3 %shard_map.50 = (f32[4,128,512]{2,1,0:T(8,128)S(1)}, bf16[256,512]{1,0:T(8,128)(2,1)S(1)}, bf16[256,512]{1,0:T(8,128)(2,1)S(1)}, s32[8]{0:T(128)S(4)}) custom-call(f32[1,4,128,512]{3,2,1,0:T(8,128)} %grads.1, bf16[1,256,512]{2,1,0:T(8,128)(2,1)} %momentum.1, s32[4]{0:T(128)} %slots.1), custom_call_target="tpu_custom_call" | custom-call | bytes 2097152 | tf_op jit(solution)/shard_map/pallas_call | solution.py:385
  2.5 0.4 %collective-permute-start.3 = (f32[4,128,512]{2,1,0:T(8,128)S(1)}, f32[4,128,512]{2,1,0:T(8,128)S(1)}, u32[]{:S(2)}, u32[]{:S(2)}) collective-permute-start(f32[4,128,512]{2,1,0:T(8,128)S(1)} %get-tuple-element.26.own), channel_id=1, source_target_pairs={{0,8},{8,0},{1,9},{9,1},{16,24},{24,16},{17,25},{25,17},{2,10},{10... | collective-permute-start | bytes 3145736 | tf_op jit(solution)/shard_map/ppermute | solution.py:340
  2.9 0.2 collective-permute-start.1
  3.1 2.7 %collective-permute-start.2 = (bf16[256,512]{1,0:T(8,128)(2,1)S(1)}, bf16[256,512]{1,0:T(8,128)(2,1)S(1)}, u32[]{:S(2)}, u32[]{:S(2)}) collective-permute-start(bf16[256,512]{1,0:T(8,128)(2,1)S(1)} %shard_map.51), channel_id=1, source_target_pairs={{8,1},{9,0},{24,17},{25,16},{0,8},{1,9},{16,24},{17,25},{10,3},{11... | collective-permute-start | bytes 786440 | tf_op jit(solution)/shard_map/ppermute | solution.py:349
  5.8 0.4 %collective-permute-start.4 = (f32[128,512]{1,0:T(8,128)S(1)}, f32[128,512]{1,0:T(8,128)S(1)}, u32[]{:S(2)}, u32[]{:S(2)}) collective-permute-start(f32[128,512]{1,0:T(8,128)S(1)} %get-tuple-element.29), channel_id=1, source_target_pairs={{8,17},{9,16},{24,1},{25,0},{0,8},{1,9},{16,24},{17,25},{10,19},{1... | collective-permute-start | bytes 786440 | tf_op jit(solution)/shard_map/ppermute | solution.py:349
  6.2 2.9 %collective-permute-start.5 = (f32[128,512]{1,0:T(8,128)S(1)}, f32[128,512]{1,0:T(8,128)S(1)}, u32[]{:S(2)}, u32[]{:S(2)}) collective-permute-start(f32[128,512]{1,0:T(8,128)S(1)} %get-tuple-element.30), channel_id=1, source_target_pairs={{8,16},{9,17},{24,0},{25,1},{0,8},{1,9},{16,24},{17,25},{10,18},{1... | collective-permute-start | bytes 786440 | tf_op jit(solution)/shard_map/ppermute | solution.py:349
  9.1 0.4 %collective-permute-done.1.mom_x = bf16[256,512]{1,0:T(8,128)(2,1)S(1)} collective-permute-done((bf16[256,512]{1,0:T(8,128)(2,1)S(1)}, bf16[256,512]{1,0:T(8,128)(2,1)S(1)}, u32[]{:S(2)}, u32[]{:S(2)}) %collective-permute-start.1) | collective-permute-done | bytes 262176 | tf_op jit(solution)/shard_map/ppermute | solution.py:349
  9.6 4.2 %collective-permute-done.2.mom_y = bf16[256,512]{1,0:T(8,128)(2,1)S(1)} collective-permute-done((bf16[256,512]{1,0:T(8,128)(2,1)S(1)}, bf16[256,512]{1,0:T(8,128)(2,1)S(1)}, u32[]{:S(2)}, u32[]{:S(2)}) %collective-permute-start.2) | collective-permute-done | bytes 262176 | tf_op jit(solution)/shard_map/ppermute | solution.py:349
  13.8 2.3 %collective-permute-done.5.in_x = f32[128,512]{1,0:T(8,128)S(1)} collective-permute-done((f32[128,512]{1,0:T(8,128)S(1)}, f32[128,512]{1,0:T(8,128)S(1)}, u32[]{:S(2)}, u32[]{:S(2)}) %collective-permute-start.5) | collective-permute-done | bytes 262176 | tf_op jit(solution)/shard_map/ppermute | solution.py:349
  16.2 0.4 %collective-permute-done.6.in_y = f32[128,512]{1,0:T(8,128)S(1)} collective-permute-done((f32[128,512]{1,0:T(8,128)S(1)}, f32[128,512]{1,0:T(8,128)S(1)}, u32[]{:S(2)}, u32[]{:S(2)}) %collective-permute-start.6) | collective-permute-done | bytes 262176 | tf_op jit(solution)/shard_map/ppermute | solution.py:349
  16.8 2.0 %shard_map.55.start = f32[256,512]{1,0:T(8,128)S(1)} custom-call(f32[256,512]{1,0:T(8,128)S(1)} %get-tuple-element.33.nesterov), custom_call_target="tpu_custom_call" | custom-call | bytes 1048576 | tf_op jit(solution)/shard_map/pallas_call | solution.py:412
  18.8 0.7 %collective-permute-start.8 = (bf16[256,512]{1,0:T(8,128)(2,1)S(1)}, bf16[256,512]{1,0:T(8,128)(2,1)S(1)}, u32[]{:S(2)}, u32[]{:S(2)}) collective-permute-start(bf16[256,512]{1,0:T(8,128)(2,1)S(1)} %broadcast_select_fusion.new), channel_id=1, source_target_pairs={{0,24},{1,25},{16,8},{17,9},{8,1},{9,0},{24,17},{25,16},{2,26},{3,... | collective-permute-start | bytes 786440 | tf_op jit(solution)/shard_map/ppermute | solution.py:355
  19.5 2.9 %shard_map.56 = (bf16[128,512]{1,0:T(8,128)(2,1)S(1)}, bf16[128,512]{1,0:T(8,128)(2,1)S(1)}) custom-call(f32[256,512]{1,0:T(8,128)S(1)} %shard_map.55.start), custom_call_target="tpu_custom_call" | custom-call | bytes 1048576 | tf_op jit(solution)/shard_map/pallas_call | solution.py:416
  22.4 0.9 %collective-permute-start.10 = (bf16[128,512]{1,0:T(8,128)(2,1)S(1)}, bf16[128,512]{1,0:T(8,128)(2,1)S(1)}, u32[]{:S(2)}, u32[]{:S(2)}) collective-permute-start(bf16[128,512]{1,0:T(8,128)(2,1)S(1)} %get-tuple-element.36.mine), channel_id=1, source_target_pairs={{0,24},{1,25},{16,8},{17,9},{8,0},{9,1},{24,16},{25,17},{2,26},{3,... | collective-permute-start | bytes 393224 | tf_op jit(solution)/shard_map/ppermute | solution.py:349
  23.3 0.2 collective-permute-start.11
  23.5 1.2 %collective-permute-done.8.back = bf16[256,512]{1,0:T(8,128)(2,1)S(1)} collective-permute-done((bf16[256,512]{1,0:T(8,128)(2,1)S(1)}, bf16[256,512]{1,0:T(8,128)(2,1)S(1)}, u32[]{:S(2)}, u32[]{:S(2)}) %collective-permute-start.8) | collective-permute-done | bytes 262176 | tf_op jit(solution)/shard_map/ppermute | solution.py:355
  24.7 0.5 %collective-permute-start.15 = (bf16[128,512]{1,0:T(8,128)(2,1)S(1)}, bf16[128,512]{1,0:T(8,128)(2,1)S(1)}, u32[]{:S(2)}, u32[]{:S(2)}) collective-permute-start(bf16[128,512]{1,0:T(8,128)(2,1)S(1)} %get-tuple-element.36.mine), channel_id=1, source_target_pairs={{0,8},{8,0},{1,9},{9,1},{16,24},{24,16},{17,25},{25,17},{2,10},{10... | collective-permute-start | bytes 393224 | tf_op jit(solution)/shard_map/ppermute | solution.py:340
  25.2 1.1 %collective-permute-start.16 = (bf16[128,512]{1,0:T(8,128)(2,1)S(1)}, bf16[128,512]{1,0:T(8,128)(2,1)S(1)}, u32[]{:S(2)}, u32[]{:S(2)}) collective-permute-start(bf16[128,512]{1,0:T(8,128)(2,1)S(1)} %collective-permute-done.14.up_d), channel_id=1, source_target_pairs={{0,8},{8,0},{1,9},{9,1},{16,24},{24,16},{17,25},{25,17},{2,10},{10... | collective-permute-start | bytes 393224 | tf_op jit(solution)/shard_map/ppermute | solution.py:340
  26.3 1.0 %collective-permute-start.12 = (bf16[128,512]{1,0:T(8,128)(2,1)S(1)}, bf16[128,512]{1,0:T(8,128)(2,1)S(1)}, u32[]{:S(2)}, u32[]{:S(2)}) collective-permute-start(bf16[128,512]{1,0:T(8,128)(2,1)S(1)} %collective-permute-done.10.up_x), channel_id=1, source_target_pairs={{0,8},{8,0},{1,9},{9,1},{16,24},{24,16},{17,25},{25,17},{2,10},{10... | collective-permute-start | bytes 393224 | tf_op jit(solution)/shard_map/ppermute | solution.py:340
  27.4 0.3 %collective-permute-start.13 = (bf16[128,512]{1,0:T(8,128)(2,1)S(1)}, bf16[128,512]{1,0:T(8,128)(2,1)S(1)}, u32[]{:S(2)}, u32[]{:S(2)}) collective-permute-start(bf16[128,512]{1,0:T(8,128)(2,1)S(1)} %collective-permute-done.11.up_y), channel_id=1, source_target_pairs={{0,8},{8,0},{1,9},{9,1},{16,24},{24,16},{17,25},{25,17},{2,10},{10... | collective-permute-start | bytes 393224 | tf_op jit(solution)/shard_map/ppermute | solution.py:340
  27.7 0.7 %shard_map.57._ = bf16[4,128,512]{2,1,0:T(8,128)(2,1)} custom-call(s32[8]{0:T(128)S(4)} %get-tuple-element.22.plan, bf16[128,512]{1,0:T(8,128)(2,1)S(1)} %collective-permute-done.14.up_d, bf16[128,512]{1,0:T(8,128)(2,1)S(1)} %collective-permute-done.15.up_l, bf16[128,512]{1,0:T(8,128)(2,1)S(1)} %collective-permute-done.16.in_d, ...), custom_call_target="tpu_custom_call" | custom-call | bytes 524288 | tf_op jit(solution)/shard_map/pallas_call | solution.py:426
  28.4 0.3 collective-permute-done.13.in_y
  28.7 0.8 %shard_map.58 = (bf16[4,128,512]{2,1,0:T(8,128)(2,1)}, bf16[1,256,512]{2,1,0:T(8,128)(2,1)}) custom-call(s32[8]{0:T(128)S(4)} %get-tuple-element.22.plan, bf16[256,512]{1,0:T(8,128)(2,1)S(1)} %get-tuple-element.23.faded, bf16[256,512]{1,0:T(8,128)(2,1)S(1)} %broadcast_select_fusion.new, ...), custom_call_target="tpu_custom_call", output_to_operand_aliasing={{0}: (9, {})} | custom-call | bytes 1048576 | tf_op jit(solution)/shard_map/pallas_call | solution.py:434
  (20 shorter events, 0.5 us)
Async XLA Ops:
  0.6 1.9 %collective-permute-start = (bf16[1,256,512]{2,1,0:T(8,128)(2,1)}, bf16[1,256,512]{2,1,0:T(8,128)(2,1)S(1)}, u32[]{:S(2)}, u32[]{:S(2)}) collective-permute-start(bf16[1,256,512]{2,1,0:T(8,128)(2,1)} %momentum.1), channel_id=1, source_target_pairs={{0,8},{8,0},{1,9},{9,1},{16,24},{24,16},{17,25},{25,17},{2,10},{10... | collective-permute-start | bytes 786440 | tf_op jit(solution)/shard_map/ppermute | solution.py:340
  2.5 3.2 %collective-permute-start.3 = (f32[4,128,512]{2,1,0:T(8,128)S(1)}, f32[4,128,512]{2,1,0:T(8,128)S(1)}, u32[]{:S(2)}, u32[]{:S(2)}) collective-permute-start(f32[4,128,512]{2,1,0:T(8,128)S(1)} %get-tuple-element.26.own), channel_id=1, source_target_pairs={{0,8},{8,0},{1,9},{9,1},{16,24},{24,16},{17,25},{25,17},{2,10},{10... | collective-permute-start | bytes 3145736 | tf_op jit(solution)/shard_map/ppermute | solution.py:340
  2.9 6.7 %collective-permute-start.1 = (bf16[256,512]{1,0:T(8,128)(2,1)S(1)}, bf16[256,512]{1,0:T(8,128)(2,1)S(1)}, u32[]{:S(2)}, u32[]{:S(2)}) collective-permute-start(bf16[256,512]{1,0:T(8,128)(2,1)S(1)} %get-tuple-element.25.mom), channel_id=1, source_target_pairs={{8,16},{9,17},{24,0},{25,1},{0,8},{1,9},{16,24},{17,25},{10,18},{1... | collective-permute-start | bytes 786440 | tf_op jit(solution)/shard_map/ppermute | solution.py:349
  3.1 10.7 %collective-permute-start.2 = (bf16[256,512]{1,0:T(8,128)(2,1)S(1)}, bf16[256,512]{1,0:T(8,128)(2,1)S(1)}, u32[]{:S(2)}, u32[]{:S(2)}) collective-permute-start(bf16[256,512]{1,0:T(8,128)(2,1)S(1)} %shard_map.51), channel_id=1, source_target_pairs={{8,1},{9,0},{24,17},{25,16},{0,8},{1,9},{16,24},{17,25},{10,3},{11... | collective-permute-start | bytes 786440 | tf_op jit(solution)/shard_map/ppermute | solution.py:349
  5.8 8.1 %collective-permute-start.4 = (f32[128,512]{1,0:T(8,128)S(1)}, f32[128,512]{1,0:T(8,128)S(1)}, u32[]{:S(2)}, u32[]{:S(2)}) collective-permute-start(f32[128,512]{1,0:T(8,128)S(1)} %get-tuple-element.29), channel_id=1, source_target_pairs={{8,17},{9,16},{24,1},{25,0},{0,8},{1,9},{16,24},{17,25},{10,19},{1... | collective-permute-start | bytes 786440 | tf_op jit(solution)/shard_map/ppermute | solution.py:349
  6.2 10.0 %collective-permute-start.5 = (f32[128,512]{1,0:T(8,128)S(1)}, f32[128,512]{1,0:T(8,128)S(1)}, u32[]{:S(2)}, u32[]{:S(2)}) collective-permute-start(f32[128,512]{1,0:T(8,128)S(1)} %get-tuple-element.30), channel_id=1, source_target_pairs={{8,16},{9,17},{24,0},{25,1},{0,8},{1,9},{16,24},{17,25},{10,18},{1... | collective-permute-start | bytes 786440 | tf_op jit(solution)/shard_map/ppermute | solution.py:349
  9.1 7.5 %collective-permute-start.6 = (f32[128,512]{1,0:T(8,128)S(1)}, f32[128,512]{1,0:T(8,128)S(1)}, u32[]{:S(2)}, u32[]{:S(2)}) collective-permute-start(f32[128,512]{1,0:T(8,128)S(1)} %get-tuple-element.31), channel_id=1, source_target_pairs={{8,1},{9,0},{24,17},{25,16},{0,8},{1,9},{16,24},{17,25},{10,3},{11... | collective-permute-start | bytes 786440 | tf_op jit(solution)/shard_map/ppermute | solution.py:349
  16.7 2.1 %collective-permute-start.7 = (bf16[256,512]{1,0:T(8,128)(2,1)S(1)}, bf16[256,512]{1,0:T(8,128)(2,1)S(1)}, u32[]{:S(2)}, u32[]{:S(2)}) collective-permute-start(bf16[256,512]{1,0:T(8,128)(2,1)S(1)} %get-tuple-element.32), channel_id=1, source_target_pairs={{0,8},{8,0},{1,9},{9,1},{16,24},{24,16},{17,25},{25,17},{2,10},{10... | collective-permute-start | bytes 786440 | tf_op jit(solution)/shard_map/ppermute | solution.py:340
  18.8 5.8 %collective-permute-start.8 = (bf16[256,512]{1,0:T(8,128)(2,1)S(1)}, bf16[256,512]{1,0:T(8,128)(2,1)S(1)}, u32[]{:S(2)}, u32[]{:S(2)}) collective-permute-start(bf16[256,512]{1,0:T(8,128)(2,1)S(1)} %broadcast_select_fusion.new), channel_id=1, source_target_pairs={{0,24},{1,25},{16,8},{17,9},{8,1},{9,0},{24,17},{25,16},{2,26},{3,... | collective-permute-start | bytes 786440 | tf_op jit(solution)/shard_map/ppermute | solution.py:355
  22.4 2.8 %collective-permute-start.14 = (bf16[128,512]{1,0:T(8,128)(2,1)S(1)}, bf16[128,512]{1,0:T(8,128)(2,1)S(1)}, u32[]{:S(2)}, u32[]{:S(2)}) collective-permute-start(bf16[128,512]{1,0:T(8,128)(2,1)S(1)} %get-tuple-element.37), channel_id=1, source_target_pairs={{0,25},{1,24},{16,9},{17,8},{8,0},{9,1},{24,16},{25,17},{2,27},{3,... | collective-permute-start | bytes 393224 | tf_op jit(solution)/shard_map/ppermute | solution.py:349
  22.4 3.9 %collective-permute-start.10 = (bf16[128,512]{1,0:T(8,128)(2,1)S(1)}, bf16[128,512]{1,0:T(8,128)(2,1)S(1)}, u32[]{:S(2)}, u32[]{:S(2)}) collective-permute-start(bf16[128,512]{1,0:T(8,128)(2,1)S(1)} %get-tuple-element.36.mine), channel_id=1, source_target_pairs={{0,24},{1,25},{16,8},{17,9},{8,0},{9,1},{24,16},{25,17},{2,26},{3,... | collective-permute-start | bytes 393224 | tf_op jit(solution)/shard_map/ppermute | solution.py:349
  23.3 4.1 %collective-permute-start.11 = (bf16[128,512]{1,0:T(8,128)(2,1)S(1)}, bf16[128,512]{1,0:T(8,128)(2,1)S(1)}, u32[]{:S(2)}, u32[]{:S(2)}) collective-permute-start(bf16[128,512]{1,0:T(8,128)(2,1)S(1)} %get-tuple-element.37), channel_id=1, source_target_pairs={{0,9},{1,8},{16,25},{17,24},{8,0},{9,1},{24,16},{25,17},{2,11},{3,... | collective-permute-start | bytes 393224 | tf_op jit(solution)/shard_map/ppermute | solution.py:349
  24.7 4.1 %collective-permute-start.9 = (bf16[256,512]{1,0:T(8,128)(2,1)S(1)}, bf16[256,512]{1,0:T(8,128)(2,1)S(1)}, u32[]{:S(2)}, u32[]{:S(2)}) collective-permute-start(bf16[256,512]{1,0:T(8,128)(2,1)S(1)} %collective-permute-done.8.back), channel_id=1, source_target_pairs={{0,8},{8,0},{1,9},{9,1},{16,24},{24,16},{17,25},{25,17},{2,10},{10... | collective-permute-start | bytes 786440 | tf_op jit(solution)/shard_map/ppermute | solution.py:340
  24.7 3.0 %collective-permute-start.15 = (bf16[128,512]{1,0:T(8,128)(2,1)S(1)}, bf16[128,512]{1,0:T(8,128)(2,1)S(1)}, u32[]{:S(2)}, u32[]{:S(2)}) collective-permute-start(bf16[128,512]{1,0:T(8,128)(2,1)S(1)} %get-tuple-element.36.mine), channel_id=1, source_target_pairs={{0,8},{8,0},{1,9},{9,1},{16,24},{24,16},{17,25},{25,17},{2,10},{10... | collective-permute-start | bytes 393224 | tf_op jit(solution)/shard_map/ppermute | solution.py:340
  25.2 2.5 %collective-permute-start.16 = (bf16[128,512]{1,0:T(8,128)(2,1)S(1)}, bf16[128,512]{1,0:T(8,128)(2,1)S(1)}, u32[]{:S(2)}, u32[]{:S(2)}) collective-permute-start(bf16[128,512]{1,0:T(8,128)(2,1)S(1)} %collective-permute-done.14.up_d), channel_id=1, source_target_pairs={{0,8},{8,0},{1,9},{9,1},{16,24},{24,16},{17,25},{25,17},{2,10},{10... | collective-permute-start | bytes 393224 | tf_op jit(solution)/shard_map/ppermute | solution.py:340
  26.3 2.1 %collective-permute-start.12 = (bf16[128,512]{1,0:T(8,128)(2,1)S(1)}, bf16[128,512]{1,0:T(8,128)(2,1)S(1)}, u32[]{:S(2)}, u32[]{:S(2)}) collective-permute-start(bf16[128,512]{1,0:T(8,128)(2,1)S(1)} %collective-permute-done.10.up_x), channel_id=1, source_target_pairs={{0,8},{8,0},{1,9},{9,1},{16,24},{24,16},{17,25},{25,17},{2,10},{10... | collective-permute-start | bytes 393224 | tf_op jit(solution)/shard_map/ppermute | solution.py:340
  27.4 1.3 %collective-permute-start.13 = (bf16[128,512]{1,0:T(8,128)(2,1)S(1)}, bf16[128,512]{1,0:T(8,128)(2,1)S(1)}, u32[]{:S(2)}, u32[]{:S(2)}) collective-permute-start(bf16[128,512]{1,0:T(8,128)(2,1)S(1)} %collective-permute-done.11.up_y), channel_id=1, source_target_pairs={{0,8},{8,0},{1,9},{9,1},{16,24},{24,16},{17,25},{25,17},{2,10},{10... | collective-permute-start | bytes 393224 | tf_op jit(solution)/shard_map/ppermute | solution.py:340
